TPU v7x, 256 devices: a whole 4x4x8 slice. The times are simulated.
256 devices in a mesh: dp: 8 (over z), tensor: 32 (over x, y, core).
Axes of the slice: x: 4, y: 4, z: 8, core: 2. Of those that a mesh axis runs over, the one named last changes fastest.
Arguments:
- tokens: bfloat16 [2048, 5120], P(('dp', 'tensor')), may hold values from -24 to 24
- gate_weight: bfloat16 [6912, 5120], P('tensor'), may hold values from -0.078125 to 0.078125
- up_weight: bfloat16 [6912, 5120], P('tensor'), may hold values from -0.078125 to 0.078125
- down_weight: bfloat16 [6912, 5120], P('tensor'), may hold values from -0.078125 to 0.078125
- residual_carry: bfloat16 [8, 32, 256, 5120], P('dp', 'tensor'), may hold values from -2.5 to 2.5
- forward_blocks: int32 [8, 32, 32, 10], P('dp', 'tensor'), may hold values from 0 to 39, as said below
- forward_counts: int32 [8, 32, 32], P('dp', 'tensor'), may hold values from 1 to 10, as said below
- cotangent: bfloat16 [2048, 5120], P(('dp', 'tensor')), may hold values from -24 to 24
- backward_blocks: int32 [8, 32, 32, 10], P('dp', 'tensor'), may hold values from 0 to 39, as said below
- backward_counts: int32 [8, 32, 32], P('dp', 'tensor'), may hold values from 1 to 10, as said below
Outputs:
- layer_output: bfloat16 [2048, 5120], P(('dp', 'tensor'))
- residual_next: bfloat16 [8, 32, 256, 5120], P('dp', 'tensor')
- input_gradient: bfloat16 [2048, 5120], P(('dp', 'tensor'))
- gate_gradient: bfloat16 [6912, 5120], P('tensor', 'dp')
- up_gradient: bfloat16 [6912, 5120], P('tensor', 'dp')
- down_gradient: bfloat16 [6912, 5120], P('tensor', 'dp')
Inputs may be any that keep to these rules, and one draw needn't show every extreme that they name: `forward_blocks`: for each group, source and destination the 10 block numbers are all different. `forward_counts`: in each dp group one destination receives 10 blocks from every source. `backward_blocks`: for each group, source and destination the 10 block numbers are all different. `backward_counts`: in each dp group one destination receives 10 blocks from every source.
All inputs are finite; a program needn't handle non-finite values.
Results may differ from a plain program's by a relative error of at most 0.005.
Values may be sent and summed in bfloat16 or wider, within the bound.
No kernel may reach another device: no remote copies, remote signals or barrier semaphores. Data moves between devices by JAX's collectives and lax.ppermute only.
A program may use at most 128 MiB of HBM per device.

v0:
```python
import jax
import jax.numpy as jnp
from jax import lax
from jax.sharding import PartitionSpec as P


def chosen_blocks(blocks, counts, column_blocks):
    slots = blocks.shape[1]
    validity = jnp.arange(slots)[None, :] < counts[:, None]
    matched = (blocks[:, :, None] == jnp.arange(column_blocks)[None, None, :]) & validity[
        :, :, None
    ]
    return (matched, validity)


def block_sum(values, blocks, counts):
    members = lax.axis_size("tensor")
    row_count = values.shape[0] // members
    column_blocks = values.shape[1] // 128
    matched, validity = chosen_blocks(blocks, counts, column_blocks)
    shaped = values.reshape(members, row_count, column_blocks, 128)
    keep_blocks = jnp.any(matched, axis=1).astype(jnp.float32)
    masked = (shaped * keep_blocks[:, None, :, None]).reshape(values.shape)
    return lax.psum_scatter(masked, "tensor", scatter_dimension=0, tiled=True)


def contract_rows(left_matrix, right_matrix):
    return lax.dot_general(
        left_matrix, right_matrix, (((0,), (0,)), ((), ())), preferred_element_type=jnp.float32
    )


def contract_columns(left_matrix, right_matrix):
    return lax.dot_general(
        left_matrix, right_matrix, (((1,), (1,)), ((), ())), preferred_element_type=jnp.float32
    )


def shards(
    tokens,
    gate_weight,
    up_weight,
    down_weight,
    residual_carry,
    forward_blocks,
    forward_counts,
    cotangent,
    backward_blocks,
    backward_counts,
):
    members = lax.axis_size("tensor")
    gathered = lax.all_gather(tokens, "tensor", axis=0, tiled=True)
    gate_act = contract_columns(gathered, gate_weight)
    up_act = contract_columns(gathered, up_weight)
    sigmoid_gate = jax.nn.sigmoid(gate_act)
    silu_gate = gate_act * sigmoid_gate
    hidden = (silu_gate * up_act).astype(jnp.bfloat16)
    partial_value = jnp.dot(hidden, down_weight, preferred_element_type=jnp.float32)
    corrected = partial_value + residual_carry[0, 0].astype(jnp.float32)
    column_blocks = corrected.shape[1] // 128
    matched, validity = chosen_blocks(forward_blocks[0, 0], forward_counts[0, 0], column_blocks)
    keep_blocks = 1.0 - jnp.any(matched, axis=1).astype(jnp.float32)
    shaped = corrected.reshape(members, corrected.shape[0] // members, column_blocks, 128)
    residual_next = (
        (shaped * keep_blocks[:, None, :, None]).reshape(residual_carry.shape).astype(jnp.bfloat16)
    )
    layer_output = block_sum(corrected, forward_blocks[0, 0], forward_counts[0, 0]).astype(
        jnp.bfloat16
    )
    cotangent_rows = lax.all_gather(cotangent, "tensor", axis=0, tiled=True)
    hidden_back = contract_columns(cotangent_rows, down_weight)
    up_back = (hidden_back * silu_gate).astype(jnp.bfloat16)
    gate_back = (
        hidden_back * up_act * (sigmoid_gate * (1.0 + gate_act * (1.0 - sigmoid_gate)))
    ).astype(jnp.bfloat16)
    input_partial = jnp.dot(gate_back, gate_weight, preferred_element_type=jnp.float32) + jnp.dot(
        up_back, up_weight, preferred_element_type=jnp.float32
    )
    input_gradient = block_sum(input_partial, backward_blocks[0, 0], backward_counts[0, 0]).astype(
        jnp.bfloat16
    )
    gate_term = contract_rows(gate_back, gathered)
    up_term = contract_rows(up_back, gathered)
    down_term = contract_rows(hidden, cotangent_rows)
    gate_total, up_total, down_total = (
        lax.psum_scatter(gate_term, "dp", scatter_dimension=1, tiled=True),
        lax.psum_scatter(up_term, "dp", scatter_dimension=1, tiled=True),
        lax.psum_scatter(down_term, "dp", scatter_dimension=1, tiled=True),
    )
    gate_gradient = gate_total.astype(jnp.bfloat16)
    up_gradient = up_total.astype(jnp.bfloat16)
    down_gradient = down_total.astype(jnp.bfloat16)
    return (layer_output, residual_next, input_gradient, gate_gradient, up_gradient, down_gradient)


def solution(mesh):
    return jax.shard_map(
        shards,
        mesh=mesh,
        in_specs=(
            P(("dp", "tensor"), None),
            P("tensor", None),
            P("tensor", None),
            P("tensor", None),
            P("dp", "tensor", None, None),
            P("dp", "tensor", None, None),
            P("dp", "tensor", None),
            P(("dp", "tensor"), None),
            P("dp", "tensor", None, None),
            P("dp", "tensor", None),
        ),
        out_specs=(
            P(("dp", "tensor"), None),
            P("dp", "tensor", None, None),
            P(("dp", "tensor"), None),
            P("tensor", "dp"),
            P("tensor", "dp"),
            P("tensor", "dp"),
        ),
        check_vma=False,
    )
```

profile of v0, /device:TPU:1, one launch (start us, length us, event | category | flops | bytes accessed | tf_op | source)
XLA Modules:
  0.0 497.7 jit_solution(9115217606495930697)
XLA Ops:
  7.2 0.7 all-gather.3.cloned.1.call-update
  8.0 0.7 all-gather.5.cloned.1.call-update
  8.7 0.7 copy.22
  9.4 0.7 iota_compare_fusion.2
  10.1 0.2 fusion.7
  10.2 54.1 %all-gather.3.cloned.1.call-done = bf16[256,5120]{1,0:T(8,128)(2,1)} async-done(((bf16[8,5120]{1,0:T(8,128)(2,1)}), bf16[256,5120]{1,0:T(8,128)(2,1)}) %all-gather.3.cloned.1.call-update) | async-done | bytes 2621456 | tf_op jit(solution)/shard_map/all_gather | solution.py:52
  64.3 3.5 fusion.9
  67.9 0.3 copy-done.3
  68.2 1.0 fusion.8
  69.2 46.6 %all-gather.5.cloned.1.call-done = bf16[256,5120]{1,0:T(8,128)(2,1)} async-done(((bf16[8,5120]{1,0:T(8,128)(2,1)}), bf16[256,5120]{1,0:T(8,128)(2,1)}) %all-gather.5.cloned.1.call-update) | async-done | bytes 2621456 | tf_op jit(solution)/shard_map/all_gather | solution.py:70
  115.8 2.9 multiply_convert_fusion
  118.7 0.9 fusion.10
  119.7 0.7 copy-done.2
  120.3 3.8 fusion
  124.1 0.0 reduce-scatter.6.cloned.1.call-start
  124.2 0.6 copy-done.5
  124.8 0.2 fusion.5
  125.0 7.2 %fusion.2 = (bf16[1,1,256,5120]{3,2,1,0:T(8,128)(2,1)}, f32[256,5120]{1,0:T(8,128)}) fusion(f32[32,40]{1,0:T(8,128)S(1)} %broadcast_subtract_fusion, f32[32,40]{1,0:T(8,128)S(1)} %convert_element_type.57, bf16[1,1,256,5120]{3,2,1,0:T(8,128)(2,1)} %param.14, bf16[256,216]{0,1:T(8,128)(2,1)S(1)} %get-tuple-element.10, bf16[216,5120]{1,0:T(8,128)(2,1)S(1)} %copy-done), kind=kOutput, calls=%fused_computation.6 | convolution fusion | flops 572784640 | bytes 12818432 | tf_op jit(solution)/shard_map/dot_general | solution.py:58
  132.2 0.0 reduce-scatter.14.cloned.1.call-start
  132.3 4.6 fusion.13
  137.0 4.7 fusion.12
  141.7 4.7 fusion.11
  146.4 67.4 %reduce-scatter.8.cloned.1.call-done = f32[8,5120]{1,0:T(8,128)} async-done(((f32[256,5120]{1,0:T(8,128)}), f32[8,5120]{1,0:T(8,128)}) %reduce-scatter.8.cloned.1.call-update) | async-done | bytes 163856 | tf_op jit(solution)/shard_map/reduce_scatter | solution.py:24
  213.9 1.6 convert_element_type.64
  215.4 94.6 %reduce-scatter.6.cloned.1.call-done = f32[8,5120]{1,0:T(8,128)} async-done(((f32[256,5120]{1,0:T(8,128)}), f32[8,5120]{1,0:T(8,128)}) %reduce-scatter.6.cloned.1.call-update) | async-done | bytes 163856 | tf_op jit(solution)/shard_map/reduce_scatter | solution.py:24
  310.0 1.6 convert_element_type.58
  311.6 59.7 %reduce-scatter.14.cloned.1.call-done = f32[216,640]{1,0:T(8,128)} async-done(((f32[216,5120]{1,0:T(8,128)}), f32[216,640]{1,0:T(8,128)}) %reduce-scatter.14.cloned.1.call-update) | async-done | bytes 552976 | tf_op jit(solution)/shard_map/reduce_scatter | solution.py:88
  371.3 1.8 convert_element_type.67
  373.0 57.0 %reduce-scatter.12.cloned.1.call-done = f32[216,640]{1,0:T(8,128)} async-done(((f32[216,5120]{1,0:T(8,128)}), f32[216,640]{1,0:T(8,128)}) %reduce-scatter.12.cloned.1.call-update) | async-done | bytes 552976 | tf_op jit(solution)/shard_map/reduce_scatter | solution.py:87
  430.1 1.8 convert_element_type.66
  431.9 57.2 %reduce-scatter.10.cloned.1.call-done = f32[216,640]{1,0:T(8,128)} async-done(((f32[216,5120]{1,0:T(8,128)}), f32[216,640]{1,0:T(8,128)}) %reduce-scatter.10.cloned.1.call-update) | async-done | bytes 552976 | tf_op jit(solution)/shard_map/reduce_scatter | solution.py:86
  489.0 1.8 convert_element_type.65
  (26 shorter events, 0.3 us)
Async XLA Ops:
  7.2 108.6 %copy-start = (bf16[216,5120]{1,0:T(8,128)(2,1)S(1)}, bf16[216,5120]{1,0:T(8,128)(2,1)}, u32[]{:S(2)}) copy-start(bf16[216,5120]{1,0:T(8,128)(2,1)} %param.13) | copy-start | bytes 6635524
  7.2 57.1 %all-gather.3.cloned.1.call-start = ((), (), s32[]{:S(2)}) async-start(), calls=%async_computation.5 | async-start | bytes 2703360 | tf_op jit(solution)/shard_map/all_gather | solution.py:52
  7.9 107.9 %all-gather.5.cloned.1.call-start = ((), (), s32[]{:S(2)}) async-start(), calls=%async_computation.7 | async-start | bytes 2703360 | tf_op jit(solution)/shard_map/all_gather | solution.py:70
  8.7 205.2 %reduce-scatter.8.cloned.1.call-start = ((), (), s32[]{:S(2)}) async-start(), calls=%async_computation.8 | async-start | bytes 5406720 | tf_op jit(solution)/shard_map/reduce_scatter | solution.py:24
  64.3 3.6 copy-start.1
  64.3 3.9 copy-start.3
  115.8 2.9 copy-start.4
  118.7 1.6 copy-start.2
  124.1 0.7 copy-start.5
  124.1 0.7 copy-start.6
  124.1 185.9 %reduce-scatter.6.cloned.1.call-start = ((), (), s32[]{:S(2)}) async-start(), calls=%async_computation.6 | async-start | bytes 5406720 | tf_op jit(solution)/shard_map/reduce_scatter | solution.py:24
  132.2 239.0 %reduce-scatter.14.cloned.1.call-start = ((), (), s32[]{:S(2)}) async-start(), calls=%async_computation.11 | async-start | bytes 4976640 | tf_op jit(solution)/shard_map/reduce_scatter | solution.py:88
  136.9 293.1 %reduce-scatter.12.cloned.1.call-start = ((), (), s32[]{:S(2)}) async-start(), calls=%async_computation.10 | async-start | bytes 4976640 | tf_op jit(solution)/shard_map/reduce_scatter | solution.py:87
  141.7 347.4 %reduce-scatter.10.cloned.1.call-start = ((), (), s32[]{:S(2)}) async-start(), calls=%async_computation.9 | async-start | bytes 4976640 | tf_op jit(solution)/shard_map/reduce_scatter | solution.py:86
Sparse Core Ops, SparseCore 0:
  10.6 53.7 all-gather.2
  66.8 48.9 all-gather.4
  124.3 89.5 reduce-scatter.7
  218.3 91.6 reduce-scatter.5
  312.4 58.7 reduce-scatter.13
  373.7 56.3 reduce-scatter.11
  432.6 56.3 reduce-scatter.9
where the time goes:
time: 498 us
  waiting for transfers between devices  438 us (88%)
  matrix products  33.3 us (7%)
  between operations  14.2 us (3%)
  other arithmetic  9.48 us (2%)
    reduce_scatter x2, waiting for transfers between devices, block_sum(): return lax.psum_scatter(masked, 'tensor', scatter_dimension=0, tiled=True)  162 us
    reduce_scatter x1, waiting for transfers between devices, shards(): lax.psum_scatter(down_term, 'dp', scatter_dimension=1, tiled=True)  59.7 us
    reduce_scatter x1, waiting for transfers between devices, shards(): lax.psum_scatter(gate_term, 'dp', scatter_dimension=1, tiled=True)  57.2 us
    reduce_scatter x1, waiting for transfers between devices, shards(): lax.psum_scatter(up_term, 'dp', scatter_dimension=1, tiled=True)  57 us
    all_gather x1, waiting for transfers between devices, shards(): gathered = lax.all_gather(tokens, 'tensor', axis=0, tiled=True)  54.1 us
    all_gather x1, waiting for transfers between devices, shards(): cotangent_rows = lax.all_gather(cotangent, 'tensor', axis=0, tiled=True)  46.6 us
    dot_general x3, matrix products, contract_rows(): lax.dot_general(left_matrix, right_matrix, (((0,), (0,)), ((), ())), pref...  14 us
  transfers between devices with their start and end apart: 7, of which 7 were waited for; matrix products, arithmetic and copies ran while one was open for 7% of the time, Pallas kernels for 0%

commit v1 on v0

v1 whole, which is shorter than its diff:
```python
import jax
import jax.numpy as jnp
from jax import lax
from jax.experimental import pallas as pl
from jax.experimental.pallas import tpu as pltpu
from jax.sharding import Mesh, PartitionSpec as P

T = ("x", "y", "core")
XY = ("x", "y")
D = 5120
F = 216
G = 256
KMAX = 10
SIDE = 128
BF = jnp.bfloat16
F32 = jnp.float32


def nt(a, b):
    return lax.dot_general(a, b, (((1,), (1,)), ((), ())), preferred_element_type=F32)


def tn(a, b):
    return lax.dot_general(a, b, (((0,), (0,)), ((), ())), preferred_element_type=F32)


def nn(a, b):
    return lax.dot_general(a, b, (((1,), (0,)), ((), ())), preferred_element_type=F32)


def acts_kernel(tok, cot, wg, wu, wd, out, ga, ua, hb):
    k = pl.program_id(0)

    @pl.when(k == 0)
    def _():
        ga[...] = jnp.zeros_like(ga)
        ua[...] = jnp.zeros_like(ua)
        hb[...] = jnp.zeros_like(hb)

    t = tok[...]
    ga[...] += nt(wg[...], t)
    ua[...] += nt(wu[...], t)
    hb[...] += nt(wd[...], cot[...])

    @pl.when(k == pl.num_programs(0) - 1)
    def _():
        g, u, b = ga[...], ua[...], hb[...]
        s = jax.nn.sigmoid(g)
        silu = g * s
        out[0] = (b * u * (s * (1.0 + g * (1.0 - s)))).astype(BF)
        out[1] = (b * silu).astype(BF)
        out[2] = (silu * u).astype(BF)


def acts(rows, wg, wu, wd):
    kb = 1024
    steps = D // kb
    wspec = pl.BlockSpec((F, kb), lambda k: (0, k))
    return pl.pallas_call(
        acts_kernel,
        grid=(steps,),
        in_specs=[
            pl.BlockSpec((G, kb), lambda k: (0, k)),
            pl.BlockSpec((G, kb), lambda k: (0, k + steps)),
            wspec,
            wspec,
            wspec,
        ],
        out_specs=pl.BlockSpec((3, F, G), lambda k: (0, 0, 0)),
        out_shape=jax.ShapeDtypeStruct((3, F, G), BF),
        scratch_shapes=[pltpu.VMEM((F, G), F32)] * 3,
        compiler_params=pltpu.CompilerParams(vmem_limit_bytes=32 << 20),
        cost_estimate=pl.CostEstimate(
            flops=6 * G * F * D, bytes_accessed=2 * (2 * G * D + 3 * F * D), transcendentals=G * F
        ),
        name="acts",
    )(rows, rows, wg, wu, wd)


def partial_kernel(fb, fc, bb, bc, act, wg, wu, wd, res, res_next, payload, sf, sb, pk):
    n = pl.program_id(0)
    nb = wg.shape[1]
    cols = pl.ds(pl.multiple_of(n * nb, nb), nb)
    sf[:, cols] = tn(act[2], wd[...]) + res[...].astype(F32)
    sb[:, cols] = tn(act[0], wg[...]) + tn(act[1], wu[...])

    @pl.when(n == pl.num_programs(0) - 1)
    def _():
        def one(t, carry):
            r = pl.ds(pl.multiple_of(t * 8, 8), 8)
            count = fc[t]
            for j in range(KMAX):
                at = pl.ds(pl.multiple_of(fb[t, j] * 128, 128), 128)
                tile = sf[r, at]
                pk[pl.ds(pl.multiple_of(t * 160 + j * 8, 8), 8), :] = tile
                sf[r, at] = jnp.where(j < count, 0.0, tile)
                ab = pl.ds(pl.multiple_of(bb[t, j] * 128, 128), 128)
                pk[pl.ds(pl.multiple_of(t * 160 + 80 + j * 8, 8), 8), :] = sb[r, ab]
            return carry

        lax.fori_loop(0, 32, one, 0)
        payload[...] = pk[...].astype(BF)
        res_next[...] = sf[...].astype(BF)


def partials(fb, fc, bb, bc, act, wg, wu, wd, res):
    nb = 1024
    wspec = pl.BlockSpec((F, nb), lambda n, *_: (0, n))
    return pl.pallas_call(
        partial_kernel,
        grid_spec=pltpu.PrefetchScalarGridSpec(
            num_scalar_prefetch=4,
            grid=(D // nb,),
            in_specs=[
                pl.BlockSpec((3, F, G), lambda n, *_: (0, 0, 0)),
                wspec,
                wspec,
                wspec,
                pl.BlockSpec((G, nb), lambda n, *_: (0, n)),
            ],
            out_specs=[
                pl.BlockSpec((G, D), lambda n, *_: (0, 0)),
                pl.BlockSpec((32 * 160, 128), lambda n, *_: (0, 0)),
            ],
            scratch_shapes=[
                pltpu.VMEM((G, D), F32),
                pltpu.VMEM((G, D), F32),
                pltpu.VMEM((32 * 160, 128), F32),
            ],
        ),
        out_shape=[
            jax.ShapeDtypeStruct((G, D), BF),
            jax.ShapeDtypeStruct((32 * 160, 128), BF),
        ],
        compiler_params=pltpu.CompilerParams(vmem_limit_bytes=48 << 20),
        cost_estimate=pl.CostEstimate(
            flops=6 * G * F * D, bytes_accessed=2 * (2 * G * D + 3 * F * D), transcendentals=0
        ),
        name="partials",
    )(fb, fc, bb, bc, act, wg, wu, wd, res)


def unpack_kernel(idx, data, of, ob, pk, af, ab):
    pk[...] = data[...].astype(F32)
    af[...] = jnp.zeros_like(af)
    ab[...] = jnp.zeros_like(ab)

    def one(t, carry):
        for j in range(KMAX):
            cf = pl.ds(pl.multiple_of(idx[t, j] * 128, 128), 128)
            cb = pl.ds(pl.multiple_of(idx[t, KMAX + j] * 128, 128), 128)
            af[:, cf] += pk[pl.ds(pl.multiple_of(t * 160 + j * 8, 8), 8), :]
            ab[:, cb] += pk[pl.ds(pl.multiple_of(t * 160 + 80 + j * 8, 8), 8), :]
        return carry

    lax.fori_loop(0, 32, one, 0)
    of[...] = af[:, :D].astype(BF)
    ob[...] = ab[:, :D].astype(BF)


def unpack(idx, data):
    whole = pl.BlockSpec(memory_space=pltpu.VMEM)
    return pl.pallas_call(
        unpack_kernel,
        in_specs=[pl.BlockSpec(memory_space=pltpu.SMEM), whole],
        out_specs=[whole, whole],
        out_shape=[jax.ShapeDtypeStruct((8, D), BF)] * 2,
        scratch_shapes=[
            pltpu.VMEM((32 * 160, 128), F32),
            pltpu.VMEM((8, D + 128), F32),
            pltpu.VMEM((8, D + 128), F32),
        ],
        compiler_params=pltpu.CompilerParams(vmem_limit_bytes=32 << 20),
        cost_estimate=pl.CostEstimate(flops=10**6, bytes_accessed=2 * 10**6, transcendentals=0),
        name="unpack",
    )(idx, data)


def grads_kernel(core, act, cm, co, og, ou, od, ag, au, ad):
    k = pl.program_id(0)

    @pl.when(k == 0)
    def _():
        ag[...] = jnp.zeros_like(ag)
        au[...] = jnp.zeros_like(au)
        ad[...] = jnp.zeros_like(ad)

    def add(tok_ref, cot_ref):
        tok = tok_ref[...].reshape(G, 640)
        cot = cot_ref[...].reshape(G, 640)
        ag[...] += nn(act[0, 0], tok)
        au[...] += nn(act[0, 1], tok)
        ad[...] += nn(act[0, 2], cot)

    @pl.when(core[0] == 0)
    def _():
        add(cm, co)

    @pl.when(core[0] != 0)
    def _():
        add(co, cm)

    @pl.when(k == pl.num_programs(0) - 1)
    def _():
        og[...] = ag[...].astype(BF)
        ou[...] = au[...].astype(BF)
        od[...] = ad[...].astype(BF)


def grads(core, act, cm, co):
    cspec = pl.BlockSpec((16, 1, 16, 640), lambda k, *_: (0, k, 0, 0))
    ospec = pl.BlockSpec((F, 640), lambda k, *_: (0, 0))
    return pl.pallas_call(
        grads_kernel,
        grid_spec=pltpu.PrefetchScalarGridSpec(
            num_scalar_prefetch=1,
            grid=(8,),
            in_specs=[pl.BlockSpec((1, 3, F, G), lambda k, *_: (k, 0, 0, 0)), cspec, cspec],
            out_specs=[ospec] * 3,
            scratch_shapes=[pltpu.VMEM((F, 640), F32)] * 3,
        ),
        out_shape=[jax.ShapeDtypeStruct((F, 640), BF)] * 3,
        compiler_params=pltpu.CompilerParams(vmem_limit_bytes=32 << 20),
        cost_estimate=pl.CostEstimate(
            flops=6 * G * F * D, bytes_accessed=8 * 10**6, transcendentals=0
        ),
        name="grads",
    )(core, act, cm, co)


def swap_core(v):
    return lax.ppermute(v, "core", [(0, 1), (1, 0)])


def shards(tok, wg, wu, wd, res, fb, fc, cot, bb, bc):
    core = lax.axis_index("core")
    me = lax.axis_index(T)
    fb, fc, bb, bc = fb[0, 0], fc[0, 0], bb[0, 0], bc[0, 0]
    slots = jnp.arange(KMAX)[None, :]
    lists = jnp.concatenate(
        [jnp.where(slots < fc[:, None], fb, 40), jnp.where(slots < bc[:, None], bb, 40)], axis=1
    )
    side = jnp.pad(lists.astype(BF).reshape(8, 80), ((0, 0), (0, SIDE - 80)))
    rows = lax.all_gather(jnp.concatenate([tok, cot, side], axis=1), T, axis=0, tiled=True)

    first = core == 0
    other = swap_core(jnp.where(first, cot, tok))
    chip = jnp.concatenate([jnp.where(first, tok, other), jnp.where(first, other, cot)], axis=0)
    chip = lax.all_to_all(chip.reshape(16, 8, 640).transpose(1, 0, 2), "dp", 0, 0, tiled=True)
    cm = lax.all_to_all(jnp.broadcast_to(chip[None], (16, 8, 16, 640)), XY, 0, 0, tiled=True)
    co = swap_core(cm)

    act = acts(rows, wg, wu, wd)
    everyone = lax.all_gather(act[None], "dp", axis=0, tiled=True)
    res_next, payload = partials(fb, fc, bb, bc, act, wg, wu, wd, res[0, 0])
    received = lax.all_to_all(payload.reshape(32, 160, 128), T, 0, 0, tiled=True)
    told = rows[:, 2 * D :].reshape(32, 8, SIDE)[:, :, :80].reshape(32, 32, 2 * KMAX)
    idx = lax.dynamic_index_in_dim(told, me, 1, keepdims=False).astype(jnp.int32)
    layer_output, input_gradient = unpack(idx, received.reshape(32 * 160, 128))
    gate_gradient, up_gradient, down_gradient = grads(
        core.astype(jnp.int32).reshape(1), everyone, cm, co
    )
    return (
        layer_output,
        res_next[None, None],
        input_gradient,
        gate_gradient,
        up_gradient,
        down_gradient,
    )


def solution(mesh):
    fine = Mesh(mesh.devices.reshape(8, 4, 4, 2), ("dp", "x", "y", "core"))
    row = P(("dp",) + T, None)
    return jax.shard_map(
        shards,
        mesh=fine,
        in_specs=(
            row,
            P(T, None),
            P(T, None),
            P(T, None),
            P("dp", T, None, None),
            P("dp", T, None, None),
            P("dp", T, None),
            row,
            P("dp", T, None, None),
            P("dp", T, None),
        ),
        out_specs=(row, P("dp", T, None, None), row, P(T, "dp"), P(T, "dp"), P(T, "dp")),
        check_vma=False,
    )
```

time: 498 us -> 162 us (0.33)
  waiting for transfers between devices: 438 us -> 65.4 us
  matrix products: 33.3 us -> 0 us
  Pallas kernels: 0 us -> 27 us
  starting transfers between devices: 0.28 us -> 17.5 us
  local copies, waits for them, and re-layouts: 2.32 us -> 18 us
  blocking collectives: 0 us -> 14.9 us
  other arithmetic: 9.48 us -> 4.27 us
    reduce_scatter x5 -> x0, waiting for transfers between devices: 336 us -> none  [the longest x2 162 us: block_sum(): return lax.psum_scatter(masked, 'tensor', scatter_dimension=0, tiled=True)]
    all_gather x2, waiting for transfers between devices: 101 us -> 45.7 us  [the longest x1 45.7 us: shards(): lax.all_gather(jnp.concatenate([tok, cot, side], axis=1), T, axis=0, tile...]
    dot_general x9 -> x0, matrix products: 33.3 us -> none  [the longest x3 14 us: contract_rows(): lax.dot_general(left_matrix, right_matrix, (((0,), (0,)), ((), ())), pref...]
    pallas_call x0 -> x4, Pallas kernels: none -> 27 us  [the longest x1 10.3 us: partials(): pl.pallas_call(partial_kernel, grid_spec=pltpu.PrefetchScalarGridSpec(num...]
    all_to_all x0 -> x2, waiting for transfers between devices: none -> 18.8 us  [the longest x1 18.8 us: shards(): lax.all_to_all(payload.reshape(32, 160, 128), T, 0, 0, tiled=True)]
    all_to_all x0 -> x1, blocking collectives: none -> 14.9 us  [shards(): lax.all_to_all(chip.reshape(16, 8, 640).transpose(1, 0, 2), 'dp', 0, 0, t...]
    all_to_all x0 -> x2, starting transfers between devices: none -> 13.8 us  [the longest x1 6.89 us: shards(): lax.all_to_all(jnp.broadcast_to(chip[None], (16, 8, 16, 640)), XY, 0, 0,...]
    unnamed x16 -> x22, local copies, waits for them, and re-layouts: 2.32 us -> 15 us
  transfers between devices with their start and end apart: 7 -> 6, of which waited for: 7 -> 3; matrix products, arithmetic and copies ran while one was open for 7% -> 3% of each run, Pallas kernels for 0% -> 12%
where the time goes in v1:
time: 162 us; the launch traced here: 161 us
  waiting for transfers between devices  65.4 us (40%)
  Pallas kernels  27 us (17%)
  local copies, waits for them, and re-layouts  18 us (11%)
  starting transfers between devices  17.5 us (11%)
  blocking collectives  14.9 us (9%)
  between operations  14.2 us (9%)
  other arithmetic  4.27 us (3%)
    all_gather x1, waiting for transfers between devices, shards(): lax.all_gather(jnp.concatenate([tok, cot, side], axis=1), T, axis=0, tile...  45.7 us
    all_to_all x1, waiting for transfers between devices, shards(): lax.all_to_all(payload.reshape(32, 160, 128), T, 0, 0, tiled=True)  18.8 us
    unnamed x22, local copies, waits for them, and re-layouts  15 us
    all_to_all x1, blocking collectives, shards(): lax.all_to_all(chip.reshape(16, 8, 640).transpose(1, 0, 2), 'dp', 0, 0, t...  14.9 us
    pallas_call x1, Pallas kernels, partials(): pl.pallas_call(partial_kernel, grid_spec=pltpu.PrefetchScalarGridSpec(num...  10.3 us
    pallas_call x1, Pallas kernels, grads(): pl.pallas_call(grads_kernel, grid_spec=pltpu.PrefetchScalarGridSpec(num_s...  7.53 us
    all_to_all x1, starting transfers between devices, shards(): lax.all_to_all(jnp.broadcast_to(chip[None], (16, 8, 16, 640)), XY, 0, 0,...  6.89 us
    all_to_all x1, starting transfers between devices, shards(): lax.all_to_all(payload.reshape(32, 160, 128), T, 0, 0, tiled=True)  6.87 us
  transfers between devices with their start and end apart: 6, of which 3 were waited for; matrix products, arithmetic and copies ran while one was open for 3% of the time, Pallas kernels for 12%

profile of v1, /device:TPU:1, one launch (start us, length us, event | category | flops | bytes accessed | tf_op | source)
XLA Modules:
  0.0 161.2 jit_solution(7055731237394299738)
XLA Ops:
  7.2 0.8 copy.23
  8.0 0.8 copy.24
  8.7 0.7 select_convert_fusion
  9.5 0.1 pad_maximum_fusion.1
  9.6 0.1 convert_element_type.12
  9.7 1.6 fusion.1
  11.3 0.9 broadcast_select_fusion.2
  12.2 3.3 %collective-permute-start = (bf16[8,5120]{1,0:T(8,128)(2,1)S(1)}, bf16[8,5120]{1,0:T(8,128)(2,1)S(1)}, u32[]{:S(2)}, u32[]{:S(2)}) collective-permute-start(bf16[8,5120]{1,0:T(8,128)(2,1)S(1)} %broadcast_select_fusion.2), channel_id=1, source_target_pairs={{0,1},{1,0},{2,3},{3,2},{4,5},{5,4},{6,7},{7,6},{8,9},{9,8},{10,11... | collective-permute-start | bytes 245768 | tf_op jit(solution)/shard_map/ppermute | solution.py:232
  15.5 0.9 collective-permute-done
  16.5 0.9 broadcast_select_fusion.1
  17.4 14.9 %all_to_all.15 = bf16[8,16,640]{2,1,0:T(8,128)(2,1)S(1)} all-to-all(bf16[8,16,640]{2,1,0:T(8,128)(2,1)S(1)} %bitcast.37), channel_id=1, replica_groups=mesh['dp'=8,'x'=4,'y'=4,'core'=2] {'dp'}, dimensions={0} | all-to-all | bytes 327680 | tf_op jit(solution)/shard_map/all_to_all | solution.py:249
  32.3 1.8 %broadcast_in_dim.21 = bf16[16,8,16,640]{3,2,1,0:T(8,128)(2,1)} broadcast(bf16[8,16,640]{2,1,0:T(8,128)(2,1)S(1)} %all_to_all.15), dimensions={1,2,3} | broadcast | bytes 2785280 | tf_op jit(solution)/shard_map/broadcast_in_dim | solution.py:250
  34.1 6.9 %all-to-all-start.2 = ((bf16[16,8,16,640]{3,2,1,0:T(8,128)(2,1)}), bf16[16,8,16,640]{3,2,1,0:T(8,128)(2,1)S(1)}, u32[]{:S(2)}, u32[]{:S(2)}) async-start(bf16[16,8,16,640]{3,2,1,0:T(8,128)(2,1)} %broadcast_in_dim.21), calls=%async_computation.2 | async-start | bytes 5242880 | tf_op jit(solution)/shard_map/all_to_all | solution.py:250
  41.0 0.0 all-gather.6.cloned.1.call-start
  41.0 45.7 %all-gather.4.cloned.1.call-done.tok.cot = bf16[256,10368]{1,0:T(8,128)(2,1)} async-done(((bf16[8,10368]{1,0:T(8,128)(2,1)}), bf16[256,10368]{1,0:T(8,128)(2,1)}) %all-gather.4.cloned.1.call-update) | async-done | bytes 5308432 | tf_op jit(solution)/shard_map/all_gather | solution.py:244
  86.7 2.5 %copy-done = bf16[256,10368]{1,0:T(8,128)(2,1)S(1)} copy-done((bf16[256,10368]{1,0:T(8,128)(2,1)S(1)}, bf16[256,10368]{1,0:T(8,128)(2,1)}, u32[]{:S(2)}) %copy-start) | copy-done | bytes 5308440
  89.2 1.6 %copy-done.1 = bf16[216,5120]{1,0:T(8,128)(2,1)S(1)} copy-done((bf16[216,5120]{1,0:T(8,128)(2,1)S(1)}, bf16[216,5120]{1,0:T(8,128)(2,1)}, u32[]{:S(2)}) %copy-start.1) | copy-done | bytes 2211864
  90.8 1.6 %copy-done.3 = bf16[216,5120]{1,0:T(8,128)(2,1)S(1)} copy-done((bf16[216,5120]{1,0:T(8,128)(2,1)S(1)}, bf16[216,5120]{1,0:T(8,128)(2,1)}, u32[]{:S(2)}) %copy-start.3) | copy-done | bytes 2211864
  92.5 1.6 %copy-done.5 = bf16[216,5120]{1,0:T(8,128)(2,1)S(1)} copy-done((bf16[216,5120]{1,0:T(8,128)(2,1)S(1)}, bf16[216,5120]{1,0:T(8,128)(2,1)}, u32[]{:S(2)}) %copy-start.5) | copy-done | bytes 2211864
  94.1 5.3 %acts.1.act = bf16[3,216,256]{2,1,0:T(8,128)(2,1)} custom-call(bf16[256,10368]{1,0:T(8,128)(2,1)S(1)} %copy-done, bf16[256,10368]{1,0:T(8,128)(2,1)S(1)} %copy-done, bf16[216,5120]{1,0:T(8,128)(2,1)S(1)} %copy-done.1, bf16[216,5120]{1,0:T(8,128)(2,1)S(1)} %copy-done.3, bf16[216,5120]{1,0:T(8,128)(2,1)S(1)} %copy-done.5), custom_call_target="tpu_custom_call" | custom-call | flops 1698693120 | bytes 11878400 | tf_op jit(solution)/shard_map/acts/pallas_call | solution.py:59
  99.4 0.3 collective-permute-start.1
  99.8 1.6 %copy-done.2 = bf16[216,5120]{1,0:T(8,128)(2,1)S(1)} copy-done((bf16[216,5120]{1,0:T(8,128)(2,1)S(1)}, bf16[216,5120]{1,0:T(8,128)(2,1)}, u32[]{:S(2)}) %copy-start.2) | copy-done | bytes 2211864
  101.4 1.6 %copy-done.4 = bf16[216,5120]{1,0:T(8,128)(2,1)S(1)} copy-done((bf16[216,5120]{1,0:T(8,128)(2,1)S(1)}, bf16[216,5120]{1,0:T(8,128)(2,1)}, u32[]{:S(2)}) %copy-start.4) | copy-done | bytes 2211864
  103.0 10.3 %partials.1 = (bf16[256,5120]{1,0:T(8,128)(2,1)}, bf16[5120,128]{1,0:T(8,128)(2,1)S(1)}) custom-call(s32[32,10]{1,0:T(8,128)S(1)} %bitcast.29, s32[32]{0:T(128)S(1)} %bitcast.34, s32[32,10]{1,0:T(8,128)S(1)} %bitcast.30, s32[32]{0:T(128)S(1)} %bitcast.32, bf16[3,216,256]{2,1,0:T(8,128)(2,1)} %acts.1.act, bf16[216,5120]{1,0:T(8,128)(2,1)S(1)} %copy-done.2, ...), custom_call_target="tpu_custom_call" | custom-call | flops 1698693120 | bytes 11878400 | tf_op jit(solution)/shard_map/partials/pallas_call | solution.py:109
  113.3 1.1 copy-done.7
  114.4 6.9 %all-to-all-start = ((bf16[32,160,128]{2,1,0:T(8,128)(2,1)}), bf16[32,160,128]{2,1,0:T(8,128)(2,1)}, u32[]{:S(2)}, u32[]{:S(2)}) async-start(bf16[32,160,128]{2,1,0:T(8,128)(2,1)} %bitcast.28), calls=%async_computation | async-start | bytes 2621440 | tf_op jit(solution)/shard_map/all_to_all | solution.py:256
  121.3 0.8 slice_bitcast_fusion
  122.2 0.2 reshape.39
  122.4 18.8 %all-to-all-done = bf16[32,160,128]{2,1,0:T(8,128)(2,1)} async-done(((bf16[32,160,128]{2,1,0:T(8,128)(2,1)}), bf16[32,160,128]{2,1,0:T(8,128)(2,1)}, u32[]{:S(2)}, u32[]{:S(2)}) %all-to-all-start) | async-done | bytes 1310752 | tf_op jit(solution)/shard_map/all_to_all | solution.py:256
  141.1 4.0 %unpack.1 = (bf16[8,5120]{1,0:T(8,128)(2,1)}, bf16[8,5120]{1,0:T(8,128)(2,1)}) custom-call(s32[32,20]{1,0:T(8,128)S(1)} %fusion.2.idx, bf16[5120,128]{1,0:T(8,128)(2,1)} %bitcast.8.data), custom_call_target="tpu_custom_call" | custom-call | flops 1000000 | bytes 2000000 | tf_op jit(solution)/shard_map/unpack/pallas_call | solution.py:163
  145.1 1.7 %copy-done.6 = bf16[24,216,256]{2,1,0:T(8,128)(2,1)S(1)} copy-done((bf16[24,216,256]{2,1,0:T(8,128)(2,1)S(1)}, bf16[24,216,256]{2,1,0:T(8,128)(2,1)}, u32[]{:S(2)}) %copy-start.6) | copy-done | bytes 2654232
  146.9 7.5 %grads.1 = (bf16[216,640]{1,0:T(8,128)(2,1)}, bf16[216,640]{1,0:T(8,128)(2,1)}, bf16[216,640]{1,0:T(8,128)(2,1)}) custom-call(s32[1]{0:T(128)} %bitcast.10.core, bf16[8,3,216,256]{3,2,1,0:T(8,128)(2,1)S(1)} %bitcast.27, bf16[16,8,16,640]{3,2,1,0:T(8,128)(2,1)S(1)} %all-to-all-done.2.cm, bf16[16,8,16,640]{3,2,1,0:T(8,128)(2,1)} %collective-permute-done.1.co), custom_call_target="tpu_custom_call" | custom-call | flops 1698693120 | bytes 8000000 | tf_op jit(solution)/shard_map/grads/pallas_call | solution.py:213
  (22 shorter events, 0.2 us)
Async XLA Ops:
  7.2 79.5 %all-gather.4.cloned.1.call-start = ((), (), s32[]{:S(2)}) async-start(), calls=%async_computation.3 | async-start | bytes 5474304 | tf_op jit(solution)/shard_map/all_gather | solution.py:244
  12.2 4.2 %collective-permute-start = (bf16[8,5120]{1,0:T(8,128)(2,1)S(1)}, bf16[8,5120]{1,0:T(8,128)(2,1)S(1)}, u32[]{:S(2)}, u32[]{:S(2)}) collective-permute-start(bf16[8,5120]{1,0:T(8,128)(2,1)S(1)} %broadcast_select_fusion.2), channel_id=1, source_target_pairs={{0,1},{1,0},{2,3},{3,2},{4,5},{5,4},{6,7},{7,6},{8,9},{9,8},{10,11... | collective-permute-start | bytes 245768 | tf_op jit(solution)/shard_map/ppermute | solution.py:232
  34.1 65.7 %copy-start.8 = (s32[1,1,32]{2,1,0:T(1,128)S(1)}, s32[1,1,32]{2,1,0:T(1,128)}, u32[]{:S(2)}) copy-start(s32[1,1,32]{2,1,0:T(1,128)} %param.19) | copy-start | bytes 388
  34.1 65.7 %copy-start.9 = (s32[1,1,32]{2,1,0:T(1,128)S(1)}, s32[1,1,32]{2,1,0:T(1,128)}, u32[]{:S(2)}) copy-start(s32[1,1,32]{2,1,0:T(1,128)} %param.16) | copy-start | bytes 388
  34.1 65.3 %all-to-all-start.2 = ((bf16[16,8,16,640]{3,2,1,0:T(8,128)(2,1)}), bf16[16,8,16,640]{3,2,1,0:T(8,128)(2,1)S(1)}, u32[]{:S(2)}, u32[]{:S(2)}) async-start(bf16[16,8,16,640]{3,2,1,0:T(8,128)(2,1)} %broadcast_in_dim.21), calls=%async_computation.2 | async-start | bytes 5242880 | tf_op jit(solution)/shard_map/all_to_all | solution.py:250
  41.0 104.1 %all-gather.6.cloned.1.call-start = ((), (), s32[]{:S(2)}) async-start(), calls=%async_computation.4 | async-start | bytes 2985984 | tf_op jit(solution)/shard_map/all_gather | solution.py:254
  86.7 2.5 %copy-start = (bf16[256,10368]{1,0:T(8,128)(2,1)S(1)}, bf16[256,10368]{1,0:T(8,128)(2,1)}, u32[]{:S(2)}) copy-start(bf16[256,10368]{1,0:T(8,128)(2,1)} %all-gather.4.cloned.1.call-done.tok.cot) | copy-start | bytes 15925252
  89.2 1.6 %copy-start.1 = (bf16[216,5120]{1,0:T(8,128)(2,1)S(1)}, bf16[216,5120]{1,0:T(8,128)(2,1)}, u32[]{:S(2)}) copy-start(bf16[216,5120]{1,0:T(8,128)(2,1)} %wg.3) | copy-start | bytes 6635524
  90.8 1.6 %copy-start.3 = (bf16[216,5120]{1,0:T(8,128)(2,1)S(1)}, bf16[216,5120]{1,0:T(8,128)(2,1)}, u32[]{:S(2)}) copy-start(bf16[216,5120]{1,0:T(8,128)(2,1)} %wu.3) | copy-start | bytes 6635524
  92.5 1.6 %copy-start.5 = (bf16[216,5120]{1,0:T(8,128)(2,1)S(1)}, bf16[216,5120]{1,0:T(8,128)(2,1)}, u32[]{:S(2)}) copy-start(bf16[216,5120]{1,0:T(8,128)(2,1)} %wd.3) | copy-start | bytes 6635524
  99.4 45.7 %collective-permute-start.1 = (bf16[16,8,16,640]{3,2,1,0:T(8,128)(2,1)S(1)}, bf16[16,8,16,640]{3,2,1,0:T(8,128)(2,1)}, u32[]{:S(2)}, u32[]{:S(2)}) collective-permute-start(bf16[16,8,16,640]{3,2,1,0:T(8,128)(2,1)S(1)} %all-to-all-done.2.cm), channel_id=1, source_target_pairs={{0,1},{1,0},{2,3},{3,2},{4,5},{5,4},{6,7},{7,6},{8,9},{9,8},{10,11... | collective-permute-start | bytes 7864328 | tf_op jit(solution)/shard_map/ppermute | solution.py:232
  99.8 1.6 %copy-start.2 = (bf16[216,5120]{1,0:T(8,128)(2,1)S(1)}, bf16[216,5120]{1,0:T(8,128)(2,1)}, u32[]{:S(2)}) copy-start(bf16[216,5120]{1,0:T(8,128)(2,1)} %wg.3) | copy-start | bytes 6635524
  101.4 1.6 %copy-start.4 = (bf16[216,5120]{1,0:T(8,128)(2,1)S(1)}, bf16[216,5120]{1,0:T(8,128)(2,1)}, u32[]{:S(2)}) copy-start(bf16[216,5120]{1,0:T(8,128)(2,1)} %wu.3) | copy-start | bytes 6635524
  113.3 1.1 copy-start.7
  114.4 26.7 %all-to-all-start = ((bf16[32,160,128]{2,1,0:T(8,128)(2,1)}), bf16[32,160,128]{2,1,0:T(8,128)(2,1)}, u32[]{:S(2)}, u32[]{:S(2)}) async-start(bf16[32,160,128]{2,1,0:T(8,128)(2,1)} %bitcast.28), calls=%async_computation | async-start | bytes 2621440 | tf_op jit(solution)/shard_map/all_to_all | solution.py:256
  145.1 1.8 %copy-start.6 = (bf16[24,216,256]{2,1,0:T(8,128)(2,1)S(1)}, bf16[24,216,256]{2,1,0:T(8,128)(2,1)}, u32[]{:S(2)}) copy-start(bf16[24,216,256]{2,1,0:T(8,128)(2,1)} %all-gather.6.cloned.1.call-done) | copy-start | bytes 7962628
Sparse Core Ops, SparseCore 0:
  11.4 75.2 all-gather.3
  99.5 36.2 all-gather.5

commit v2 on v1

v2 whole, which is shorter than its diff:
```python
import jax
import jax.numpy as jnp
from jax import lax
from jax.experimental import pallas as pl
from jax.experimental.pallas import tpu as pltpu
from jax.sharding import Mesh, PartitionSpec as P

T = ("x", "y", "core")
XY = ("x", "y")
D = 5120
F = 216
G = 256
KMAX = 10
MSG = 176
VMEM_LIMIT = 60 << 20
BF = jnp.bfloat16
F32 = jnp.float32


def nt(a, b):
    return lax.dot_general(a, b, (((1,), (1,)), ((), ())), preferred_element_type=F32)


def tn(a, b):
    return lax.dot_general(a, b, (((0,), (0,)), ((), ())), preferred_element_type=F32)


def nn(a, b):
    return lax.dot_general(a, b, (((1,), (0,)), ((), ())), preferred_element_type=F32)


def acts_kernel(order, tok, cot, wg, wu, wd, nat, out, ga, ua, hb):
    k = pl.program_id(0)

    @pl.when(k == 0)
    def _():
        ga[...] = jnp.zeros_like(ga)
        ua[...] = jnp.zeros_like(ua)
        hb[...] = jnp.zeros_like(hb)

    t = tok[...]
    ga[...] += nt(t, wg[...])
    ua[...] += nt(t, wu[...])
    hb[...] += nt(cot[...], wd[...])

    @pl.when(k == pl.num_programs(0) - 1)
    def _():
        g, u, b = ga[...], ua[...], hb[...]
        s = jax.nn.sigmoid(g)
        silu = g * s
        place = (lax.broadcasted_iota(jnp.int32, (G, G), 0) == order[0:1, :]).astype(BF)
        values = (b * u * (s * (1.0 + g * (1.0 - s))), b * silu, silu * u)
        for j in range(3):
            v = values[j].astype(BF)
            nat[j] = v
            out[j] = tn(v, place).astype(BF)


def acts(order, rows, wg, wu, wd):
    kb = 1280
    steps = D // kb
    wspec = pl.BlockSpec((F, kb), lambda k: (0, k))
    return pl.pallas_call(
        acts_kernel,
        grid=(steps,),
        in_specs=[
            pl.BlockSpec((8, G), lambda k: (0, 0)),
            pl.BlockSpec((G, kb), lambda k: (0, k)),
            pl.BlockSpec((G, kb), lambda k: (0, k + steps)),
            wspec,
            wspec,
            wspec,
        ],
        out_specs=[
            pl.BlockSpec((3, G, F), lambda k: (0, 0, 0)),
            pl.BlockSpec((3, F, G), lambda k: (0, 0, 0)),
        ],
        out_shape=[
            jax.ShapeDtypeStruct((3, G, F), BF),
            jax.ShapeDtypeStruct((3, F, G), BF),
        ],
        scratch_shapes=[pltpu.VMEM((G, F), F32)] * 3,
        compiler_params=pltpu.CompilerParams(vmem_limit_bytes=VMEM_LIMIT),
        cost_estimate=pl.CostEstimate(
            flops=6 * G * F * D, bytes_accessed=2 * (2 * G * D + 3 * F * D), transcendentals=G * F
        ),
        name="acts",
    )(order, rows, rows, wg, wu, wd)


def partial_kernel(
    fb, fc, bb, bc, act, side, wg, wu, wd, res, res_next, payload, sf, sb, pk
):
    n = pl.program_id(0)
    nb = wg.shape[1]
    cols = pl.ds(pl.multiple_of(n * nb, nb), nb)
    sf[:, cols] = nn(act[2], wd[...]) + res[...].astype(F32)
    sb[:, cols] = nn(act[0], wg[...]) + nn(act[1], wu[...])

    @pl.when(n == pl.num_programs(0) - 1)
    def _():
        def one(t, carry):
            r = pl.ds(pl.multiple_of(t * 8, 8), 8)
            count = fc[t]
            for j in range(KMAX):
                at = pl.ds(pl.multiple_of(fb[t, j] * 128, 128), 128)
                tile = sf[r, at]
                pk[pl.ds(pl.multiple_of(t * MSG + j * 8, 8), 8), :] = tile
                sf[r, at] = jnp.where(j < count, 0.0, tile)
                ab = pl.ds(pl.multiple_of(bb[t, j] * 128, 128), 128)
                pk[pl.ds(pl.multiple_of(t * MSG + 80 + j * 8, 8), 8), :] = sb[r, ab]
            pk[pl.ds(pl.multiple_of(t * MSG + 160, 8), 16), :] = side[t]
            return carry

        lax.fori_loop(0, 32, one, 0)
        payload[...] = pk[...].astype(BF)
        res_next[...] = sf[...].astype(BF)


def partials(fb, fc, bb, bc, act, side, wg, wu, wd, res):
    nb = 1280
    wspec = pl.BlockSpec((F, nb), lambda n, *_: (0, n))
    return pl.pallas_call(
        partial_kernel,
        grid_spec=pltpu.PrefetchScalarGridSpec(
            num_scalar_prefetch=4,
            grid=(D // nb,),
            in_specs=[
                pl.BlockSpec((3, G, F), lambda n, *_: (0, 0, 0)),
                pl.BlockSpec((32, 16, 128), lambda n, *_: (0, 0, 0)),
                wspec,
                wspec,
                wspec,
                pl.BlockSpec((G, nb), lambda n, *_: (0, n)),
            ],
            out_specs=[
                pl.BlockSpec((G, D), lambda n, *_: (0, 0)),
                pl.BlockSpec((32 * MSG, 128), lambda n, *_: (0, 0)),
            ],
            scratch_shapes=[
                pltpu.VMEM((G, D), F32),
                pltpu.VMEM((G, D), F32),
                pltpu.VMEM((32 * MSG, 128), F32),
            ],
        ),
        out_shape=[
            jax.ShapeDtypeStruct((G, D), BF),
            jax.ShapeDtypeStruct((32 * MSG, 128), BF),
        ],
        compiler_params=pltpu.CompilerParams(vmem_limit_bytes=VMEM_LIMIT),
        cost_estimate=pl.CostEstimate(
            flops=6 * G * F * D, bytes_accessed=2 * (2 * G * D + 3 * F * D), transcendentals=0
        ),
        name="partials",
    )(fb, fc, bb, bc, act, side, wg, wu, wd, res)


def unpack_kernel(idx, data, of, ob, pk, af, ab):
    pk[...] = data[...].astype(F32)
    af[...] = jnp.zeros_like(af)
    ab[...] = jnp.zeros_like(ab)

    def one(t, carry):
        for j in range(KMAX):
            cf = pl.ds(pl.multiple_of(idx[t, j] * 128, 128), 128)
            cb = pl.ds(pl.multiple_of(idx[t, KMAX + j] * 128, 128), 128)
            af[:, cf] += pk[pl.ds(pl.multiple_of(t * MSG + j * 8, 8), 8), :]
            ab[:, cb] += pk[pl.ds(pl.multiple_of(t * MSG + 80 + j * 8, 8), 8), :]
        return carry

    lax.fori_loop(0, 32, one, 0)
    of[...] = af[:, :D].astype(BF)
    ob[...] = ab[:, :D].astype(BF)


def unpack(idx, data):
    whole = pl.BlockSpec(memory_space=pltpu.VMEM)
    return pl.pallas_call(
        unpack_kernel,
        in_specs=[pl.BlockSpec(memory_space=pltpu.SMEM), whole],
        out_specs=[whole, whole],
        out_shape=[jax.ShapeDtypeStruct((8, D), BF)] * 2,
        scratch_shapes=[
            pltpu.VMEM((32 * MSG, 128), F32),
            pltpu.VMEM((8, D + 128), F32),
            pltpu.VMEM((8, D + 128), F32),
        ],
        compiler_params=pltpu.CompilerParams(vmem_limit_bytes=VMEM_LIMIT),
        cost_estimate=pl.CostEstimate(flops=10**6, bytes_accessed=2 * 10**6, transcendentals=0),
        name="unpack",
    )(idx, data)


def grads_kernel(core, *refs):
    act, mine, other = refs[0], refs[1:9], refs[9:17]
    og, ou, od = refs[17:]

    def rows(pieces, s, n0, n1):
        blocks = []
        for i in range(4):
            for j in range(4):
                if s < 4:
                    blocks.append(pieces[i][j, s, :, n0:n1])
                else:
                    blocks.append(pieces[4 + j][i, s - 4, :, n0:n1])
        return jnp.concatenate(blocks, axis=0)

    def run(tok, cot):
        for pieces, wanted in ((tok, ((0, og), (1, ou))), (cot, ((2, od),))):
            for n0, n1 in ((0, 256), (256, 512), (512, 640)):
                total = [None] * len(wanted)
                for s in range(8):
                    rhs = rows(pieces, s, n0, n1)
                    for q, (j, _) in enumerate(wanted):
                        term = nn(act[s, j], rhs)
                        total[q] = term if total[q] is None else total[q] + term
                for q, (_, out) in enumerate(wanted):
                    out[:, n0:n1] = total[q].astype(BF)

    @pl.when(core[0] == 0)
    def _():
        run(mine, other)

    @pl.when(core[0] != 0)
    def _():
        run(other, mine)


def grads(core, act, mine, other):
    whole = pl.BlockSpec(memory_space=pltpu.VMEM)
    return pl.pallas_call(
        grads_kernel,
        in_specs=[pl.BlockSpec(memory_space=pltpu.SMEM)] + [whole] * 17,
        out_specs=[whole] * 3,
        out_shape=[jax.ShapeDtypeStruct((F, 640), BF)] * 3,
        compiler_params=pltpu.CompilerParams(vmem_limit_bytes=VMEM_LIMIT),
        cost_estimate=pl.CostEstimate(
            flops=6 * G * F * D, bytes_accessed=8 * 10**6, transcendentals=0
        ),
        name="grads",
    )(core, act, *mine, *other)


def swap_core(v):
    return lax.ppermute(v, "core", [(0, 1), (1, 0)])


def shift(v, axis, size, by):
    return lax.ppermute(v, axis, [(i, (i + by) % size) for i in range(size)])


def shards(tok, wg, wu, wd, res, fb, fc, cot, bb, bc):
    core = lax.axis_index("core")
    first = core == 0
    which = core.astype(jnp.int32).reshape(1)
    fb, fc, bb, bc = fb[0, 0], fc[0, 0], bb[0, 0], bc[0, 0]

    rows = lax.all_gather(jnp.concatenate([tok, cot], axis=1), T, axis=0, tiled=True)

    other = swap_core(jnp.where(first, cot, tok))
    chip = jnp.concatenate([jnp.where(first, tok, other), jnp.where(first, other, cot)], axis=0)
    cols = lax.all_to_all(chip.reshape(16, 8, 640).transpose(1, 0, 2), "dp", 0, 0, tiled=True)
    halves = [cols[:4], cols[4:]]
    steps = [shift(halves[h], a, 4, s) for s in (2, 1, 3) for h, a in ((0, "x"), (1, "y"))]
    steps = lax.optimization_barrier(tuple(steps))
    four = [jnp.stack([halves[h], steps[2 + h], steps[h], steps[4 + h]]) for h in range(2)]
    four = lax.optimization_barrier(tuple(four))
    mine = [four[0], None, None, None, four[1], None, None, None]
    for s in (2, 1, 3):
        mine[s] = shift(four[0], "y", 4, s)
        mine[4 + s] = shift(four[1], "x", 4, s)
    rows, *mine = lax.optimization_barrier((rows, *mine))

    x, y = lax.axis_index("x"), lax.axis_index("y")
    a = jnp.arange(G)
    order = (((x - (a // 16) % 4) % 4) * 4 + (y - a // 64) % 4) * 16 + a % 16
    order = jnp.broadcast_to(order.astype(jnp.int32)[None], (8, G))
    slots = jnp.arange(KMAX)[None, :]
    lists = jnp.concatenate(
        [jnp.where(slots < fc[:, None], fb, 40), jnp.where(slots < bc[:, None], bb, 40)], axis=1
    )
    lists = jnp.broadcast_to(lists[:, None, :], (32, 16, 2 * KMAX))
    side = jnp.pad(lists, ((0, 0), (0, 0), (0, 128 - 2 * KMAX))).astype(F32)

    nat, act = acts(order, rows, wg, wu, wd)
    everyone = lax.all_gather(act[None], "dp", axis=0, tiled=True)
    res_next, payload = partials(fb, fc, bb, bc, nat, side, wg, wu, wd, res[0, 0])
    received = lax.all_to_all(payload.reshape(32, MSG, 128), T, 0, 0, tiled=True)
    res_next, *mine = lax.optimization_barrier((res_next, *mine))
    others = [swap_core(v) for v in mine]
    idx = received[:, 160, : 2 * KMAX].astype(jnp.int32)
    layer_output, input_gradient = unpack(idx, received.reshape(32 * MSG, 128))
    gate_gradient, up_gradient, down_gradient = grads(which, everyone, mine, others)
    return (
        layer_output,
        res_next[None, None],
        input_gradient,
        gate_gradient,
        up_gradient,
        down_gradient,
    )


def solution(mesh):
    fine = Mesh(mesh.devices.reshape(8, 4, 4, 2), ("dp", "x", "y", "core"))
    row = P(("dp",) + T, None)
    return jax.shard_map(
        shards,
        mesh=fine,
        in_specs=(
            row,
            P(T, None),
            P(T, None),
            P(T, None),
            P("dp", T, None, None),
            P("dp", T, None, None),
            P("dp", T, None),
            row,
            P("dp", T, None, None),
            P("dp", T, None),
        ),
        out_specs=(row, P("dp", T, None, None), row, P(T, "dp"), P(T, "dp"), P(T, "dp")),
        check_vma=False,
    )
```

time: 162 us -> 143 us (0.88)
  waiting for transfers between devices: 65.4 us -> 49.6 us
  local copies, waits for them, and re-layouts: 18 us -> 2.93 us
  starting transfers between devices: 17.5 us -> 27.1 us
  Pallas kernels: 27 us -> 29 us
    all_gather x1, waiting for transfers between devices: 45.7 us -> 7.34 us  [shards(): lax.all_gather(jnp.concatenate([tok, cot], axis=1), T, axis=0, tiled=True)]
    ppermute x0 -> x12, waiting for transfers between devices: none -> 22.9 us  [shift(): return lax.ppermute(v, axis, [(i, (i + by) % size) for i in range(size)])]
    ppermute x0 -> x12, starting transfers between devices: none -> 17.3 us  [shift(): return lax.ppermute(v, axis, [(i, (i + by) % size) for i in range(size)])]
    unnamed x22 -> x44, local copies, waits for them, and re-layouts: 15 us -> 2.26 us
    all_to_all x2 -> x1, starting transfers between devices: 13.8 us -> 4.3 us  [shards(): lax.all_to_all(payload.reshape(32, MSG, 128), T, 0, 0, tiled=True)]
    ppermute x2 -> x9, starting transfers between devices: 3.67 us -> 5.38 us  [swap_core(): return lax.ppermute(v, 'core', [(0, 1), (1, 0)])]
    all_to_all x2 -> x1, waiting for transfers between devices: 18.8 us -> 17.1 us  [shards(): lax.all_to_all(payload.reshape(32, MSG, 128), T, 0, 0, tiled=True)]
  transfers between devices with their start and end apart: 6 -> 24, of which waited for: 3 -> 12; matrix products, arithmetic and copies ran while one was open for 3% -> 3% of each run, Pallas kernels for 12% -> 10%
where the time goes in v2:
time: 143 us
  waiting for transfers between devices  49.6 us (35%)
  Pallas kernels  29 us (20%)
  starting transfers between devices  27.1 us (19%)
  blocking collectives  14.9 us (10%)
  between operations  14.3 us (10%)
  other arithmetic  5.09 us (4%)
  local copies, waits for them, and re-layouts  2.93 us (2%)
    ppermute x12, waiting for transfers between devices, shift(): return lax.ppermute(v, axis, [(i, (i + by) % size) for i in range(size)])  22.9 us
    ppermute x12, starting transfers between devices, shift(): return lax.ppermute(v, axis, [(i, (i + by) % size) for i in range(size)])  17.3 us
    all_to_all x1, waiting for transfers between devices, shards(): lax.all_to_all(payload.reshape(32, MSG, 128), T, 0, 0, tiled=True)  17.1 us
    all_to_all x1, blocking collectives, shards(): lax.all_to_all(chip.reshape(16, 8, 640).transpose(1, 0, 2), 'dp', 0, 0, t...  14.9 us
    pallas_call x1, Pallas kernels, partials(): pl.pallas_call(partial_kernel, grid_spec=pltpu.PrefetchScalarGridSpec(num...  11 us
    pallas_call x1, Pallas kernels, acts(): pl.pallas_call(acts_kernel, grid=(steps,), in_specs=[pl.BlockSpec((8, G),...  7.63 us
    all_gather x1, waiting for transfers between devices, shards(): lax.all_gather(jnp.concatenate([tok, cot], axis=1), T, axis=0, tiled=True)  7.34 us
    pallas_call x1, Pallas kernels, grads(): pl.pallas_call(grads_kernel, in_specs=[pl.BlockSpec(memory_space=pltpu.SM...  6.41 us
  transfers between devices with their start and end apart: 24, of which 12 were waited for; matrix products, arithmetic and copies ran while one was open for 3% of the time, Pallas kernels for 10%

profile of v2, /device:TPU:1, one launch (start us, length us, event | category | flops | bytes accessed | tf_op | source)
XLA Modules:
  0.0 142.9 jit_solution(3521720070527057347)
XLA Ops:
  7.2 1.6 %pad_maximum_fusion.2 = bf16[8,10240]{1,0:T(8,128)(2,1)} fusion(bf16[8,5120]{1,0:T(8,128)(2,1)} %param.17, bf16[8,5120]{1,0:T(8,128)(2,1)} %param.10), kind=kLoop, calls=%fused_computation.4 | loop fusion | flops 327680 | bytes 327680 | tf_op jit(solution)/shard_map/concatenate | solution.py:258
  8.9 0.9 broadcast_select_fusion.2
  9.8 3.3 %collective-permute-start = (bf16[8,5120]{1,0:T(8,128)(2,1)S(1)}, bf16[8,5120]{1,0:T(8,128)(2,1)S(1)}, u32[]{:S(2)}, u32[]{:S(2)}) collective-permute-start(bf16[8,5120]{1,0:T(8,128)(2,1)S(1)} %broadcast_select_fusion.2), channel_id=1, source_target_pairs={{0,1},{1,0},{2,3},{3,2},{4,5},{5,4},{6,7},{7,6},{8,9},{9,8},{10,11... | collective-permute-start | bytes 245768 | tf_op jit(solution)/shard_map/ppermute | solution.py:245
  13.1 0.9 collective-permute-done
  14.1 0.9 broadcast_select_fusion.1
  15.0 14.9 %all_to_all.10 = bf16[8,16,640]{2,1,0:T(8,128)(2,1)S(1)} all-to-all(bf16[8,16,640]{2,1,0:T(8,128)(2,1)S(1)} %bitcast.39), channel_id=1, replica_groups=mesh['dp'=8,'x'=4,'y'=4,'core'=2] {'dp'}, dimensions={0} | all-to-all | bytes 327680 | tf_op jit(solution)/shard_map/all_to_all | solution.py:262
  29.9 2.8 %collective-permute-start.6 = (bf16[4,16,640]{2,1,0:T(8,128)(2,1)S(1)}, bf16[4,16,640]{2,1,0:T(8,128)(2,1)S(1)}, u32[]{:S(2)}, u32[]{:S(2)}) collective-permute-start(bf16[4,16,640]{2,1,0:T(8,128)(2,1)S(1)} %get-tuple-element.78), channel_id=1, source_target_pairs={{0,6},{2,0},{4,2},{6,4},{1,7},{3,1},{5,3},{7,5},{8,14},{10,8},{12,... | collective-permute-start | bytes 245768 | tf_op jit(solution)/shard_map/ppermute | solution.py:249
  32.7 1.6 %collective-permute-start.2 = (bf16[4,16,640]{2,1,0:T(8,128)(2,1)S(1)}, bf16[4,16,640]{2,1,0:T(8,128)(2,1)S(1)}, u32[]{:S(2)}, u32[]{:S(2)}) collective-permute-start(bf16[4,16,640]{2,1,0:T(8,128)(2,1)S(1)} %get-tuple-element.78), channel_id=1, source_target_pairs={{0,4},{2,6},{4,0},{6,2},{1,5},{3,7},{5,1},{7,3},{8,12},{10,14},{12... | collective-permute-start | bytes 245768 | tf_op jit(solution)/shard_map/ppermute | solution.py:249
  34.4 1.2 collective-permute-start.3
  35.6 2.5 %collective-permute-start.1 = (bf16[4,16,640]{2,1,0:T(8,128)(2,1)S(1)}, bf16[4,16,640]{2,1,0:T(8,128)(2,1)S(1)}, u32[]{:S(2)}, u32[]{:S(2)}) collective-permute-start(bf16[4,16,640]{2,1,0:T(8,128)(2,1)S(1)} %get-tuple-element.79), channel_id=1, source_target_pairs={{0,16},{8,24},{16,0},{24,8},{1,17},{9,25},{17,1},{25,9},{2,18},{10... | collective-permute-start | bytes 245768 | tf_op jit(solution)/shard_map/ppermute | solution.py:249
  38.0 1.2 collective-permute-start.5
  39.2 1.9 %collective-permute-done.1 = bf16[4,16,640]{2,1,0:T(8,128)(2,1)S(1)} collective-permute-done((bf16[4,16,640]{2,1,0:T(8,128)(2,1)S(1)}, bf16[4,16,640]{2,1,0:T(8,128)(2,1)S(1)}, u32[]{:S(2)}, u32[]{:S(2)}) %collective-permute-start.1) | collective-permute-done | bytes 81952 | tf_op jit(solution)/shard_map/ppermute | solution.py:249
  41.1 0.5 collective-permute-done.5
  41.8 1.2 collective-permute-start.9
  43.0 2.0 %collective-permute-start.8 = (bf16[4,4,16,640]{3,2,1,0:T(8,128)(2,1)S(1)}, bf16[4,4,16,640]{3,2,1,0:T(8,128)(2,1)S(1)}, u32[]{:S(2)}, u32[]{:S(2)}) collective-permute-start(bf16[4,4,16,640]{3,2,1,0:T(8,128)(2,1)S(1)} %get-tuple-element.65.refs_1_), channel_id=1, source_target_pairs={{0,4},{2,6},{4,0},{6,2},{1,5},{3,7},{5,1},{7,3},{8,12},{10,14},{12... | collective-permute-start | bytes 983048 | tf_op jit(solution)/shard_map/ppermute | solution.py:249
  44.9 2.4 %collective-permute-start.12 = (bf16[4,4,16,640]{3,2,1,0:T(8,128)(2,1)S(1)}, bf16[4,4,16,640]{3,2,1,0:T(8,128)(2,1)S(1)}, u32[]{:S(2)}, u32[]{:S(2)}) collective-permute-start(bf16[4,4,16,640]{3,2,1,0:T(8,128)(2,1)S(1)} %get-tuple-element.69.refs_5_), channel_id=1, source_target_pairs={{0,24},{8,0},{16,8},{24,16},{1,25},{9,1},{17,9},{25,17},{2,26},{10... | collective-permute-start | bytes 983048 | tf_op jit(solution)/shard_map/ppermute | solution.py:249
  47.8 2.3 %collective-permute-start.10 = (bf16[4,4,16,640]{3,2,1,0:T(8,128)(2,1)S(1)}, bf16[4,4,16,640]{3,2,1,0:T(8,128)(2,1)S(1)}, u32[]{:S(2)}, u32[]{:S(2)}) collective-permute-start(bf16[4,4,16,640]{3,2,1,0:T(8,128)(2,1)S(1)} %get-tuple-element.69.refs_5_), channel_id=1, source_target_pairs={{0,8},{8,16},{16,24},{24,0},{1,9},{9,17},{17,25},{25,1},{2,10},{10... | collective-permute-start | bytes 983048 | tf_op jit(solution)/shard_map/ppermute | solution.py:249
  50.5 9.3 %collective-permute-done.7.refs_2_ = bf16[4,4,16,640]{3,2,1,0:T(8,128)(2,1)S(1)} collective-permute-done((bf16[4,4,16,640]{3,2,1,0:T(8,128)(2,1)S(1)}, bf16[4,4,16,640]{3,2,1,0:T(8,128)(2,1)S(1)}, u32[]{:S(2)}, u32[]{:S(2)}) %collective-permute-start.7) | collective-permute-done | bytes 327712 | tf_op jit(solution)/shard_map/ppermute | solution.py:249
  59.8 10.5 %collective-permute-done.10.refs_6_ = bf16[4,4,16,640]{3,2,1,0:T(8,128)(2,1)S(1)} collective-permute-done((bf16[4,4,16,640]{3,2,1,0:T(8,128)(2,1)S(1)}, bf16[4,4,16,640]{3,2,1,0:T(8,128)(2,1)S(1)}, u32[]{:S(2)}, u32[]{:S(2)}) %collective-permute-start.10) | collective-permute-done | bytes 327712 | tf_op jit(solution)/shard_map/ppermute | solution.py:249
  70.3 7.3 %all-gather.4.cloned.1.call-done.tok.cot = bf16[256,10240]{1,0:T(8,128)(2,1)} async-done(((bf16[8,10240]{1,0:T(8,128)(2,1)}), bf16[256,10240]{1,0:T(8,128)(2,1)}) %all-gather.4.cloned.1.call-update) | async-done | bytes 5242896 | tf_op jit(solution)/shard_map/all_gather | solution.py:258
  77.7 0.6 broadcast_in_dim.24.order
  78.3 7.6 %acts.1 = (bf16[3,256,216]{2,1,0:T(8,128)(2,1)}, bf16[3,216,256]{2,1,0:T(8,128)(2,1)}) custom-call(s32[8,256]{1,0:T(8,128)} %broadcast_in_dim.24.order, bf16[256,10240]{1,0:T(8,128)(2,1)} %all-gather.4.cloned.1.call-done.tok.cot, bf16[256,10240]{1,0:T(8,128)(2,1)} %all-gather.4.cloned.1.call-done.tok.cot, bf16[216,5120]{1,0:T(8,128)(2,1)} %wg.3, ...), custom_call_target="tpu_custom_call" | custom-call | flops 1698693120 | bytes 11878400 | tf_op jit(solution)/shard_map/acts/pallas_call | solution.py:63
  86.3 0.7 pad_convert_fusion.side
  87.1 11.0 %partials.1 = (bf16[256,5120]{1,0:T(8,128)(2,1)}, bf16[5632,128]{1,0:T(8,128)(2,1)}) custom-call(s32[32,10]{1,0:T(8,128)} %bitcast.40, s32[32]{0:T(128)} %bitcast.48, s32[32,10]{1,0:T(8,128)} %bitcast.41, s32[32]{0:T(128)} %bitcast.50, bf16[3,256,216]{2,1,0:T(8,128)(2,1)} %get-tuple-element.50.act, f32[32,16,128]{2,1,0:T(8,128)} %pad_convert_fusion.side, ...), custom_call_target="tpu_custom_call" | custom-call | flops 1698693120 | bytes 11878400 | tf_op jit(solution)/shard_map/partials/pallas_call | solution.py:123
  98.0 4.3 %all-to-all-start.1 = ((bf16[32,176,128]{2,1,0:T(8,128)(2,1)}), bf16[32,176,128]{2,1,0:T(8,128)(2,1)S(1)}, u32[]{:S(2)}, u32[]{:S(2)}) async-start(bf16[32,176,128]{2,1,0:T(8,128)(2,1)} %bitcast.37), calls=%async_computation.1 | async-start | bytes 2883584 | tf_op jit(solution)/shard_map/all_to_all | solution.py:288
  104.8 0.7 collective-permute-done.15.refs_11_
  105.5 0.7 copy-done.11
  106.5 17.1 %all-to-all-done.1 = bf16[32,176,128]{2,1,0:T(8,128)(2,1)S(1)} async-done(((bf16[32,176,128]{2,1,0:T(8,128)(2,1)}), bf16[32,176,128]{2,1,0:T(8,128)(2,1)S(1)}, u32[]{:S(2)}, u32[]{:S(2)}) %all-to-all-start.1) | async-done | bytes 1441824 | tf_op jit(solution)/shard_map/all_to_all | solution.py:288
  123.6 0.7 fusion.2.idx
  124.7 4.0 %unpack.1 = (bf16[8,5120]{1,0:T(8,128)(2,1)}, bf16[8,5120]{1,0:T(8,128)(2,1)}) custom-call(s32[32,20]{1,0:T(8,128)} %fusion.2.idx, bf16[5632,128]{1,0:T(8,128)(2,1)} %bitcast.34), custom_call_target="tpu_custom_call" | custom-call | flops 1000000 | bytes 2000000 | tf_op jit(solution)/shard_map/unpack/pallas_call | solution.py:178
  128.8 0.6 copy-done.12
  129.6 6.4 %grads.1 = (bf16[216,640]{1,0:T(8,128)(2,1)}, bf16[216,640]{1,0:T(8,128)(2,1)}, bf16[216,640]{1,0:T(8,128)(2,1)}) custom-call(s32[1]{0:T(128)} %bitcast.18.core, bf16[8,3,216,256]{3,2,1,0:T(8,128)(2,1)} %bitcast.35, bf16[4,4,16,640]{3,2,1,0:T(8,128)(2,1)} %copy-done.1, bf16[4,4,16,640]{3,2,1,0:T(8,128)(2,1)} %copy-done.5, bf16[4,4,16,640]{3,2,1,0:T(8,128)(2,1)} %copy-done.4, ...), custom_call_target="tpu_custom_call" | custom-call | flops 1698693120 | bytes 8000000 | tf_op jit(solution)/shard_map/grads/pallas_call | solution.py:231
  (82 shorter events, 4.9 us)
Async XLA Ops:
  7.2 70.5 %all-gather.4.cloned.1.call-start = ((), (), s32[]{:S(2)}) async-start(), calls=%async_computation.2 | async-start | bytes 5406720 | tf_op jit(solution)/shard_map/all_gather | solution.py:258
  8.8 119.9 %all-gather.6.cloned.1.call-start = ((), (), s32[]{:S(2)}) async-start(), calls=%async_computation.3 | async-start | bytes 2985984 | tf_op jit(solution)/shard_map/all_gather | solution.py:286
  9.8 4.2 %collective-permute-start = (bf16[8,5120]{1,0:T(8,128)(2,1)S(1)}, bf16[8,5120]{1,0:T(8,128)(2,1)S(1)}, u32[]{:S(2)}, u32[]{:S(2)}) collective-permute-start(bf16[8,5120]{1,0:T(8,128)(2,1)S(1)} %broadcast_select_fusion.2), channel_id=1, source_target_pairs={{0,1},{1,0},{2,3},{3,2},{4,5},{5,4},{6,7},{7,6},{8,9},{9,8},{10,11... | collective-permute-start | bytes 245768 | tf_op jit(solution)/shard_map/ppermute | solution.py:245
  29.9 8.1 %collective-permute-start.6 = (bf16[4,16,640]{2,1,0:T(8,128)(2,1)S(1)}, bf16[4,16,640]{2,1,0:T(8,128)(2,1)S(1)}, u32[]{:S(2)}, u32[]{:S(2)}) collective-permute-start(bf16[4,16,640]{2,1,0:T(8,128)(2,1)S(1)} %get-tuple-element.78), channel_id=1, source_target_pairs={{0,6},{2,0},{4,2},{6,4},{1,7},{3,1},{5,3},{7,5},{8,14},{10,8},{12,... | collective-permute-start | bytes 245768 | tf_op jit(solution)/shard_map/ppermute | solution.py:249
  32.7 6.5 %collective-permute-start.4 = (bf16[4,16,640]{2,1,0:T(8,128)(2,1)S(1)}, bf16[4,16,640]{2,1,0:T(8,128)(2,1)S(1)}, u32[]{:S(2)}, u32[]{:S(2)}) collective-permute-start(bf16[4,16,640]{2,1,0:T(8,128)(2,1)S(1)} %get-tuple-element.78), channel_id=1, source_target_pairs={{0,2},{2,4},{4,6},{6,0},{1,3},{3,5},{5,7},{7,1},{8,10},{10,12},{12... | collective-permute-start | bytes 245768 | tf_op jit(solution)/shard_map/ppermute | solution.py:249
  32.7 6.5 %collective-permute-start.2 = (bf16[4,16,640]{2,1,0:T(8,128)(2,1)S(1)}, bf16[4,16,640]{2,1,0:T(8,128)(2,1)S(1)}, u32[]{:S(2)}, u32[]{:S(2)}) collective-permute-start(bf16[4,16,640]{2,1,0:T(8,128)(2,1)S(1)} %get-tuple-element.78), channel_id=1, source_target_pairs={{0,4},{2,6},{4,0},{6,2},{1,5},{3,7},{5,1},{7,3},{8,12},{10,14},{12... | collective-permute-start | bytes 245768 | tf_op jit(solution)/shard_map/ppermute | solution.py:249
  34.4 4.8 %collective-permute-start.3 = (bf16[4,16,640]{2,1,0:T(8,128)(2,1)S(1)}, bf16[4,16,640]{2,1,0:T(8,128)(2,1)S(1)}, u32[]{:S(2)}, u32[]{:S(2)}) collective-permute-start(bf16[4,16,640]{2,1,0:T(8,128)(2,1)S(1)} %get-tuple-element.79), channel_id=1, source_target_pairs={{0,8},{8,16},{16,24},{24,0},{1,9},{9,17},{17,25},{25,1},{2,10},{10... | collective-permute-start | bytes 245768 | tf_op jit(solution)/shard_map/ppermute | solution.py:249
  35.6 5.5 %collective-permute-start.1 = (bf16[4,16,640]{2,1,0:T(8,128)(2,1)S(1)}, bf16[4,16,640]{2,1,0:T(8,128)(2,1)S(1)}, u32[]{:S(2)}, u32[]{:S(2)}) collective-permute-start(bf16[4,16,640]{2,1,0:T(8,128)(2,1)S(1)} %get-tuple-element.79), channel_id=1, source_target_pairs={{0,16},{8,24},{16,0},{24,8},{1,17},{9,25},{17,1},{25,9},{2,18},{10... | collective-permute-start | bytes 245768 | tf_op jit(solution)/shard_map/ppermute | solution.py:249
  38.0 3.6 %collective-permute-start.5 = (bf16[4,16,640]{2,1,0:T(8,128)(2,1)S(1)}, bf16[4,16,640]{2,1,0:T(8,128)(2,1)S(1)}, u32[]{:S(2)}, u32[]{:S(2)}) collective-permute-start(bf16[4,16,640]{2,1,0:T(8,128)(2,1)S(1)} %get-tuple-element.79), channel_id=1, source_target_pairs={{0,24},{8,0},{16,8},{24,16},{1,25},{9,1},{17,9},{25,17},{2,26},{10... | collective-permute-start | bytes 245768 | tf_op jit(solution)/shard_map/ppermute | solution.py:249
  41.7 60.6 %copy-start.1 = (bf16[4,4,16,640]{3,2,1,0:T(8,128)(2,1)}, bf16[4,4,16,640]{3,2,1,0:T(8,128)(2,1)S(1)}, u32[]{:S(2)}) copy-start(bf16[4,4,16,640]{3,2,1,0:T(8,128)(2,1)S(1)} %get-tuple-element.65.refs_1_) | copy-start | bytes 983044
  41.7 61.7 %copy-start.2 = (bf16[4,4,16,640]{3,2,1,0:T(8,128)(2,1)}, bf16[4,4,16,640]{3,2,1,0:T(8,128)(2,1)S(1)}, u32[]{:S(2)}) copy-start(bf16[4,4,16,640]{3,2,1,0:T(8,128)(2,1)S(1)} %get-tuple-element.69.refs_5_) | copy-start | bytes 983044
  41.8 6.0 %collective-permute-start.9 = (bf16[4,4,16,640]{3,2,1,0:T(8,128)(2,1)S(1)}, bf16[4,4,16,640]{3,2,1,0:T(8,128)(2,1)S(1)}, u32[]{:S(2)}, u32[]{:S(2)}) collective-permute-start(bf16[4,4,16,640]{3,2,1,0:T(8,128)(2,1)S(1)} %get-tuple-element.65.refs_1_), channel_id=1, source_target_pairs={{0,6},{2,0},{4,2},{6,4},{1,7},{3,1},{5,3},{7,5},{8,14},{10,8},{12,... | collective-permute-start | bytes 983048 | tf_op jit(solution)/shard_map/ppermute | solution.py:249
  43.0 7.5 %collective-permute-start.8 = (bf16[4,4,16,640]{3,2,1,0:T(8,128)(2,1)S(1)}, bf16[4,4,16,640]{3,2,1,0:T(8,128)(2,1)S(1)}, u32[]{:S(2)}, u32[]{:S(2)}) collective-permute-start(bf16[4,4,16,640]{3,2,1,0:T(8,128)(2,1)S(1)} %get-tuple-element.65.refs_1_), channel_id=1, source_target_pairs={{0,4},{2,6},{4,0},{6,2},{1,5},{3,7},{5,1},{7,3},{8,12},{10,14},{12... | collective-permute-start | bytes 983048 | tf_op jit(solution)/shard_map/ppermute | solution.py:249
  44.9 14.9 %collective-permute-start.7 = (bf16[4,4,16,640]{3,2,1,0:T(8,128)(2,1)S(1)}, bf16[4,4,16,640]{3,2,1,0:T(8,128)(2,1)S(1)}, u32[]{:S(2)}, u32[]{:S(2)}) collective-permute-start(bf16[4,4,16,640]{3,2,1,0:T(8,128)(2,1)S(1)} %get-tuple-element.65.refs_1_), channel_id=1, source_target_pairs={{0,2},{2,4},{4,6},{6,0},{1,3},{3,5},{5,7},{7,1},{8,10},{10,12},{12... | collective-permute-start | bytes 983048 | tf_op jit(solution)/shard_map/ppermute | solution.py:249
  44.9 14.9 %collective-permute-start.12 = (bf16[4,4,16,640]{3,2,1,0:T(8,128)(2,1)S(1)}, bf16[4,4,16,640]{3,2,1,0:T(8,128)(2,1)S(1)}, u32[]{:S(2)}, u32[]{:S(2)}) collective-permute-start(bf16[4,4,16,640]{3,2,1,0:T(8,128)(2,1)S(1)} %get-tuple-element.69.refs_5_), channel_id=1, source_target_pairs={{0,24},{8,0},{16,8},{24,16},{1,25},{9,1},{17,9},{25,17},{2,26},{10... | collective-permute-start | bytes 983048 | tf_op jit(solution)/shard_map/ppermute | solution.py:249
  47.3 12.5 %collective-permute-start.11 = (bf16[4,4,16,640]{3,2,1,0:T(8,128)(2,1)S(1)}, bf16[4,4,16,640]{3,2,1,0:T(8,128)(2,1)S(1)}, u32[]{:S(2)}, u32[]{:S(2)}) collective-permute-start(bf16[4,4,16,640]{3,2,1,0:T(8,128)(2,1)S(1)} %get-tuple-element.69.refs_5_), channel_id=1, source_target_pairs={{0,16},{8,24},{16,0},{24,8},{1,17},{9,25},{17,1},{25,9},{2,18},{10... | collective-permute-start | bytes 983048 | tf_op jit(solution)/shard_map/ppermute | solution.py:249
  47.8 55.5 %copy-start.3 = (bf16[4,4,16,640]{3,2,1,0:T(8,128)(2,1)}, bf16[4,4,16,640]{3,2,1,0:T(8,128)(2,1)S(1)}, u32[]{:S(2)}) copy-start(bf16[4,4,16,640]{3,2,1,0:T(8,128)(2,1)S(1)} %collective-permute-done.9.refs_4_) | copy-start | bytes 983044
  47.8 22.6 %collective-permute-start.10 = (bf16[4,4,16,640]{3,2,1,0:T(8,128)(2,1)S(1)}, bf16[4,4,16,640]{3,2,1,0:T(8,128)(2,1)S(1)}, u32[]{:S(2)}, u32[]{:S(2)}) collective-permute-start(bf16[4,4,16,640]{3,2,1,0:T(8,128)(2,1)S(1)} %get-tuple-element.69.refs_5_), channel_id=1, source_target_pairs={{0,8},{8,16},{16,24},{24,0},{1,9},{9,17},{17,25},{25,1},{2,10},{10... | collective-permute-start | bytes 983048 | tf_op jit(solution)/shard_map/ppermute | solution.py:249
  50.5 52.5 %copy-start.4 = (bf16[4,4,16,640]{3,2,1,0:T(8,128)(2,1)}, bf16[4,4,16,640]{3,2,1,0:T(8,128)(2,1)S(1)}, u32[]{:S(2)}) copy-start(bf16[4,4,16,640]{3,2,1,0:T(8,128)(2,1)S(1)} %collective-permute-done.8.refs_3_) | copy-start | bytes 983044
  59.8 42.9 %copy-start.5 = (bf16[4,4,16,640]{3,2,1,0:T(8,128)(2,1)}, bf16[4,4,16,640]{3,2,1,0:T(8,128)(2,1)S(1)}, u32[]{:S(2)}) copy-start(bf16[4,4,16,640]{3,2,1,0:T(8,128)(2,1)S(1)} %collective-permute-done.7.refs_2_) | copy-start | bytes 983044
  59.8 45.7 %copy-start.6 = (bf16[4,4,16,640]{3,2,1,0:T(8,128)(2,1)}, bf16[4,4,16,640]{3,2,1,0:T(8,128)(2,1)S(1)}, u32[]{:S(2)}) copy-start(bf16[4,4,16,640]{3,2,1,0:T(8,128)(2,1)S(1)} %collective-permute-done.12.refs_8_) | copy-start | bytes 983044
  59.8 26.1 %copy-start.7 = (bf16[4,4,16,640]{3,2,1,0:T(8,128)(2,1)}, bf16[4,4,16,640]{3,2,1,0:T(8,128)(2,1)S(1)}, u32[]{:S(2)}) copy-start(bf16[4,4,16,640]{3,2,1,0:T(8,128)(2,1)S(1)} %collective-permute-done.11.refs_7_) | copy-start | bytes 983044
  70.3 15.6 %copy-start.8 = (bf16[4,4,16,640]{3,2,1,0:T(8,128)(2,1)}, bf16[4,4,16,640]{3,2,1,0:T(8,128)(2,1)S(1)}, u32[]{:S(2)}) copy-start(bf16[4,4,16,640]{3,2,1,0:T(8,128)(2,1)S(1)} %collective-permute-done.10.refs_6_) | copy-start | bytes 983044
  98.0 25.5 %all-to-all-start.1 = ((bf16[32,176,128]{2,1,0:T(8,128)(2,1)}), bf16[32,176,128]{2,1,0:T(8,128)(2,1)S(1)}, u32[]{:S(2)}, u32[]{:S(2)}) async-start(bf16[32,176,128]{2,1,0:T(8,128)(2,1)} %bitcast.37), calls=%async_computation.1 | async-start | bytes 2883584 | tf_op jit(solution)/shard_map/all_to_all | solution.py:288
  102.4 1.7 %collective-permute-start.13 = (bf16[4,4,16,640]{3,2,1,0:T(8,128)(2,1)S(1)}, bf16[4,4,16,640]{3,2,1,0:T(8,128)(2,1)S(1)}, u32[]{:S(2)}, u32[]{:S(2)}) collective-permute-start(bf16[4,4,16,640]{3,2,1,0:T(8,128)(2,1)S(1)} %get-tuple-element.65.refs_1_), channel_id=1, source_target_pairs={{0,1},{1,0},{2,3},{3,2},{4,5},{5,4},{6,7},{7,6},{8,9},{9,8},{10,11... | collective-permute-start | bytes 983048 | tf_op jit(solution)/shard_map/ppermute | solution.py:245
  102.7 1.9 %collective-permute-start.14 = (bf16[4,4,16,640]{3,2,1,0:T(8,128)(2,1)S(1)}, bf16[4,4,16,640]{3,2,1,0:T(8,128)(2,1)S(1)}, u32[]{:S(2)}, u32[]{:S(2)}) collective-permute-start(bf16[4,4,16,640]{3,2,1,0:T(8,128)(2,1)S(1)} %collective-permute-done.7.refs_2_), channel_id=1, source_target_pairs={{0,1},{1,0},{2,3},{3,2},{4,5},{5,4},{6,7},{7,6},{8,9},{9,8},{10,11... | collective-permute-start | bytes 983048 | tf_op jit(solution)/shard_map/ppermute | solution.py:245
  103.0 2.5 %collective-permute-start.15 = (bf16[4,4,16,640]{3,2,1,0:T(8,128)(2,1)S(1)}, bf16[4,4,16,640]{3,2,1,0:T(8,128)(2,1)S(1)}, u32[]{:S(2)}, u32[]{:S(2)}) collective-permute-start(bf16[4,4,16,640]{3,2,1,0:T(8,128)(2,1)S(1)} %collective-permute-done.8.refs_3_), channel_id=1, source_target_pairs={{0,1},{1,0},{2,3},{3,2},{4,5},{5,4},{6,7},{7,6},{8,9},{9,8},{10,11... | collective-permute-start | bytes 983048 | tf_op jit(solution)/shard_map/ppermute | solution.py:245
  103.2 25.5 %collective-permute-start.16 = (bf16[4,4,16,640]{3,2,1,0:T(8,128)(2,1)S(1)}, bf16[4,4,16,640]{3,2,1,0:T(8,128)(2,1)}, u32[]{:S(2)}, u32[]{:S(2)}) collective-permute-start(bf16[4,4,16,640]{3,2,1,0:T(8,128)(2,1)S(1)} %collective-permute-done.9.refs_4_), channel_id=1, source_target_pairs={{0,1},{1,0},{2,3},{3,2},{4,5},{5,4},{6,7},{7,6},{8,9},{9,8},{10,11... | collective-permute-start | bytes 983048 | tf_op jit(solution)/shard_map/ppermute | solution.py:245
  103.5 25.2 %collective-permute-start.17 = (bf16[4,4,16,640]{3,2,1,0:T(8,128)(2,1)S(1)}, bf16[4,4,16,640]{3,2,1,0:T(8,128)(2,1)}, u32[]{:S(2)}, u32[]{:S(2)}) collective-permute-start(bf16[4,4,16,640]{3,2,1,0:T(8,128)(2,1)S(1)} %get-tuple-element.69.refs_5_), channel_id=1, source_target_pairs={{0,1},{1,0},{2,3},{3,2},{4,5},{5,4},{6,7},{7,6},{8,9},{9,8},{10,11... | collective-permute-start | bytes 983048 | tf_op jit(solution)/shard_map/ppermute | solution.py:245
  104.1 24.6 %collective-permute-start.18 = (bf16[4,4,16,640]{3,2,1,0:T(8,128)(2,1)}, bf16[4,4,16,640]{3,2,1,0:T(8,128)(2,1)S(1)}, u32[]{:S(2)}, u32[]{:S(2)}) collective-permute-start(bf16[4,4,16,640]{3,2,1,0:T(8,128)(2,1)} %copy-done.8), channel_id=1, source_target_pairs={{0,1},{1,0},{2,3},{3,2},{4,5},{5,4},{6,7},{7,6},{8,9},{9,8},{10,11... | collective-permute-start | bytes 983048 | tf_op jit(solution)/shard_map/ppermute | solution.py:245
  104.6 24.1 %collective-permute-start.19 = (bf16[4,4,16,640]{3,2,1,0:T(8,128)(2,1)}, bf16[4,4,16,640]{3,2,1,0:T(8,128)(2,1)S(1)}, u32[]{:S(2)}, u32[]{:S(2)}) collective-permute-start(bf16[4,4,16,640]{3,2,1,0:T(8,128)(2,1)} %copy-done.7), channel_id=1, source_target_pairs={{0,1},{1,0},{2,3},{3,2},{4,5},{5,4},{6,7},{7,6},{8,9},{9,8},{10,11... | collective-permute-start | bytes 983048 | tf_op jit(solution)/shard_map/ppermute | solution.py:245
  106.2 22.5 %collective-permute-start.20 = (bf16[4,4,16,640]{3,2,1,0:T(8,128)(2,1)S(1)}, bf16[4,4,16,640]{3,2,1,0:T(8,128)(2,1)S(1)}, u32[]{:S(2)}, u32[]{:S(2)}) collective-permute-start(bf16[4,4,16,640]{3,2,1,0:T(8,128)(2,1)S(1)} %collective-permute-done.12.refs_8_), channel_id=1, source_target_pairs={{0,1},{1,0},{2,3},{3,2},{4,5},{5,4},{6,7},{7,6},{8,9},{9,8},{10,11... | collective-permute-start | bytes 983048 | tf_op jit(solution)/shard_map/ppermute | solution.py:245
  (13 other events, 39.7 us)
Sparse Core Ops, SparseCore 0:
  11.1 66.5 all-gather.3
  86.1 36.7 all-gather.5

commit v3 on v2

--- a/solution.py
+++ b/solution.py
@@ -12,7 +12,7 @@
 G = 256
 KMAX = 10
 MSG = 176
-VMEM_LIMIT = 60 << 20
+VMEM_LIMIT = 56 << 20
 BF = jnp.bfloat16
 F32 = jnp.float32
 
@@ -57,7 +57,7 @@
 
 
 def acts(order, rows, wg, wu, wd):
-    kb = 1280
+    kb = 2560
     steps = D // kb
     wspec = pl.BlockSpec((F, kb), lambda k: (0, k))
     return pl.pallas_call(
@@ -88,14 +88,99 @@
     )(order, rows, rows, wg, wu, wd)
 
 
-def partial_kernel(
-    fb, fc, bb, bc, act, side, wg, wu, wd, res, res_next, payload, sf, sb, pk
-):
+def hbm(v):
+    return pltpu.with_memory_space_constraint(v, pltpu.HBM)
+
+
+CHUNK = 1280
+CHUNKS = D // CHUNK
+
+
+def pack_kernel(fb, bb, act, side, wg, wu, wd, res, payload, *scratch):
+    vg, vu, vd, vr, sf, sb, pf, pb, po, sem = scratch
+    loads = []
+    for n, (far, near) in enumerate(((wg, vg), (wu, vu), (wd, vd), (res, vr))):
+        loads.append([])
+        for k in range(CHUNKS):
+            cols = pl.ds(k * CHUNK, CHUNK)
+            at = sem.at[n * CHUNKS + k]
+            loads[-1].append(pltpu.make_async_copy(far.at[:, cols], near.at[:, cols], at))
+    for pair in (loads[:2], loads[2:]):
+        for k in range(CHUNKS):
+            pair[0][k].start()
+            pair[1][k].start()
+
+    def pack(blocks, source, packed):
+        def one(t, carry):
+            r = pl.ds(pl.multiple_of(t * 8, 8), 8)
+            for j in range(KMAX):
+                at = pl.ds(pl.multiple_of(blocks[t, j] * 128, 128), 128)
+                packed[t, j * 8 : j * 8 + 8, :] = source[r, at]
+            return carry
+
+        lax.fori_loop(0, 32, one, 0)
+
+    def send(i, lo, hi):
+        part = pl.ds(lo, hi - lo)
+        return pltpu.make_async_copy(
+            po.at[:, part, :], payload.at[:, part, :], sem.at[4 * CHUNKS + i]
+        )
+
+    for k in range(CHUNKS):
+        cols = pl.ds(k * CHUNK, CHUNK)
+        loads[0][k].wait()
+        loads[1][k].wait()
+        sb[:, cols] = nn(act[0], vg[:, cols]) + nn(act[1], vu[:, cols])
+    pack(bb, sb, pb)
+    po[:, 80:160, :] = pb[...].astype(BF)
+    po[:, 160:MSG, :] = side[...].astype(BF)
+    back = send(0, 80, MSG)
+    back.start()
+    for k in range(CHUNKS):
+        cols = pl.ds(k * CHUNK, CHUNK)
+        loads[2][k].wait()
+        loads[3][k].wait()
+        sf[:, cols] = nn(act[2], vd[:, cols]) + vr[:, cols].astype(F32)
+    pack(fb, sf, pf)
+    po[:, 0:80, :] = pf[...].astype(BF)
+    ahead = send(1, 0, 80)
+    ahead.start()
+    back.wait()
+    ahead.wait()
+
+
+def pack_selected(fb, bb, act, side, wg, wu, wd, res):
+    whole = pl.BlockSpec(memory_space=pltpu.VMEM)
+    smem = pl.BlockSpec(memory_space=pltpu.SMEM)
+    anywhere = pl.BlockSpec(memory_space=pl.ANY)
+    return pl.pallas_call(
+        pack_kernel,
+        in_specs=[smem] * 2 + [whole] * 2 + [anywhere] * 4,
+        out_specs=anywhere,
+        out_shape=pltpu.HBM((32, MSG, 128), BF),
+        scratch_shapes=[pltpu.VMEM((F, D), BF)] * 3
+        + [
+            pltpu.VMEM((G, D), BF),
+            pltpu.VMEM((G, D), F32),
+            pltpu.VMEM((G, D), F32),
+            pltpu.VMEM((32, 80, 128), F32),
+            pltpu.VMEM((32, 80, 128), F32),
+            pltpu.VMEM((32, MSG, 128), BF),
+            pltpu.SemaphoreType.DMA((4 * CHUNKS + 2,)),
+        ],
+        compiler_params=pltpu.CompilerParams(vmem_limit_bytes=VMEM_LIMIT),
+        cost_estimate=pl.CostEstimate(
+            flops=6 * G * F * D, bytes_accessed=2 * (G * D + 3 * F * D), transcendentals=0
+        ),
+        name="pack_selected",
+    )(fb, bb, act, side, hbm(wg), hbm(wu), hbm(wd), hbm(res))
+
+
+def residual_kernel(fb, fc, act, wd, res, res_next, sf):
     n = pl.program_id(0)
-    nb = wg.shape[1]
+    nb = wd.shape[1]
     cols = pl.ds(pl.multiple_of(n * nb, nb), nb)
-    sf[:, cols] = nn(act[2], wd[...]) + res[...].astype(F32)
-    sb[:, cols] = nn(act[0], wg[...]) + nn(act[1], wu[...])
+    sf[:, cols] = nn(act[0], wd[...]) + res[...].astype(F32)
 
     @pl.when(n == pl.num_programs(0) - 1)
     def _():
@@ -104,73 +189,55 @@
             count = fc[t]
             for j in range(KMAX):
                 at = pl.ds(pl.multiple_of(fb[t, j] * 128, 128), 128)
-                tile = sf[r, at]
-                pk[pl.ds(pl.multiple_of(t * MSG + j * 8, 8), 8), :] = tile
-                sf[r, at] = jnp.where(j < count, 0.0, tile)
-                ab = pl.ds(pl.multiple_of(bb[t, j] * 128, 128), 128)
-                pk[pl.ds(pl.multiple_of(t * MSG + 80 + j * 8, 8), 8), :] = sb[r, ab]
-            pk[pl.ds(pl.multiple_of(t * MSG + 160, 8), 16), :] = side[t]
+                sf[r, at] = jnp.where(j < count, 0.0, sf[r, at])
             return carry
 
         lax.fori_loop(0, 32, one, 0)
-        payload[...] = pk[...].astype(BF)
         res_next[...] = sf[...].astype(BF)
 
 
-def partials(fb, fc, bb, bc, act, side, wg, wu, wd, res):
+def next_residual(fb, fc, act, wd, res):
     nb = 1280
-    wspec = pl.BlockSpec((F, nb), lambda n, *_: (0, n))
     return pl.pallas_call(
-        partial_kernel,
+        residual_kernel,
         grid_spec=pltpu.PrefetchScalarGridSpec(
-            num_scalar_prefetch=4,
+            num_scalar_prefetch=2,
             grid=(D // nb,),
             in_specs=[
-                pl.BlockSpec((3, G, F), lambda n, *_: (0, 0, 0)),
-                pl.BlockSpec((32, 16, 128), lambda n, *_: (0, 0, 0)),
-                wspec,
-                wspec,
-                wspec,
+                pl.BlockSpec((1, G, F), lambda n, *_: (2, 0, 0)),
+                pl.BlockSpec((F, nb), lambda n, *_: (0, n)),
                 pl.BlockSpec((G, nb), lambda n, *_: (0, n)),
             ],
-            out_specs=[
-                pl.BlockSpec((G, D), lambda n, *_: (0, 0)),
-                pl.BlockSpec((32 * MSG, 128), lambda n, *_: (0, 0)),
-            ],
-            scratch_shapes=[
-                pltpu.VMEM((G, D), F32),
-                pltpu.VMEM((G, D), F32),
-                pltpu.VMEM((32 * MSG, 128), F32),
-            ],
-        ),
-        out_shape=[
-            jax.ShapeDtypeStruct((G, D), BF),
-            jax.ShapeDtypeStruct((32 * MSG, 128), BF),
-        ],
+            out_specs=pl.BlockSpec((G, D), lambda n, *_: (0, 0)),
+            scratch_shapes=[pltpu.VMEM((G, D), F32)],
+        ),
+        out_shape=jax.ShapeDtypeStruct((G, D), BF),
         compiler_params=pltpu.CompilerParams(vmem_limit_bytes=VMEM_LIMIT),
         cost_estimate=pl.CostEstimate(
-            flops=6 * G * F * D, bytes_accessed=2 * (2 * G * D + 3 * F * D), transcendentals=0
-        ),
-        name="partials",
-    )(fb, fc, bb, bc, act, side, wg, wu, wd, res)
-
-
-def unpack_kernel(idx, data, of, ob, pk, af, ab):
+            flops=2 * G * F * D, bytes_accessed=2 * (2 * G * D + F * D), transcendentals=0
+        ),
+        name="next_residual",
+    )(fb, fc, act, wd, res)
+
+
+def unpack_kernel(idx, data, of, ob, pk, *accs):
     pk[...] = data[...].astype(F32)
-    af[...] = jnp.zeros_like(af)
-    ab[...] = jnp.zeros_like(ab)
-
-    def one(t, carry):
+    for acc in accs:
+        acc[...] = jnp.zeros_like(acc)
+
+    def one(i, carry):
         for j in range(KMAX):
-            cf = pl.ds(pl.multiple_of(idx[t, j] * 128, 128), 128)
-            cb = pl.ds(pl.multiple_of(idx[t, KMAX + j] * 128, 128), 128)
-            af[:, cf] += pk[pl.ds(pl.multiple_of(t * MSG + j * 8, 8), 8), :]
-            ab[:, cb] += pk[pl.ds(pl.multiple_of(t * MSG + 80 + j * 8, 8), 8), :]
+            for q in range(4):
+                t = (q // 2) * 16 + i
+                back = q % 2
+                at = pl.ds(pl.multiple_of(idx[t, back * KMAX + j] * 128, 128), 128)
+                row = pl.multiple_of(t * MSG + back * 80 + j * 8, 8)
+                accs[q][:, at] += pk[pl.ds(row, 8), :]
         return carry
 
-    lax.fori_loop(0, 32, one, 0)
-    of[...] = af[:, :D].astype(BF)
-    ob[...] = ab[:, :D].astype(BF)
+    lax.fori_loop(0, 16, one, 0)
+    of[...] = (accs[0][:, :D] + accs[2][:, :D]).astype(BF)
+    ob[...] = (accs[1][:, :D] + accs[3][:, :D]).astype(BF)
 
 
 def unpack(idx, data):
@@ -182,63 +249,83 @@
         out_shape=[jax.ShapeDtypeStruct((8, D), BF)] * 2,
         scratch_shapes=[
             pltpu.VMEM((32 * MSG, 128), F32),
-            pltpu.VMEM((8, D + 128), F32),
-            pltpu.VMEM((8, D + 128), F32),
-        ],
+        ]
+        + [pltpu.VMEM((8, D + 128), F32)] * 4,
         compiler_params=pltpu.CompilerParams(vmem_limit_bytes=VMEM_LIMIT),
         cost_estimate=pl.CostEstimate(flops=10**6, bytes_accessed=2 * 10**6, transcendentals=0),
         name="unpack",
     )(idx, data)
 
 
-def grads_kernel(core, *refs):
-    act, mine, other = refs[0], refs[1:9], refs[9:17]
-    og, ou, od = refs[17:]
-
-    def rows(pieces, s, n0, n1):
+def grads_kernel(core, act, *refs):
+    far = refs[:16]
+    og, ou, od, av, pv, acc, sem = refs[16:]
+    copies = []
+    for q in range(2):
+        part = pl.ds(4 * q, 4)
+        copies.append([pltpu.make_async_copy(act.at[part], av.at[part], sem.at[16 + q])])
+        for i in (*range(4 * q, 4 * q + 4), *range(8 + 4 * q, 12 + 4 * q)):
+            copies[-1].append(pltpu.make_async_copy(far[i], pv.at[i], sem.at[i]))
+        for c in copies[-1]:
+            c.start()
+
+    def rows(first, s, n0, n1):
         blocks = []
         for i in range(4):
             for j in range(4):
                 if s < 4:
-                    blocks.append(pieces[i][j, s, :, n0:n1])
+                    blocks.append(pv[first + i, j, s, :, n0:n1])
                 else:
-                    blocks.append(pieces[4 + j][i, s - 4, :, n0:n1])
+                    blocks.append(pv[first + 4 + j, i, s - 4, :, n0:n1])
         return jnp.concatenate(blocks, axis=0)
 
-    def run(tok, cot):
-        for pieces, wanted in ((tok, ((0, og), (1, ou))), (cot, ((2, od),))):
+    def run(q, tok, cot):
+        for first, wanted in ((tok, ((0, og), (1, ou))), (cot, ((2, od),))):
             for n0, n1 in ((0, 256), (256, 512), (512, 640)):
                 total = [None] * len(wanted)
-                for s in range(8):
-                    rhs = rows(pieces, s, n0, n1)
-                    for q, (j, _) in enumerate(wanted):
-                        term = nn(act[s, j], rhs)
-                        total[q] = term if total[q] is None else total[q] + term
-                for q, (_, out) in enumerate(wanted):
-                    out[:, n0:n1] = total[q].astype(BF)
-
-    @pl.when(core[0] == 0)
-    def _():
-        run(mine, other)
-
-    @pl.when(core[0] != 0)
-    def _():
-        run(other, mine)
+                for s in range(4 * q, 4 * q + 4):
+                    rhs = rows(first, s, n0, n1)
+                    for w, (j, _) in enumerate(wanted):
+                        term = nn(av[s, j], rhs)
+                        total[w] = term if total[w] is None else total[w] + term
+                for w, (j, out) in enumerate(wanted):
+                    if q == 0:
+                        acc[j, :, n0:n1] = total[w]
+                    else:
+                        out[:, n0:n1] = (acc[j, :, n0:n1] + total[w]).astype(BF)
+
+    for q in range(2):
+        for c in copies[q]:
+            c.wait()
+
+        @pl.when(core[0] == 0)
+        def _():
+            run(q, 0, 8)
+
+        @pl.when(core[0] != 0)
+        def _():
+            run(q, 8, 0)
 
 
 def grads(core, act, mine, other):
     whole = pl.BlockSpec(memory_space=pltpu.VMEM)
     return pl.pallas_call(
         grads_kernel,
-        in_specs=[pl.BlockSpec(memory_space=pltpu.SMEM)] + [whole] * 17,
+        in_specs=[pl.BlockSpec(memory_space=pltpu.SMEM)] + [pl.BlockSpec(memory_space=pl.ANY)] * 17,
         out_specs=[whole] * 3,
         out_shape=[jax.ShapeDtypeStruct((F, 640), BF)] * 3,
+        scratch_shapes=[
+            pltpu.VMEM((8, 3, F, G), BF),
+            pltpu.VMEM((16, 4, 4, 16, 640), BF),
+            pltpu.VMEM((3, F, 640), F32),
+            pltpu.SemaphoreType.DMA((18,)),
+        ],
         compiler_params=pltpu.CompilerParams(vmem_limit_bytes=VMEM_LIMIT),
         cost_estimate=pl.CostEstimate(
             flops=6 * G * F * D, bytes_accessed=8 * 10**6, transcendentals=0
         ),
         name="grads",
-    )(core, act, *mine, *other)
+    )(core, hbm(act), *[hbm(v) for v in (*mine, *other)])
 
 
 def swap_core(v):
@@ -284,9 +371,10 @@
 
     nat, act = acts(order, rows, wg, wu, wd)
     everyone = lax.all_gather(act[None], "dp", axis=0, tiled=True)
-    res_next, payload = partials(fb, fc, bb, bc, nat, side, wg, wu, wd, res[0, 0])
-    received = lax.all_to_all(payload.reshape(32, MSG, 128), T, 0, 0, tiled=True)
-    res_next, *mine = lax.optimization_barrier((res_next, *mine))
+    payload = pack_selected(fb, bb, nat, side, wg, wu, wd, res[0, 0])
+    payload, nat, *mine = lax.optimization_barrier((payload, nat, *mine))
+    received = lax.all_to_all(payload, T, 0, 0, tiled=True)
+    res_next = next_residual(fb, fc, nat, wd, res[0, 0])
     others = [swap_core(v) for v in mine]
     idx = received[:, 160, : 2 * KMAX].astype(jnp.int32)
     layer_output, input_gradient = unpack(idx, received.reshape(32 * MSG, 128))

time: 143 us -> 139 us (0.972)
  waiting for transfers between devices: 49.6 us -> 42 us
  Pallas kernels: 29 us -> 32.4 us
    all_to_all x1, waiting for transfers between devices: 17.1 us -> 9.52 us  [shards(): received = lax.all_to_all(payload, T, 0, 0, tiled=True)]
    pallas_call x1 -> x2, Pallas kernels: 11 us -> 16.4 us  [the longest x1 8.86 us: pack_selected(): pl.pallas_call(pack_kernel, in_specs=[smem] * 2 + [whole] * 2 + [anywhere...]
  transfers between devices with their start and end apart: 24 -> 24, of which waited for: 12 -> 12; matrix products, arithmetic and copies ran while one was open for 3% -> 3% of each run, Pallas kernels for 10% -> 14%
where the time goes in v3:
time: 139 us
  waiting for transfers between devices  42 us (30%)
  Pallas kernels  32.4 us (23%)
  starting transfers between devices  27.1 us (19%)
  blocking collectives  14.9 us (11%)
  between operations  14.3 us (10%)
  other arithmetic  5.09 us (4%)
  local copies, waits for them, and re-layouts  2.96 us (2%)
    ppermute x12, waiting for transfers between devices, shift(): return lax.ppermute(v, axis, [(i, (i + by) % size) for i in range(size)])  22.9 us
    ppermute x12, starting transfers between devices, shift(): return lax.ppermute(v, axis, [(i, (i + by) % size) for i in range(size)])  17.3 us
    all_to_all x1, blocking collectives, shards(): lax.all_to_all(chip.reshape(16, 8, 640).transpose(1, 0, 2), 'dp', 0, 0, t...  14.9 us
    all_to_all x1, waiting for transfers between devices, shards(): received = lax.all_to_all(payload, T, 0, 0, tiled=True)  9.52 us
    pallas_call x1, Pallas kernels, pack_selected(): pl.pallas_call(pack_kernel, in_specs=[smem] * 2 + [whole] * 2 + [anywhere...  8.86 us
    pallas_call x1, Pallas kernels, next_residual(): pl.pallas_call(residual_kernel, grid_spec=pltpu.PrefetchScalarGridSpec(nu...  7.58 us
    all_gather x1, waiting for transfers between devices, shards(): lax.all_gather(jnp.concatenate([tok, cot], axis=1), T, axis=0, tiled=True)  7.34 us
    pallas_call x1, Pallas kernels, acts(): pl.pallas_call(acts_kernel, grid=(steps,), in_specs=[pl.BlockSpec((8, G),...  7 us
  transfers between devices with their start and end apart: 24, of which 12 were waited for; matrix products, arithmetic and copies ran while one was open for 3% of the time, Pallas kernels for 14%

profile of v3, /device:TPU:1, one launch (start us, length us, event | category | flops | bytes accessed | tf_op | source)
XLA Modules:
  0.0 138.8 jit_solution(8875477796190291424)
XLA Ops:
  7.2 1.6 %pad_maximum_fusion.2 = bf16[8,10240]{1,0:T(8,128)(2,1)} fusion(bf16[8,5120]{1,0:T(8,128)(2,1)} %param.17, bf16[8,5120]{1,0:T(8,128)(2,1)} %param.10), kind=kLoop, calls=%fused_computation.4 | loop fusion | flops 327680 | bytes 327680 | tf_op jit(solution)/shard_map/concatenate | solution.py:345
  8.9 0.9 broadcast_select_fusion.2
  9.8 3.3 %collective-permute-start = (bf16[8,5120]{1,0:T(8,128)(2,1)S(1)}, bf16[8,5120]{1,0:T(8,128)(2,1)S(1)}, u32[]{:S(2)}, u32[]{:S(2)}) collective-permute-start(bf16[8,5120]{1,0:T(8,128)(2,1)S(1)} %broadcast_select_fusion.2), channel_id=1, source_target_pairs={{0,1},{1,0},{2,3},{3,2},{4,5},{5,4},{6,7},{7,6},{8,9},{9,8},{10,11... | collective-permute-start | bytes 245768 | tf_op jit(solution)/shard_map/ppermute | solution.py:332
  13.1 0.9 collective-permute-done
  14.1 0.9 broadcast_select_fusion.1
  15.0 14.9 %all_to_all.10 = bf16[8,16,640]{2,1,0:T(8,128)(2,1)S(1)} all-to-all(bf16[8,16,640]{2,1,0:T(8,128)(2,1)S(1)} %bitcast.39), channel_id=1, replica_groups=mesh['dp'=8,'x'=4,'y'=4,'core'=2] {'dp'}, dimensions={0} | all-to-all | bytes 327680 | tf_op jit(solution)/shard_map/all_to_all | solution.py:349
  29.9 2.8 %collective-permute-start.6 = (bf16[4,16,640]{2,1,0:T(8,128)(2,1)S(1)}, bf16[4,16,640]{2,1,0:T(8,128)(2,1)S(1)}, u32[]{:S(2)}, u32[]{:S(2)}) collective-permute-start(bf16[4,16,640]{2,1,0:T(8,128)(2,1)S(1)} %get-tuple-element.76), channel_id=1, source_target_pairs={{0,6},{2,0},{4,2},{6,4},{1,7},{3,1},{5,3},{7,5},{8,14},{10,8},{12,... | collective-permute-start | bytes 245768 | tf_op jit(solution)/shard_map/ppermute | solution.py:336
  32.7 1.6 %collective-permute-start.2 = (bf16[4,16,640]{2,1,0:T(8,128)(2,1)S(1)}, bf16[4,16,640]{2,1,0:T(8,128)(2,1)S(1)}, u32[]{:S(2)}, u32[]{:S(2)}) collective-permute-start(bf16[4,16,640]{2,1,0:T(8,128)(2,1)S(1)} %get-tuple-element.76), channel_id=1, source_target_pairs={{0,4},{2,6},{4,0},{6,2},{1,5},{3,7},{5,1},{7,3},{8,12},{10,14},{12... | collective-permute-start | bytes 245768 | tf_op jit(solution)/shard_map/ppermute | solution.py:336
  34.4 1.2 collective-permute-start.3
  35.6 2.5 %collective-permute-start.1 = (bf16[4,16,640]{2,1,0:T(8,128)(2,1)S(1)}, bf16[4,16,640]{2,1,0:T(8,128)(2,1)S(1)}, u32[]{:S(2)}, u32[]{:S(2)}) collective-permute-start(bf16[4,16,640]{2,1,0:T(8,128)(2,1)S(1)} %get-tuple-element.77), channel_id=1, source_target_pairs={{0,16},{8,24},{16,0},{24,8},{1,17},{9,25},{17,1},{25,9},{2,18},{10... | collective-permute-start | bytes 245768 | tf_op jit(solution)/shard_map/ppermute | solution.py:336
  38.0 1.2 collective-permute-start.5
  39.2 1.9 %collective-permute-done.1 = bf16[4,16,640]{2,1,0:T(8,128)(2,1)S(1)} collective-permute-done((bf16[4,16,640]{2,1,0:T(8,128)(2,1)S(1)}, bf16[4,16,640]{2,1,0:T(8,128)(2,1)S(1)}, u32[]{:S(2)}, u32[]{:S(2)}) %collective-permute-start.1) | collective-permute-done | bytes 81952 | tf_op jit(solution)/shard_map/ppermute | solution.py:336
  41.8 1.2 collective-permute-start.9
  43.0 2.0 %collective-permute-start.8 = (bf16[4,4,16,640]{3,2,1,0:T(8,128)(2,1)S(1)}, bf16[4,4,16,640]{3,2,1,0:T(8,128)(2,1)S(1)}, u32[]{:S(2)}, u32[]{:S(2)}) collective-permute-start(bf16[4,4,16,640]{3,2,1,0:T(8,128)(2,1)S(1)} %get-tuple-element.63.refs_0_), channel_id=1, source_target_pairs={{0,4},{2,6},{4,0},{6,2},{1,5},{3,7},{5,1},{7,3},{8,12},{10,14},{12... | collective-permute-start | bytes 983048 | tf_op jit(solution)/shard_map/ppermute | solution.py:336
  44.9 2.4 %collective-permute-start.12 = (bf16[4,4,16,640]{3,2,1,0:T(8,128)(2,1)S(1)}, bf16[4,4,16,640]{3,2,1,0:T(8,128)(2,1)S(1)}, u32[]{:S(2)}, u32[]{:S(2)}) collective-permute-start(bf16[4,4,16,640]{3,2,1,0:T(8,128)(2,1)S(1)} %get-tuple-element.67.refs_4_), channel_id=1, source_target_pairs={{0,24},{8,0},{16,8},{24,16},{1,25},{9,1},{17,9},{25,17},{2,26},{10... | collective-permute-start | bytes 983048 | tf_op jit(solution)/shard_map/ppermute | solution.py:336
  47.8 2.3 %collective-permute-start.10 = (bf16[4,4,16,640]{3,2,1,0:T(8,128)(2,1)S(1)}, bf16[4,4,16,640]{3,2,1,0:T(8,128)(2,1)S(1)}, u32[]{:S(2)}, u32[]{:S(2)}) collective-permute-start(bf16[4,4,16,640]{3,2,1,0:T(8,128)(2,1)S(1)} %get-tuple-element.67.refs_4_), channel_id=1, source_target_pairs={{0,8},{8,16},{16,24},{24,0},{1,9},{9,17},{17,25},{25,1},{2,10},{10... | collective-permute-start | bytes 983048 | tf_op jit(solution)/shard_map/ppermute | solution.py:336
  50.5 9.3 %collective-permute-done.7.refs_1_ = bf16[4,4,16,640]{3,2,1,0:T(8,128)(2,1)S(1)} collective-permute-done((bf16[4,4,16,640]{3,2,1,0:T(8,128)(2,1)S(1)}, bf16[4,4,16,640]{3,2,1,0:T(8,128)(2,1)S(1)}, u32[]{:S(2)}, u32[]{:S(2)}) %collective-permute-start.7) | collective-permute-done | bytes 327712 | tf_op jit(solution)/shard_map/ppermute | solution.py:336
  59.8 10.5 %collective-permute-done.10.refs_5_ = bf16[4,4,16,640]{3,2,1,0:T(8,128)(2,1)S(1)} collective-permute-done((bf16[4,4,16,640]{3,2,1,0:T(8,128)(2,1)S(1)}, bf16[4,4,16,640]{3,2,1,0:T(8,128)(2,1)S(1)}, u32[]{:S(2)}, u32[]{:S(2)}) %collective-permute-start.10) | collective-permute-done | bytes 327712 | tf_op jit(solution)/shard_map/ppermute | solution.py:336
  70.3 7.3 %all-gather.4.cloned.1.call-done.tok.cot = bf16[256,10240]{1,0:T(8,128)(2,1)} async-done(((bf16[8,10240]{1,0:T(8,128)(2,1)}), bf16[256,10240]{1,0:T(8,128)(2,1)}) %all-gather.4.cloned.1.call-update) | async-done | bytes 5242896 | tf_op jit(solution)/shard_map/all_gather | solution.py:345
  77.7 0.6 broadcast_in_dim.24.order
  78.3 7.0 %acts.1 = (bf16[3,256,216]{2,1,0:T(8,128)(2,1)}, bf16[3,216,256]{2,1,0:T(8,128)(2,1)}) custom-call(s32[8,256]{1,0:T(8,128)} %broadcast_in_dim.24.order, bf16[256,10240]{1,0:T(8,128)(2,1)} %all-gather.4.cloned.1.call-done.tok.cot, bf16[256,10240]{1,0:T(8,128)(2,1)} %all-gather.4.cloned.1.call-done.tok.cot, bf16[216,5120]{1,0:T(8,128)(2,1)} %wg.3, ...), custom_call_target="tpu_custom_call" | custom-call | flops 1698693120 | bytes 11878400 | tf_op jit(solution)/shard_map/acts/pallas_call | solution.py:63
  85.7 0.7 pad_convert_fusion.side
  86.4 8.9 %pack_selected.1 = bf16[32,176,128]{2,1,0:T(8,128)(2,1)} custom-call(s32[32,10]{1,0:T(8,128)} %bitcast.40, s32[32,10]{1,0:T(8,128)} %bitcast.42, bf16[3,256,216]{2,1,0:T(8,128)(2,1)} %get-tuple-element.60.act, f32[32,16,128]{2,1,0:T(8,128)} %pad_convert_fusion.side, bf16[216,5120]{1,0:T(8,128)(2,1)} %wg.3, bf16[216,5120]{1,0:T(8,128)(2,1)} %wu.3, ...), custom_call_target="tpu_custom_call" | custom-call | flops 1698693120 | bytes 9256960 | tf_op jit(solution)/shard_map/pack_selected/pallas_call | solution.py:156
  95.3 4.3 %all-to-all-start.1 = ((bf16[32,176,128]{2,1,0:T(8,128)(2,1)}), bf16[32,176,128]{2,1,0:T(8,128)(2,1)S(1)}, u32[]{:S(2)}, u32[]{:S(2)}) async-start(bf16[32,176,128]{2,1,0:T(8,128)(2,1)} %pack_selected.1), calls=%async_computation.1 | async-start | bytes 2883584 | tf_op jit(solution)/shard_map/all_to_all | solution.py:376
  102.1 0.7 collective-permute-done.15.refs_10_
  102.8 0.7 copy-done.11
  103.7 7.6 %next_residual.1 = bf16[256,5120]{1,0:T(8,128)(2,1)} custom-call(s32[32,10]{1,0:T(8,128)} %bitcast.41, s32[32]{0:T(128)} %bitcast.49, bf16[3,256,216]{2,1,0:T(8,128)(2,1)} %get-tuple-element.60.act, bf16[216,5120]{1,0:T(8,128)(2,1)} %wd.5, bf16[256,5120]{1,0:T(8,128)(2,1)} %bitcast.34), custom_call_target="tpu_custom_call" | custom-call | flops 566231040 | bytes 7454720 | tf_op jit(solution)/shard_map/next_residual/pallas_call | solution.py:201
  111.3 9.5 %all-to-all-done.1 = bf16[32,176,128]{2,1,0:T(8,128)(2,1)S(1)} async-done(((bf16[32,176,128]{2,1,0:T(8,128)(2,1)}), bf16[32,176,128]{2,1,0:T(8,128)(2,1)S(1)}, u32[]{:S(2)}, u32[]{:S(2)}) %all-to-all-start.1) | async-done | bytes 1441824 | tf_op jit(solution)/shard_map/all_to_all | solution.py:376
  120.9 0.7 fusion.2.idx
  122.0 3.4 %unpack.1 = (bf16[8,5120]{1,0:T(8,128)(2,1)}, bf16[8,5120]{1,0:T(8,128)(2,1)}) custom-call(s32[32,20]{1,0:T(8,128)} %fusion.2.idx, bf16[5632,128]{1,0:T(8,128)(2,1)} %bitcast.35), custom_call_target="tpu_custom_call" | custom-call | flops 1000000 | bytes 2000000 | tf_op jit(solution)/shard_map/unpack/pallas_call | solution.py:245
  125.4 0.7 copy-done.12
  126.3 5.6 %grads.1 = (bf16[216,640]{1,0:T(8,128)(2,1)}, bf16[216,640]{1,0:T(8,128)(2,1)}, bf16[216,640]{1,0:T(8,128)(2,1)}) custom-call(s32[1]{0:T(128)} %bitcast.17.core, bf16[8,3,216,256]{3,2,1,0:T(8,128)(2,1)} %bitcast.36, bf16[4,4,16,640]{3,2,1,0:T(8,128)(2,1)} %copy-done.1, bf16[4,4,16,640]{3,2,1,0:T(8,128)(2,1)} %copy-done.5, bf16[4,4,16,640]{3,2,1,0:T(8,128)(2,1)} %copy-done.4, ...), custom_call_target="tpu_custom_call" | custom-call | flops 1698693120 | bytes 8000000 | tf_op jit(solution)/shard_map/grads/pallas_call | solution.py:312
  (83 shorter events, 5.4 us)
Async XLA Ops:
  7.2 70.5 %all-gather.4.cloned.1.call-start = ((), (), s32[]{:S(2)}) async-start(), calls=%async_computation.2 | async-start | bytes 5406720 | tf_op jit(solution)/shard_map/all_gather | solution.py:345
  8.8 116.6 %all-gather.6.cloned.1.call-start = ((), (), s32[]{:S(2)}) async-start(), calls=%async_computation.3 | async-start | bytes 2985984 | tf_op jit(solution)/shard_map/all_gather | solution.py:373
  9.8 4.2 %collective-permute-start = (bf16[8,5120]{1,0:T(8,128)(2,1)S(1)}, bf16[8,5120]{1,0:T(8,128)(2,1)S(1)}, u32[]{:S(2)}, u32[]{:S(2)}) collective-permute-start(bf16[8,5120]{1,0:T(8,128)(2,1)S(1)} %broadcast_select_fusion.2), channel_id=1, source_target_pairs={{0,1},{1,0},{2,3},{3,2},{4,5},{5,4},{6,7},{7,6},{8,9},{9,8},{10,11... | collective-permute-start | bytes 245768 | tf_op jit(solution)/shard_map/ppermute | solution.py:332
  29.9 8.1 %collective-permute-start.6 = (bf16[4,16,640]{2,1,0:T(8,128)(2,1)S(1)}, bf16[4,16,640]{2,1,0:T(8,128)(2,1)S(1)}, u32[]{:S(2)}, u32[]{:S(2)}) collective-permute-start(bf16[4,16,640]{2,1,0:T(8,128)(2,1)S(1)} %get-tuple-element.76), channel_id=1, source_target_pairs={{0,6},{2,0},{4,2},{6,4},{1,7},{3,1},{5,3},{7,5},{8,14},{10,8},{12,... | collective-permute-start | bytes 245768 | tf_op jit(solution)/shard_map/ppermute | solution.py:336
  32.7 6.5 %collective-permute-start.4 = (bf16[4,16,640]{2,1,0:T(8,128)(2,1)S(1)}, bf16[4,16,640]{2,1,0:T(8,128)(2,1)S(1)}, u32[]{:S(2)}, u32[]{:S(2)}) collective-permute-start(bf16[4,16,640]{2,1,0:T(8,128)(2,1)S(1)} %get-tuple-element.76), channel_id=1, source_target_pairs={{0,2},{2,4},{4,6},{6,0},{1,3},{3,5},{5,7},{7,1},{8,10},{10,12},{12... | collective-permute-start | bytes 245768 | tf_op jit(solution)/shard_map/ppermute | solution.py:336
  32.7 6.5 %collective-permute-start.2 = (bf16[4,16,640]{2,1,0:T(8,128)(2,1)S(1)}, bf16[4,16,640]{2,1,0:T(8,128)(2,1)S(1)}, u32[]{:S(2)}, u32[]{:S(2)}) collective-permute-start(bf16[4,16,640]{2,1,0:T(8,128)(2,1)S(1)} %get-tuple-element.76), channel_id=1, source_target_pairs={{0,4},{2,6},{4,0},{6,2},{1,5},{3,7},{5,1},{7,3},{8,12},{10,14},{12... | collective-permute-start | bytes 245768 | tf_op jit(solution)/shard_map/ppermute | solution.py:336
  34.4 4.8 %collective-permute-start.3 = (bf16[4,16,640]{2,1,0:T(8,128)(2,1)S(1)}, bf16[4,16,640]{2,1,0:T(8,128)(2,1)S(1)}, u32[]{:S(2)}, u32[]{:S(2)}) collective-permute-start(bf16[4,16,640]{2,1,0:T(8,128)(2,1)S(1)} %get-tuple-element.77), channel_id=1, source_target_pairs={{0,8},{8,16},{16,24},{24,0},{1,9},{9,17},{17,25},{25,1},{2,10},{10... | collective-permute-start | bytes 245768 | tf_op jit(solution)/shard_map/ppermute | solution.py:336
  35.6 5.5 %collective-permute-start.1 = (bf16[4,16,640]{2,1,0:T(8,128)(2,1)S(1)}, bf16[4,16,640]{2,1,0:T(8,128)(2,1)S(1)}, u32[]{:S(2)}, u32[]{:S(2)}) collective-permute-start(bf16[4,16,640]{2,1,0:T(8,128)(2,1)S(1)} %get-tuple-element.77), channel_id=1, source_target_pairs={{0,16},{8,24},{16,0},{24,8},{1,17},{9,25},{17,1},{25,9},{2,18},{10... | collective-permute-start | bytes 245768 | tf_op jit(solution)/shard_map/ppermute | solution.py:336
  38.0 3.6 %collective-permute-start.5 = (bf16[4,16,640]{2,1,0:T(8,128)(2,1)S(1)}, bf16[4,16,640]{2,1,0:T(8,128)(2,1)S(1)}, u32[]{:S(2)}, u32[]{:S(2)}) collective-permute-start(bf16[4,16,640]{2,1,0:T(8,128)(2,1)S(1)} %get-tuple-element.77), channel_id=1, source_target_pairs={{0,24},{8,0},{16,8},{24,16},{1,25},{9,1},{17,9},{25,17},{2,26},{10... | collective-permute-start | bytes 245768 | tf_op jit(solution)/shard_map/ppermute | solution.py:336
  41.7 57.9 %copy-start.1 = (bf16[4,4,16,640]{3,2,1,0:T(8,128)(2,1)}, bf16[4,4,16,640]{3,2,1,0:T(8,128)(2,1)S(1)}, u32[]{:S(2)}) copy-start(bf16[4,4,16,640]{3,2,1,0:T(8,128)(2,1)S(1)} %get-tuple-element.63.refs_0_) | copy-start | bytes 983044
  41.7 59.0 %copy-start.2 = (bf16[4,4,16,640]{3,2,1,0:T(8,128)(2,1)}, bf16[4,4,16,640]{3,2,1,0:T(8,128)(2,1)S(1)}, u32[]{:S(2)}) copy-start(bf16[4,4,16,640]{3,2,1,0:T(8,128)(2,1)S(1)} %get-tuple-element.67.refs_4_) | copy-start | bytes 983044
  41.8 6.0 %collective-permute-start.9 = (bf16[4,4,16,640]{3,2,1,0:T(8,128)(2,1)S(1)}, bf16[4,4,16,640]{3,2,1,0:T(8,128)(2,1)S(1)}, u32[]{:S(2)}, u32[]{:S(2)}) collective-permute-start(bf16[4,4,16,640]{3,2,1,0:T(8,128)(2,1)S(1)} %get-tuple-element.63.refs_0_), channel_id=1, source_target_pairs={{0,6},{2,0},{4,2},{6,4},{1,7},{3,1},{5,3},{7,5},{8,14},{10,8},{12,... | collective-permute-start | bytes 983048 | tf_op jit(solution)/shard_map/ppermute | solution.py:336
  43.0 7.5 %collective-permute-start.8 = (bf16[4,4,16,640]{3,2,1,0:T(8,128)(2,1)S(1)}, bf16[4,4,16,640]{3,2,1,0:T(8,128)(2,1)S(1)}, u32[]{:S(2)}, u32[]{:S(2)}) collective-permute-start(bf16[4,4,16,640]{3,2,1,0:T(8,128)(2,1)S(1)} %get-tuple-element.63.refs_0_), channel_id=1, source_target_pairs={{0,4},{2,6},{4,0},{6,2},{1,5},{3,7},{5,1},{7,3},{8,12},{10,14},{12... | collective-permute-start | bytes 983048 | tf_op jit(solution)/shard_map/ppermute | solution.py:336
  44.9 14.9 %collective-permute-start.7 = (bf16[4,4,16,640]{3,2,1,0:T(8,128)(2,1)S(1)}, bf16[4,4,16,640]{3,2,1,0:T(8,128)(2,1)S(1)}, u32[]{:S(2)}, u32[]{:S(2)}) collective-permute-start(bf16[4,4,16,640]{3,2,1,0:T(8,128)(2,1)S(1)} %get-tuple-element.63.refs_0_), channel_id=1, source_target_pairs={{0,2},{2,4},{4,6},{6,0},{1,3},{3,5},{5,7},{7,1},{8,10},{10,12},{12... | collective-permute-start | bytes 983048 | tf_op jit(solution)/shard_map/ppermute | solution.py:336
  44.9 14.9 %collective-permute-start.12 = (bf16[4,4,16,640]{3,2,1,0:T(8,128)(2,1)S(1)}, bf16[4,4,16,640]{3,2,1,0:T(8,128)(2,1)S(1)}, u32[]{:S(2)}, u32[]{:S(2)}) collective-permute-start(bf16[4,4,16,640]{3,2,1,0:T(8,128)(2,1)S(1)} %get-tuple-element.67.refs_4_), channel_id=1, source_target_pairs={{0,24},{8,0},{16,8},{24,16},{1,25},{9,1},{17,9},{25,17},{2,26},{10... | collective-permute-start | bytes 983048 | tf_op jit(solution)/shard_map/ppermute | solution.py:336
  47.3 12.5 %collective-permute-start.11 = (bf16[4,4,16,640]{3,2,1,0:T(8,128)(2,1)S(1)}, bf16[4,4,16,640]{3,2,1,0:T(8,128)(2,1)S(1)}, u32[]{:S(2)}, u32[]{:S(2)}) collective-permute-start(bf16[4,4,16,640]{3,2,1,0:T(8,128)(2,1)S(1)} %get-tuple-element.67.refs_4_), channel_id=1, source_target_pairs={{0,16},{8,24},{16,0},{24,8},{1,17},{9,25},{17,1},{25,9},{2,18},{10... | collective-permute-start | bytes 983048 | tf_op jit(solution)/shard_map/ppermute | solution.py:336
  47.8 52.7 %copy-start.3 = (bf16[4,4,16,640]{3,2,1,0:T(8,128)(2,1)}, bf16[4,4,16,640]{3,2,1,0:T(8,128)(2,1)S(1)}, u32[]{:S(2)}) copy-start(bf16[4,4,16,640]{3,2,1,0:T(8,128)(2,1)S(1)} %collective-permute-done.9.refs_3_) | copy-start | bytes 983044
  47.8 22.6 %collective-permute-start.10 = (bf16[4,4,16,640]{3,2,1,0:T(8,128)(2,1)S(1)}, bf16[4,4,16,640]{3,2,1,0:T(8,128)(2,1)S(1)}, u32[]{:S(2)}, u32[]{:S(2)}) collective-permute-start(bf16[4,4,16,640]{3,2,1,0:T(8,128)(2,1)S(1)} %get-tuple-element.67.refs_4_), channel_id=1, source_target_pairs={{0,8},{8,16},{16,24},{24,0},{1,9},{9,17},{17,25},{25,1},{2,10},{10... | collective-permute-start | bytes 983048 | tf_op jit(solution)/shard_map/ppermute | solution.py:336
  50.5 49.7 %copy-start.4 = (bf16[4,4,16,640]{3,2,1,0:T(8,128)(2,1)}, bf16[4,4,16,640]{3,2,1,0:T(8,128)(2,1)S(1)}, u32[]{:S(2)}) copy-start(bf16[4,4,16,640]{3,2,1,0:T(8,128)(2,1)S(1)} %collective-permute-done.8.refs_2_) | copy-start | bytes 983044
  59.8 40.1 %copy-start.5 = (bf16[4,4,16,640]{3,2,1,0:T(8,128)(2,1)}, bf16[4,4,16,640]{3,2,1,0:T(8,128)(2,1)S(1)}, u32[]{:S(2)}) copy-start(bf16[4,4,16,640]{3,2,1,0:T(8,128)(2,1)S(1)} %collective-permute-done.7.refs_1_) | copy-start | bytes 983044
  59.8 42.9 %copy-start.6 = (bf16[4,4,16,640]{3,2,1,0:T(8,128)(2,1)}, bf16[4,4,16,640]{3,2,1,0:T(8,128)(2,1)S(1)}, u32[]{:S(2)}) copy-start(bf16[4,4,16,640]{3,2,1,0:T(8,128)(2,1)S(1)} %collective-permute-done.12.refs_7_) | copy-start | bytes 983044
  59.8 25.5 %copy-start.7 = (bf16[4,4,16,640]{3,2,1,0:T(8,128)(2,1)}, bf16[4,4,16,640]{3,2,1,0:T(8,128)(2,1)S(1)}, u32[]{:S(2)}) copy-start(bf16[4,4,16,640]{3,2,1,0:T(8,128)(2,1)S(1)} %collective-permute-done.11.refs_6_) | copy-start | bytes 983044
  70.3 15.0 %copy-start.8 = (bf16[4,4,16,640]{3,2,1,0:T(8,128)(2,1)}, bf16[4,4,16,640]{3,2,1,0:T(8,128)(2,1)S(1)}, u32[]{:S(2)}) copy-start(bf16[4,4,16,640]{3,2,1,0:T(8,128)(2,1)S(1)} %collective-permute-done.10.refs_5_) | copy-start | bytes 983044
  95.3 25.5 %all-to-all-start.1 = ((bf16[32,176,128]{2,1,0:T(8,128)(2,1)}), bf16[32,176,128]{2,1,0:T(8,128)(2,1)S(1)}, u32[]{:S(2)}, u32[]{:S(2)}) async-start(bf16[32,176,128]{2,1,0:T(8,128)(2,1)} %pack_selected.1), calls=%async_computation.1 | async-start | bytes 2883584 | tf_op jit(solution)/shard_map/all_to_all | solution.py:376
  99.6 1.7 %collective-permute-start.13 = (bf16[4,4,16,640]{3,2,1,0:T(8,128)(2,1)S(1)}, bf16[4,4,16,640]{3,2,1,0:T(8,128)(2,1)S(1)}, u32[]{:S(2)}, u32[]{:S(2)}) collective-permute-start(bf16[4,4,16,640]{3,2,1,0:T(8,128)(2,1)S(1)} %get-tuple-element.63.refs_0_), channel_id=1, source_target_pairs={{0,1},{1,0},{2,3},{3,2},{4,5},{5,4},{6,7},{7,6},{8,9},{9,8},{10,11... | collective-permute-start | bytes 983048 | tf_op jit(solution)/shard_map/ppermute | solution.py:332
  100.0 1.9 %collective-permute-start.14 = (bf16[4,4,16,640]{3,2,1,0:T(8,128)(2,1)S(1)}, bf16[4,4,16,640]{3,2,1,0:T(8,128)(2,1)S(1)}, u32[]{:S(2)}, u32[]{:S(2)}) collective-permute-start(bf16[4,4,16,640]{3,2,1,0:T(8,128)(2,1)S(1)} %collective-permute-done.7.refs_1_), channel_id=1, source_target_pairs={{0,1},{1,0},{2,3},{3,2},{4,5},{5,4},{6,7},{7,6},{8,9},{9,8},{10,11... | collective-permute-start | bytes 983048 | tf_op jit(solution)/shard_map/ppermute | solution.py:332
  100.2 2.5 %collective-permute-start.15 = (bf16[4,4,16,640]{3,2,1,0:T(8,128)(2,1)S(1)}, bf16[4,4,16,640]{3,2,1,0:T(8,128)(2,1)S(1)}, u32[]{:S(2)}, u32[]{:S(2)}) collective-permute-start(bf16[4,4,16,640]{3,2,1,0:T(8,128)(2,1)S(1)} %collective-permute-done.8.refs_2_), channel_id=1, source_target_pairs={{0,1},{1,0},{2,3},{3,2},{4,5},{5,4},{6,7},{7,6},{8,9},{9,8},{10,11... | collective-permute-start | bytes 983048 | tf_op jit(solution)/shard_map/ppermute | solution.py:332
  100.5 24.9 %collective-permute-start.16 = (bf16[4,4,16,640]{3,2,1,0:T(8,128)(2,1)S(1)}, bf16[4,4,16,640]{3,2,1,0:T(8,128)(2,1)}, u32[]{:S(2)}, u32[]{:S(2)}) collective-permute-start(bf16[4,4,16,640]{3,2,1,0:T(8,128)(2,1)S(1)} %collective-permute-done.9.refs_3_), channel_id=1, source_target_pairs={{0,1},{1,0},{2,3},{3,2},{4,5},{5,4},{6,7},{7,6},{8,9},{9,8},{10,11... | collective-permute-start | bytes 983048 | tf_op jit(solution)/shard_map/ppermute | solution.py:332
  100.8 24.6 %collective-permute-start.17 = (bf16[4,4,16,640]{3,2,1,0:T(8,128)(2,1)S(1)}, bf16[4,4,16,640]{3,2,1,0:T(8,128)(2,1)}, u32[]{:S(2)}, u32[]{:S(2)}) collective-permute-start(bf16[4,4,16,640]{3,2,1,0:T(8,128)(2,1)S(1)} %get-tuple-element.67.refs_4_), channel_id=1, source_target_pairs={{0,1},{1,0},{2,3},{3,2},{4,5},{5,4},{6,7},{7,6},{8,9},{9,8},{10,11... | collective-permute-start | bytes 983048 | tf_op jit(solution)/shard_map/ppermute | solution.py:332
  101.3 24.0 %collective-permute-start.18 = (bf16[4,4,16,640]{3,2,1,0:T(8,128)(2,1)}, bf16[4,4,16,640]{3,2,1,0:T(8,128)(2,1)S(1)}, u32[]{:S(2)}, u32[]{:S(2)}) collective-permute-start(bf16[4,4,16,640]{3,2,1,0:T(8,128)(2,1)} %copy-done.8), channel_id=1, source_target_pairs={{0,1},{1,0},{2,3},{3,2},{4,5},{5,4},{6,7},{7,6},{8,9},{9,8},{10,11... | collective-permute-start | bytes 983048 | tf_op jit(solution)/shard_map/ppermute | solution.py:332
  101.8 23.6 %collective-permute-start.19 = (bf16[4,4,16,640]{3,2,1,0:T(8,128)(2,1)}, bf16[4,4,16,640]{3,2,1,0:T(8,128)(2,1)S(1)}, u32[]{:S(2)}, u32[]{:S(2)}) collective-permute-start(bf16[4,4,16,640]{3,2,1,0:T(8,128)(2,1)} %copy-done.7), channel_id=1, source_target_pairs={{0,1},{1,0},{2,3},{3,2},{4,5},{5,4},{6,7},{7,6},{8,9},{9,8},{10,11... | collective-permute-start | bytes 983048 | tf_op jit(solution)/shard_map/ppermute | solution.py:332
  103.5 21.9 %collective-permute-start.20 = (bf16[4,4,16,640]{3,2,1,0:T(8,128)(2,1)S(1)}, bf16[4,4,16,640]{3,2,1,0:T(8,128)(2,1)S(1)}, u32[]{:S(2)}, u32[]{:S(2)}) collective-permute-start(bf16[4,4,16,640]{3,2,1,0:T(8,128)(2,1)S(1)} %collective-permute-done.12.refs_7_), channel_id=1, source_target_pairs={{0,1},{1,0},{2,3},{3,2},{4,5},{5,4},{6,7},{7,6},{8,9},{9,8},{10,11... | collective-permute-start | bytes 983048 | tf_op jit(solution)/shard_map/ppermute | solution.py:332
  (13 other events, 37.3 us)
Sparse Core Ops, SparseCore 0:
  11.1 66.5 all-gather.3
  85.4 36.8 all-gather.5

commit v4 on v3

--- a/solution.py
+++ b/solution.py
@@ -29,7 +29,7 @@
     return lax.dot_general(a, b, (((1,), (0,)), ((), ())), preferred_element_type=F32)
 
 
-def acts_kernel(order, tok, cot, wg, wu, wd, nat, out, ga, ua, hb):
+def acts_kernel(where, tok, cot, wg, wu, wd, nat, out, ga, ua, hb):
     k = pl.program_id(0)
 
     @pl.when(k == 0)
@@ -48,7 +48,11 @@
         g, u, b = ga[...], ua[...], hb[...]
         s = jax.nn.sigmoid(g)
         silu = g * s
-        place = (lax.broadcasted_iota(jnp.int32, (G, G), 0) == order[0:1, :]).astype(BF)
+        at = lax.broadcasted_iota(jnp.int32, (G, G), 1)
+        gx = (where[0] - ((at >> 4) & 3)) & 3
+        gy = (where[1] - (at >> 6)) & 3
+        order = ((gx * 4 + gy) << 4) + (at & 15)
+        place = (lax.broadcasted_iota(jnp.int32, (G, G), 0) == order).astype(BF)
         values = (b * u * (s * (1.0 + g * (1.0 - s))), b * silu, silu * u)
         for j in range(3):
             v = values[j].astype(BF)
@@ -56,7 +60,7 @@
             out[j] = tn(v, place).astype(BF)
 
 
-def acts(order, rows, wg, wu, wd):
+def acts(where, rows, wg, wu, wd):
     kb = 2560
     steps = D // kb
     wspec = pl.BlockSpec((F, kb), lambda k: (0, k))
@@ -64,7 +68,7 @@
         acts_kernel,
         grid=(steps,),
         in_specs=[
-            pl.BlockSpec((8, G), lambda k: (0, 0)),
+            pl.BlockSpec(memory_space=pltpu.SMEM),
             pl.BlockSpec((G, kb), lambda k: (0, k)),
             pl.BlockSpec((G, kb), lambda k: (0, k + steps)),
             wspec,
@@ -85,7 +89,7 @@
             flops=6 * G * F * D, bytes_accessed=2 * (2 * G * D + 3 * F * D), transcendentals=G * F
         ),
         name="acts",
-    )(order, rows, rows, wg, wu, wd)
+    )(where, rows, rows, wg, wu, wd)
 
 
 def hbm(v):
@@ -338,38 +342,35 @@
 
 def shards(tok, wg, wu, wd, res, fb, fc, cot, bb, bc):
     core = lax.axis_index("core")
-    first = core == 0
     which = core.astype(jnp.int32).reshape(1)
     fb, fc, bb, bc = fb[0, 0], fc[0, 0], bb[0, 0], bc[0, 0]
 
     rows = lax.all_gather(jnp.concatenate([tok, cot], axis=1), T, axis=0, tiled=True)
 
-    other = swap_core(jnp.where(first, cot, tok))
-    chip = jnp.concatenate([jnp.where(first, tok, other), jnp.where(first, other, cot)], axis=0)
-    cols = lax.all_to_all(chip.reshape(16, 8, 640).transpose(1, 0, 2), "dp", 0, 0, tiled=True)
+    blocks = [v.reshape(8, 8, 640).transpose(1, 0, 2) for v in (tok, cot)]
+    blocks = jnp.stack(blocks, axis=1).reshape(16, 8, 640)
+    cols = lax.all_to_all(blocks, ("dp", "core"), 0, 0, tiled=True).reshape(8, 16, 640)
     halves = [cols[:4], cols[4:]]
-    steps = [shift(halves[h], a, 4, s) for s in (2, 1, 3) for h, a in ((0, "x"), (1, "y"))]
+    steps = [shift(halves[h], a, 4, s) for s in (1, 3) for h, a in ((0, "x"), (1, "y"))]
+    steps = [shift(steps[0], "x", 4, 1), shift(steps[1], "y", 4, 1), *steps]
     steps = lax.optimization_barrier(tuple(steps))
     four = [jnp.stack([halves[h], steps[2 + h], steps[h], steps[4 + h]]) for h in range(2)]
-    four = lax.optimization_barrier(tuple(four))
-    mine = [four[0], None, None, None, four[1], None, None, None]
-    for s in (2, 1, 3):
-        mine[s] = shift(four[0], "y", 4, s)
-        mine[4 + s] = shift(four[1], "x", 4, s)
-    rows, *mine = lax.optimization_barrier((rows, *mine))
-
-    x, y = lax.axis_index("x"), lax.axis_index("y")
-    a = jnp.arange(G)
-    order = (((x - (a // 16) % 4) % 4) * 4 + (y - a // 64) % 4) * 16 + a % 16
-    order = jnp.broadcast_to(order.astype(jnp.int32)[None], (8, G))
     slots = jnp.arange(KMAX)[None, :]
     lists = jnp.concatenate(
         [jnp.where(slots < fc[:, None], fb, 40), jnp.where(slots < bc[:, None], bb, 40)], axis=1
     )
     lists = jnp.broadcast_to(lists[:, None, :], (32, 16, 2 * KMAX))
     side = jnp.pad(lists, ((0, 0), (0, 0), (0, 128 - 2 * KMAX))).astype(F32)
-
-    nat, act = acts(order, rows, wg, wu, wd)
+    *four, side = lax.optimization_barrier((*four, side))
+    mine = [four[0], None, None, None, four[1], None, None, None]
+    for s in (1, 3):
+        mine[s] = shift(four[0], "y", 4, s)
+        mine[4 + s] = shift(four[1], "x", 4, s)
+    mine[2], mine[6] = shift(mine[3], "y", 4, -1), shift(mine[7], "x", 4, -1)
+    rows, *mine = lax.optimization_barrier((rows, *mine))
+
+    where = jnp.stack([lax.axis_index("x"), lax.axis_index("y")]).astype(jnp.int32)
+    nat, act = acts(where, rows, wg, wu, wd)
     everyone = lax.all_gather(act[None], "dp", axis=0, tiled=True)
     payload = pack_selected(fb, bb, nat, side, wg, wu, wd, res[0, 0])
     payload, nat, *mine = lax.optimization_barrier((payload, nat, *mine))

time: 139 us -> 134 us (0.964)
  blocking collectives: 14.9 us -> 0 us
  waiting for transfers between devices: 42 us -> 46.5 us
  starting transfers between devices: 27.1 us -> 30.2 us
    all_to_all x1 -> x0, blocking collectives: 14.9 us -> none  [shards(): lax.all_to_all(chip.reshape(16, 8, 640).transpose(1, 0, 2), 'dp', 0, 0, t...]
    all_to_all x0 -> x1, starting transfers between devices: none -> 10 us  [shards(): lax.all_to_all(blocks, ('dp', 'core'), 0, 0, tiled=True).reshape(8, 16, 640)]
    all_to_all x0 -> x1, waiting for transfers between devices: none -> 7.3 us  [shards(): lax.all_to_all(blocks, ('dp', 'core'), 0, 0, tiled=True).reshape(8, 16, 640)]
    ppermute x12, starting transfers between devices: 17.3 us -> 12.3 us  [shift(): return lax.ppermute(v, axis, [(i, (i + by) % size) for i in range(size)])]
    ppermute x9 -> x8, starting transfers between devices: 5.38 us -> 2.05 us  [swap_core(): return lax.ppermute(v, 'core', [(0, 1), (1, 0)])]
    select_n x2 -> x0, other arithmetic: 1.81 us -> none  [the longest x1 0.91 us: shards(): other = swap_core(jnp.where(first, cot, tok))]
    all_gather x1, waiting for transfers between devices: 7.34 us -> 5.71 us  [shards(): lax.all_gather(jnp.concatenate([tok, cot], axis=1), T, axis=0, tiled=True)]
    another operation x0 -> x2, other arithmetic: none -> 1.6 us  [the longest x1 0.95 us: shards(): blocks = jnp.stack(blocks, axis=1).reshape(16, 8, 640)]
  transfers between devices with their start and end apart: 24 -> 24, of which waited for: 12 -> 13; matrix products, arithmetic and copies ran while one was open for 3% -> 5% of each run, Pallas kernels for 14% -> 15%
where the time goes in v4:
time: 134 us; the launch traced here: 133 us
  waiting for transfers between devices  46.5 us (35%)
  Pallas kernels  32.3 us (24%)
  starting transfers between devices  30.2 us (23%)
  between operations  14.2 us (11%)
  other arithmetic  5.53 us (4%)
  local copies, waits for them, and re-layouts  4.27 us (3%)
    ppermute x12, waiting for transfers between devices, shift(): return lax.ppermute(v, axis, [(i, (i + by) % size) for i in range(size)])  22.6 us
    ppermute x12, starting transfers between devices, shift(): return lax.ppermute(v, axis, [(i, (i + by) % size) for i in range(size)])  12.3 us
    all_to_all x1, starting transfers between devices, shards(): lax.all_to_all(blocks, ('dp', 'core'), 0, 0, tiled=True).reshape(8, 16, 640)  10 us
    all_to_all x1, waiting for transfers between devices, shards(): received = lax.all_to_all(payload, T, 0, 0, tiled=True)  9.34 us
    pallas_call x1, Pallas kernels, pack_selected(): pl.pallas_call(pack_kernel, in_specs=[smem] * 2 + [whole] * 2 + [anywhere...  8.83 us
    pallas_call x1, Pallas kernels, next_residual(): pl.pallas_call(residual_kernel, grid_spec=pltpu.PrefetchScalarGridSpec(nu...  7.58 us
    all_to_all x1, waiting for transfers between devices, shards(): lax.all_to_all(blocks, ('dp', 'core'), 0, 0, tiled=True).reshape(8, 16, 640)  7.3 us
    pallas_call x1, Pallas kernels, acts(): pl.pallas_call(acts_kernel, grid=(steps,), in_specs=[pl.BlockSpec(memory_...  6.89 us
  transfers between devices with their start and end apart: 24, of which 13 were waited for; matrix products, arithmetic and copies ran while one was open for 5% of the time, Pallas kernels for 15%

profile of v4, /device:TPU:1, one launch (start us, length us, event | category | flops | bytes accessed | tf_op | source)
XLA Modules:
  0.0 133.0 jit_solution(1453495061774073616)
XLA Ops:
  7.2 1.6 %pad_maximum_fusion.2 = bf16[8,10240]{1,0:T(8,128)(2,1)} fusion(bf16[8,5120]{1,0:T(8,128)(2,1)} %param.17, bf16[8,5120]{1,0:T(8,128)(2,1)} %param.10), kind=kLoop, calls=%fused_computation.3 | loop fusion | flops 327680 | bytes 327680 | tf_op jit(solution)/shard_map/concatenate | solution.py:348
  8.8 0.9 pad_maximum_fusion.3
  9.8 0.7 copy.23
  10.5 10.0 %all-to-all-start = ((bf16[16,8,640]{2,1,0:T(8,128)(2,1)}), bf16[16,8,640]{2,1,0:T(8,128)(2,1)S(1)}, u32[]{:S(2)}, u32[]{:S(2)}) async-start(bf16[16,8,640]{2,1,0:T(8,128)(2,1)} %bitcast.10), calls=%async_computation | async-start | bytes 327680 | tf_op jit(solution)/shard_map/all_to_all | solution.py:352
  20.5 0.8 copy.21
  21.3 0.8 copy.22
  22.1 0.8 fusion
  22.8 7.3 %all-to-all-done = bf16[16,8,640]{2,1,0:T(8,128)(2,1)S(1)} async-done(((bf16[16,8,640]{2,1,0:T(8,128)(2,1)}), bf16[16,8,640]{2,1,0:T(8,128)(2,1)S(1)}, u32[]{:S(2)}, u32[]{:S(2)}) %all-to-all-start) | async-done | bytes 163872 | tf_op jit(solution)/shard_map/all_to_all | solution.py:352
  30.2 1.3 collective-permute-start
  31.4 1.3 collective-permute-start.2
  32.8 1.5 %collective-permute-start.4 = (bf16[4,16,640]{2,1,0:T(8,128)(2,1)S(1)}, bf16[4,16,640]{2,1,0:T(8,128)(2,1)S(1)}, u32[]{:S(2)}, u32[]{:S(2)}) collective-permute-start(bf16[4,16,640]{2,1,0:T(8,128)(2,1)S(1)} %bitcast.48), channel_id=1, source_target_pairs={{0,24},{8,0},{16,8},{24,16},{1,25},{9,1},{17,9},{25,17},{2,26},{10... | collective-permute-start | bytes 245768 | tf_op jit(solution)/shard_map/ppermute | solution.py:340
  34.3 1.4 %collective-permute-start.5 = (bf16[4,16,640]{2,1,0:T(8,128)(2,1)S(1)}, bf16[4,16,640]{2,1,0:T(8,128)(2,1)S(1)}, u32[]{:S(2)}, u32[]{:S(2)}) collective-permute-start(bf16[4,16,640]{2,1,0:T(8,128)(2,1)S(1)} %bitcast.45), channel_id=1, source_target_pairs={{0,6},{2,0},{4,2},{6,4},{1,7},{3,1},{5,3},{7,5},{8,14},{10,8},{12,... | collective-permute-start | bytes 245768 | tf_op jit(solution)/shard_map/ppermute | solution.py:340
  36.5 1.7 %collective-permute-done.2 = bf16[4,16,640]{2,1,0:T(8,128)(2,1)S(1)} collective-permute-done((bf16[4,16,640]{2,1,0:T(8,128)(2,1)S(1)}, bf16[4,16,640]{2,1,0:T(8,128)(2,1)S(1)}, u32[]{:S(2)}, u32[]{:S(2)}) %collective-permute-start.2) | collective-permute-done | bytes 81952 | tf_op jit(solution)/shard_map/ppermute | solution.py:340
  38.3 0.7 pad_convert_fusion.side
  39.0 2.0 %collective-permute-done.1 = bf16[4,16,640]{2,1,0:T(8,128)(2,1)S(1)} collective-permute-done((bf16[4,16,640]{2,1,0:T(8,128)(2,1)S(1)}, bf16[4,16,640]{2,1,0:T(8,128)(2,1)S(1)}, u32[]{:S(2)}, u32[]{:S(2)}) %collective-permute-start.1) | collective-permute-done | bytes 81952 | tf_op jit(solution)/shard_map/ppermute | solution.py:340
  41.0 1.8 %collective-permute-done.3 = bf16[4,16,640]{2,1,0:T(8,128)(2,1)S(1)} collective-permute-done((bf16[4,16,640]{2,1,0:T(8,128)(2,1)S(1)}, bf16[4,16,640]{2,1,0:T(8,128)(2,1)S(1)}, u32[]{:S(2)}, u32[]{:S(2)}) %collective-permute-start.3) | collective-permute-done | bytes 81952 | tf_op jit(solution)/shard_map/ppermute | solution.py:340
  42.9 1.0 collective-permute-start.7
  43.9 1.5 %collective-permute-start.10 = (bf16[4,4,16,640]{3,2,1,0:T(8,128)(2,1)S(1)}, bf16[4,4,16,640]{3,2,1,0:T(8,128)(2,1)S(1)}, u32[]{:S(2)}, u32[]{:S(2)}) collective-permute-start(bf16[4,4,16,640]{3,2,1,0:T(8,128)(2,1)S(1)} %get-tuple-element.69.refs_4_), channel_id=1, source_target_pairs={{0,24},{8,0},{16,8},{24,16},{1,25},{9,1},{17,9},{25,17},{2,26},{10... | collective-permute-start | bytes 983048 | tf_op jit(solution)/shard_map/ppermute | solution.py:340
  45.9 4.6 %collective-permute-done.7.refs_3_ = bf16[4,4,16,640]{3,2,1,0:T(8,128)(2,1)S(1)} collective-permute-done((bf16[4,4,16,640]{3,2,1,0:T(8,128)(2,1)S(1)}, bf16[4,4,16,640]{3,2,1,0:T(8,128)(2,1)S(1)}, u32[]{:S(2)}, u32[]{:S(2)}) %collective-permute-start.7) | collective-permute-done | bytes 327712 | tf_op jit(solution)/shard_map/ppermute | solution.py:340
  50.6 2.0 %collective-permute-start.8 = (bf16[4,4,16,640]{3,2,1,0:T(8,128)(2,1)S(1)}, bf16[4,4,16,640]{3,2,1,0:T(8,128)(2,1)S(1)}, u32[]{:S(2)}, u32[]{:S(2)}) collective-permute-start(bf16[4,4,16,640]{3,2,1,0:T(8,128)(2,1)S(1)} %collective-permute-done.7.refs_3_), channel_id=1, source_target_pairs={{0,6},{2,0},{4,2},{6,4},{1,7},{3,1},{5,3},{7,5},{8,14},{10,8},{12,... | collective-permute-start | bytes 983048 | tf_op jit(solution)/shard_map/ppermute | solution.py:340
  52.6 1.2 collective-permute-start.11
  54.5 11.7 %collective-permute-done.8.refs_2_ = bf16[4,4,16,640]{3,2,1,0:T(8,128)(2,1)S(1)} collective-permute-done((bf16[4,4,16,640]{3,2,1,0:T(8,128)(2,1)S(1)}, bf16[4,4,16,640]{3,2,1,0:T(8,128)(2,1)S(1)}, u32[]{:S(2)}, u32[]{:S(2)}) %collective-permute-start.8) | collective-permute-done | bytes 327712 | tf_op jit(solution)/shard_map/ppermute | solution.py:340
  66.7 5.7 %all-gather.4.cloned.1.call-done.tok.cot = bf16[256,10240]{1,0:T(8,128)(2,1)} async-done(((bf16[8,10240]{1,0:T(8,128)(2,1)}), bf16[256,10240]{1,0:T(8,128)(2,1)}) %all-gather.4.cloned.1.call-update) | async-done | bytes 5242896 | tf_op jit(solution)/shard_map/all_gather | solution.py:348
  72.4 6.9 %acts.1 = (bf16[3,256,216]{2,1,0:T(8,128)(2,1)}, bf16[3,216,256]{2,1,0:T(8,128)(2,1)}) custom-call(s32[2]{0:T(128)} %pad_add_fusion.1.where, bf16[256,10240]{1,0:T(8,128)(2,1)} %all-gather.4.cloned.1.call-done.tok.cot, bf16[256,10240]{1,0:T(8,128)(2,1)} %all-gather.4.cloned.1.call-done.tok.cot, bf16[216,5120]{1,0:T(8,128)(2,1)} %wg.3, bf16[216,5120]{1,0:T(8,128)(2,1)} %wu.3, ...), custom_call_target="tpu_custom_call" | custom-call | flops 1698693120 | bytes 11878400 | tf_op jit(solution)/shard_map/acts/pallas_call | solution.py:67
  79.3 8.8 %pack_selected.1 = bf16[32,176,128]{2,1,0:T(8,128)(2,1)} custom-call(s32[32,10]{1,0:T(8,128)} %bitcast.52, s32[32,10]{1,0:T(8,128)} %bitcast.54, bf16[3,256,216]{2,1,0:T(8,128)(2,1)} %get-tuple-element.62.act, f32[32,16,128]{2,1,0:T(8,128)} %pad_convert_fusion.side, bf16[216,5120]{1,0:T(8,128)(2,1)} %wg.3, bf16[216,5120]{1,0:T(8,128)(2,1)} %wu.3, ...), custom_call_target="tpu_custom_call" | custom-call | flops 1698693120 | bytes 9256960 | tf_op jit(solution)/shard_map/pack_selected/pallas_call | solution.py:160
  88.2 5.8 %all-to-all-start.1 = ((bf16[32,176,128]{2,1,0:T(8,128)(2,1)}), bf16[32,176,128]{2,1,0:T(8,128)(2,1)S(1)}, u32[]{:S(2)}, u32[]{:S(2)}) async-start(bf16[32,176,128]{2,1,0:T(8,128)(2,1)} %pack_selected.1), calls=%async_computation.1 | async-start | bytes 2883584 | tf_op jit(solution)/shard_map/all_to_all | solution.py:377
  96.4 0.9 collective-permute-done.14.refs_10_
  97.3 0.7 copy-done.11
  98.3 7.6 %next_residual.1 = bf16[256,5120]{1,0:T(8,128)(2,1)} custom-call(s32[32,10]{1,0:T(8,128)} %bitcast.53, s32[32]{0:T(128)} %bitcast.62, bf16[3,256,216]{2,1,0:T(8,128)(2,1)} %get-tuple-element.62.act, bf16[216,5120]{1,0:T(8,128)(2,1)} %wd.5, bf16[256,5120]{1,0:T(8,128)(2,1)} %bitcast.40), custom_call_target="tpu_custom_call" | custom-call | flops 566231040 | bytes 7454720 | tf_op jit(solution)/shard_map/next_residual/pallas_call | solution.py:205
  105.9 9.3 %all-to-all-done.1 = bf16[32,176,128]{2,1,0:T(8,128)(2,1)S(1)} async-done(((bf16[32,176,128]{2,1,0:T(8,128)(2,1)}), bf16[32,176,128]{2,1,0:T(8,128)(2,1)S(1)}, u32[]{:S(2)}, u32[]{:S(2)}) %all-to-all-start.1) | async-done | bytes 1441824 | tf_op jit(solution)/shard_map/all_to_all | solution.py:377
  116.3 3.4 %unpack.1 = (bf16[8,5120]{1,0:T(8,128)(2,1)}, bf16[8,5120]{1,0:T(8,128)(2,1)}) custom-call(s32[32,20]{1,0:T(8,128)} %fusion.2.idx, bf16[5632,128]{1,0:T(8,128)(2,1)} %bitcast.41), custom_call_target="tpu_custom_call" | custom-call | flops 1000000 | bytes 2000000 | tf_op jit(solution)/shard_map/unpack/pallas_call | solution.py:249
  120.6 5.6 %grads.1 = (bf16[216,640]{1,0:T(8,128)(2,1)}, bf16[216,640]{1,0:T(8,128)(2,1)}, bf16[216,640]{1,0:T(8,128)(2,1)}) custom-call(s32[1]{0:T(128)} %bitcast.27.core, bf16[8,3,216,256]{3,2,1,0:T(8,128)(2,1)} %bitcast.42, bf16[4,4,16,640]{3,2,1,0:T(8,128)(2,1)} %copy-done.1, bf16[4,4,16,640]{3,2,1,0:T(8,128)(2,1)} %copy-done.5, bf16[4,4,16,640]{3,2,1,0:T(8,128)(2,1)} %copy-done.7, ...), custom_call_target="tpu_custom_call" | custom-call | flops 1698693120 | bytes 8000000 | tf_op jit(solution)/shard_map/grads/pallas_call | solution.py:316
  (69 shorter events, 7.6 us)
Async XLA Ops:
  7.2 65.2 %all-gather.4.cloned.1.call-start = ((), (), s32[]{:S(2)}) async-start(), calls=%async_computation.2 | async-start | bytes 5406720 | tf_op jit(solution)/shard_map/all_gather | solution.py:348
  10.5 19.7 %all-to-all-start = ((bf16[16,8,640]{2,1,0:T(8,128)(2,1)}), bf16[16,8,640]{2,1,0:T(8,128)(2,1)S(1)}, u32[]{:S(2)}, u32[]{:S(2)}) async-start(bf16[16,8,640]{2,1,0:T(8,128)(2,1)} %bitcast.10), calls=%async_computation | async-start | bytes 327680 | tf_op jit(solution)/shard_map/all_to_all | solution.py:352
  20.5 99.3 %all-gather.6.cloned.1.call-start = ((), (), s32[]{:S(2)}) async-start(), calls=%async_computation.3 | async-start | bytes 2985984 | tf_op jit(solution)/shard_map/all_gather | solution.py:374
  21.3 58.0 %copy-start.14 = (s32[1,1,32,10]{3,2,1,0:T(8,128)}, s32[1,1,32,10]{3,2,1,0:T(8,128)S(1)}, u32[]{:S(2)}) copy-start(s32[1,1,32,10]{3,2,1,0:T(8,128)S(1)} %copy.21) | copy-start | bytes 3844
  22.1 57.2 %copy-start.15 = (s32[1,1,32,10]{3,2,1,0:T(8,128)}, s32[1,1,32,10]{3,2,1,0:T(8,128)S(1)}, u32[]{:S(2)}) copy-start(s32[1,1,32,10]{3,2,1,0:T(8,128)S(1)} %copy.22) | copy-start | bytes 3844
  30.2 5.8 %collective-permute-start = (bf16[4,16,640]{2,1,0:T(8,128)(2,1)S(1)}, bf16[4,16,640]{2,1,0:T(8,128)(2,1)S(1)}, u32[]{:S(2)}, u32[]{:S(2)}) collective-permute-start(bf16[4,16,640]{2,1,0:T(8,128)(2,1)S(1)} %bitcast.47), channel_id=1, source_target_pairs={{0,8},{8,16},{16,24},{24,0},{1,9},{9,17},{17,25},{25,1},{2,10},{10... | collective-permute-start | bytes 245768 | tf_op jit(solution)/shard_map/ppermute | solution.py:340
  31.4 6.9 %collective-permute-start.2 = (bf16[4,16,640]{2,1,0:T(8,128)(2,1)S(1)}, bf16[4,16,640]{2,1,0:T(8,128)(2,1)S(1)}, u32[]{:S(2)}, u32[]{:S(2)}) collective-permute-start(bf16[4,16,640]{2,1,0:T(8,128)(2,1)S(1)} %bitcast.44), channel_id=1, source_target_pairs={{0,2},{2,4},{4,6},{6,0},{1,3},{3,5},{5,7},{7,1},{8,10},{10,12},{12... | collective-permute-start | bytes 245768 | tf_op jit(solution)/shard_map/ppermute | solution.py:340
  32.8 6.2 %collective-permute-start.4 = (bf16[4,16,640]{2,1,0:T(8,128)(2,1)S(1)}, bf16[4,16,640]{2,1,0:T(8,128)(2,1)S(1)}, u32[]{:S(2)}, u32[]{:S(2)}) collective-permute-start(bf16[4,16,640]{2,1,0:T(8,128)(2,1)S(1)} %bitcast.48), channel_id=1, source_target_pairs={{0,24},{8,0},{16,8},{24,16},{1,25},{9,1},{17,9},{25,17},{2,26},{10... | collective-permute-start | bytes 245768 | tf_op jit(solution)/shard_map/ppermute | solution.py:340
  34.3 4.8 %collective-permute-start.5 = (bf16[4,16,640]{2,1,0:T(8,128)(2,1)S(1)}, bf16[4,16,640]{2,1,0:T(8,128)(2,1)S(1)}, u32[]{:S(2)}, u32[]{:S(2)}) collective-permute-start(bf16[4,16,640]{2,1,0:T(8,128)(2,1)S(1)} %bitcast.45), channel_id=1, source_target_pairs={{0,6},{2,0},{4,2},{6,4},{1,7},{3,1},{5,3},{7,5},{8,14},{10,8},{12,... | collective-permute-start | bytes 245768 | tf_op jit(solution)/shard_map/ppermute | solution.py:340
  36.0 5.1 %collective-permute-start.1 = (bf16[4,16,640]{2,1,0:T(8,128)(2,1)S(1)}, bf16[4,16,640]{2,1,0:T(8,128)(2,1)S(1)}, u32[]{:S(2)}, u32[]{:S(2)}) collective-permute-start(bf16[4,16,640]{2,1,0:T(8,128)(2,1)S(1)} %collective-permute-done), channel_id=1, source_target_pairs={{0,8},{8,16},{16,24},{24,0},{1,9},{9,17},{17,25},{25,1},{2,10},{10... | collective-permute-start | bytes 245768 | tf_op jit(solution)/shard_map/ppermute | solution.py:340
  38.3 4.5 %collective-permute-start.3 = (bf16[4,16,640]{2,1,0:T(8,128)(2,1)S(1)}, bf16[4,16,640]{2,1,0:T(8,128)(2,1)S(1)}, u32[]{:S(2)}, u32[]{:S(2)}) collective-permute-start(bf16[4,16,640]{2,1,0:T(8,128)(2,1)S(1)} %collective-permute-done.2), channel_id=1, source_target_pairs={{0,2},{2,4},{4,6},{6,0},{1,3},{3,5},{5,7},{7,1},{8,10},{10,12},{12... | collective-permute-start | bytes 245768 | tf_op jit(solution)/shard_map/ppermute | solution.py:340
  42.9 51.1 %copy-start.1 = (bf16[4,4,16,640]{3,2,1,0:T(8,128)(2,1)}, bf16[4,4,16,640]{3,2,1,0:T(8,128)(2,1)S(1)}, u32[]{:S(2)}) copy-start(bf16[4,4,16,640]{3,2,1,0:T(8,128)(2,1)S(1)} %get-tuple-element.65.refs_0_) | copy-start | bytes 983044
  42.9 52.2 %copy-start.2 = (bf16[4,4,16,640]{3,2,1,0:T(8,128)(2,1)}, bf16[4,4,16,640]{3,2,1,0:T(8,128)(2,1)S(1)}, u32[]{:S(2)}) copy-start(bf16[4,4,16,640]{3,2,1,0:T(8,128)(2,1)S(1)} %get-tuple-element.69.refs_4_) | copy-start | bytes 983044
  42.9 7.7 %collective-permute-start.7 = (bf16[4,4,16,640]{3,2,1,0:T(8,128)(2,1)S(1)}, bf16[4,4,16,640]{3,2,1,0:T(8,128)(2,1)S(1)}, u32[]{:S(2)}, u32[]{:S(2)}) collective-permute-start(bf16[4,4,16,640]{3,2,1,0:T(8,128)(2,1)S(1)} %get-tuple-element.65.refs_0_), channel_id=1, source_target_pairs={{0,6},{2,0},{4,2},{6,4},{1,7},{3,1},{5,3},{7,5},{8,14},{10,8},{12,... | collective-permute-start | bytes 983048 | tf_op jit(solution)/shard_map/ppermute | solution.py:340
  43.9 8.7 %collective-permute-start.10 = (bf16[4,4,16,640]{3,2,1,0:T(8,128)(2,1)S(1)}, bf16[4,4,16,640]{3,2,1,0:T(8,128)(2,1)S(1)}, u32[]{:S(2)}, u32[]{:S(2)}) collective-permute-start(bf16[4,4,16,640]{3,2,1,0:T(8,128)(2,1)S(1)} %get-tuple-element.69.refs_4_), channel_id=1, source_target_pairs={{0,24},{8,0},{16,8},{24,16},{1,25},{9,1},{17,9},{25,17},{2,26},{10... | collective-permute-start | bytes 983048 | tf_op jit(solution)/shard_map/ppermute | solution.py:340
  45.3 9.1 %collective-permute-start.6 = (bf16[4,4,16,640]{3,2,1,0:T(8,128)(2,1)S(1)}, bf16[4,4,16,640]{3,2,1,0:T(8,128)(2,1)S(1)}, u32[]{:S(2)}, u32[]{:S(2)}) collective-permute-start(bf16[4,4,16,640]{3,2,1,0:T(8,128)(2,1)S(1)} %get-tuple-element.65.refs_0_), channel_id=1, source_target_pairs={{0,2},{2,4},{4,6},{6,0},{1,3},{3,5},{5,7},{7,1},{8,10},{10,12},{12... | collective-permute-start | bytes 983048 | tf_op jit(solution)/shard_map/ppermute | solution.py:340
  45.3 9.1 %collective-permute-start.9 = (bf16[4,4,16,640]{3,2,1,0:T(8,128)(2,1)S(1)}, bf16[4,4,16,640]{3,2,1,0:T(8,128)(2,1)S(1)}, u32[]{:S(2)}, u32[]{:S(2)}) collective-permute-start(bf16[4,4,16,640]{3,2,1,0:T(8,128)(2,1)S(1)} %get-tuple-element.69.refs_4_), channel_id=1, source_target_pairs={{0,8},{8,16},{16,24},{24,0},{1,9},{9,17},{17,25},{25,1},{2,10},{10... | collective-permute-start | bytes 983048 | tf_op jit(solution)/shard_map/ppermute | solution.py:340
  50.6 44.3 %copy-start.3 = (bf16[4,4,16,640]{3,2,1,0:T(8,128)(2,1)}, bf16[4,4,16,640]{3,2,1,0:T(8,128)(2,1)S(1)}, u32[]{:S(2)}) copy-start(bf16[4,4,16,640]{3,2,1,0:T(8,128)(2,1)S(1)} %collective-permute-done.7.refs_3_) | copy-start | bytes 983044
  50.6 15.6 %collective-permute-start.8 = (bf16[4,4,16,640]{3,2,1,0:T(8,128)(2,1)S(1)}, bf16[4,4,16,640]{3,2,1,0:T(8,128)(2,1)S(1)}, u32[]{:S(2)}, u32[]{:S(2)}) collective-permute-start(bf16[4,4,16,640]{3,2,1,0:T(8,128)(2,1)S(1)} %collective-permute-done.7.refs_3_), channel_id=1, source_target_pairs={{0,6},{2,0},{4,2},{6,4},{1,7},{3,1},{5,3},{7,5},{8,14},{10,8},{12,... | collective-permute-start | bytes 983048 | tf_op jit(solution)/shard_map/ppermute | solution.py:340
  52.6 44.7 %copy-start.4 = (bf16[4,4,16,640]{3,2,1,0:T(8,128)(2,1)}, bf16[4,4,16,640]{3,2,1,0:T(8,128)(2,1)S(1)}, u32[]{:S(2)}) copy-start(bf16[4,4,16,640]{3,2,1,0:T(8,128)(2,1)S(1)} %collective-permute-done.10.refs_7_) | copy-start | bytes 983044
  52.6 14.1 %collective-permute-start.11 = (bf16[4,4,16,640]{3,2,1,0:T(8,128)(2,1)S(1)}, bf16[4,4,16,640]{3,2,1,0:T(8,128)(2,1)S(1)}, u32[]{:S(2)}, u32[]{:S(2)}) collective-permute-start(bf16[4,4,16,640]{3,2,1,0:T(8,128)(2,1)S(1)} %collective-permute-done.10.refs_7_), channel_id=1, source_target_pairs={{0,24},{8,0},{16,8},{24,16},{1,25},{9,1},{17,9},{25,17},{2,26},{10... | collective-permute-start | bytes 983048 | tf_op jit(solution)/shard_map/ppermute | solution.py:340
  54.4 39.9 %copy-start.5 = (bf16[4,4,16,640]{3,2,1,0:T(8,128)(2,1)}, bf16[4,4,16,640]{3,2,1,0:T(8,128)(2,1)S(1)}, u32[]{:S(2)}) copy-start(bf16[4,4,16,640]{3,2,1,0:T(8,128)(2,1)S(1)} %collective-permute-done.6.refs_1_) | copy-start | bytes 983044
  54.5 41.2 %copy-start.6 = (bf16[4,4,16,640]{3,2,1,0:T(8,128)(2,1)}, bf16[4,4,16,640]{3,2,1,0:T(8,128)(2,1)S(1)}, u32[]{:S(2)}) copy-start(bf16[4,4,16,640]{3,2,1,0:T(8,128)(2,1)S(1)} %collective-permute-done.9.refs_5_) | copy-start | bytes 983044
  88.2 27.0 %all-to-all-start.1 = ((bf16[32,176,128]{2,1,0:T(8,128)(2,1)}), bf16[32,176,128]{2,1,0:T(8,128)(2,1)S(1)}, u32[]{:S(2)}, u32[]{:S(2)}) async-start(bf16[32,176,128]{2,1,0:T(8,128)(2,1)} %pack_selected.1), calls=%async_computation.1 | async-start | bytes 2883584 | tf_op jit(solution)/shard_map/all_to_all | solution.py:377
  94.0 1.7 %collective-permute-start.12 = (bf16[4,4,16,640]{3,2,1,0:T(8,128)(2,1)S(1)}, bf16[4,4,16,640]{3,2,1,0:T(8,128)(2,1)S(1)}, u32[]{:S(2)}, u32[]{:S(2)}) collective-permute-start(bf16[4,4,16,640]{3,2,1,0:T(8,128)(2,1)S(1)} %get-tuple-element.65.refs_0_), channel_id=1, source_target_pairs={{0,1},{1,0},{2,3},{3,2},{4,5},{5,4},{6,7},{7,6},{8,9},{9,8},{10,11... | collective-permute-start | bytes 983048 | tf_op jit(solution)/shard_map/ppermute | solution.py:336
  94.3 1.9 %collective-permute-start.13 = (bf16[4,4,16,640]{3,2,1,0:T(8,128)(2,1)S(1)}, bf16[4,4,16,640]{3,2,1,0:T(8,128)(2,1)S(1)}, u32[]{:S(2)}, u32[]{:S(2)}) collective-permute-start(bf16[4,4,16,640]{3,2,1,0:T(8,128)(2,1)S(1)} %collective-permute-done.6.refs_1_), channel_id=1, source_target_pairs={{0,1},{1,0},{2,3},{3,2},{4,5},{5,4},{6,7},{7,6},{8,9},{9,8},{10,11... | collective-permute-start | bytes 983048 | tf_op jit(solution)/shard_map/ppermute | solution.py:336
  94.6 2.7 %collective-permute-start.14 = (bf16[4,4,16,640]{3,2,1,0:T(8,128)(2,1)}, bf16[4,4,16,640]{3,2,1,0:T(8,128)(2,1)S(1)}, u32[]{:S(2)}, u32[]{:S(2)}) collective-permute-start(bf16[4,4,16,640]{3,2,1,0:T(8,128)(2,1)} %copy-done.7), channel_id=1, source_target_pairs={{0,1},{1,0},{2,3},{3,2},{4,5},{5,4},{6,7},{7,6},{8,9},{9,8},{10,11... | collective-permute-start | bytes 983048 | tf_op jit(solution)/shard_map/ppermute | solution.py:336
  94.8 24.9 %collective-permute-start.15 = (bf16[4,4,16,640]{3,2,1,0:T(8,128)(2,1)S(1)}, bf16[4,4,16,640]{3,2,1,0:T(8,128)(2,1)}, u32[]{:S(2)}, u32[]{:S(2)}) collective-permute-start(bf16[4,4,16,640]{3,2,1,0:T(8,128)(2,1)S(1)} %collective-permute-done.7.refs_3_), channel_id=1, source_target_pairs={{0,1},{1,0},{2,3},{3,2},{4,5},{5,4},{6,7},{7,6},{8,9},{9,8},{10,11... | collective-permute-start | bytes 983048 | tf_op jit(solution)/shard_map/ppermute | solution.py:336
  95.1 24.6 %collective-permute-start.16 = (bf16[4,4,16,640]{3,2,1,0:T(8,128)(2,1)S(1)}, bf16[4,4,16,640]{3,2,1,0:T(8,128)(2,1)}, u32[]{:S(2)}, u32[]{:S(2)}) collective-permute-start(bf16[4,4,16,640]{3,2,1,0:T(8,128)(2,1)S(1)} %get-tuple-element.69.refs_4_), channel_id=1, source_target_pairs={{0,1},{1,0},{2,3},{3,2},{4,5},{5,4},{6,7},{7,6},{8,9},{9,8},{10,11... | collective-permute-start | bytes 983048 | tf_op jit(solution)/shard_map/ppermute | solution.py:336
  95.7 24.0 %collective-permute-start.17 = (bf16[4,4,16,640]{3,2,1,0:T(8,128)(2,1)S(1)}, bf16[4,4,16,640]{3,2,1,0:T(8,128)(2,1)S(1)}, u32[]{:S(2)}, u32[]{:S(2)}) collective-permute-start(bf16[4,4,16,640]{3,2,1,0:T(8,128)(2,1)S(1)} %collective-permute-done.9.refs_5_), channel_id=1, source_target_pairs={{0,1},{1,0},{2,3},{3,2},{4,5},{5,4},{6,7},{7,6},{8,9},{9,8},{10,11... | collective-permute-start | bytes 983048 | tf_op jit(solution)/shard_map/ppermute | solution.py:336
  96.2 23.5 %collective-permute-start.18 = (bf16[4,4,16,640]{3,2,1,0:T(8,128)(2,1)}, bf16[4,4,16,640]{3,2,1,0:T(8,128)(2,1)S(1)}, u32[]{:S(2)}, u32[]{:S(2)}) collective-permute-start(bf16[4,4,16,640]{3,2,1,0:T(8,128)(2,1)} %copy-done.8), channel_id=1, source_target_pairs={{0,1},{1,0},{2,3},{3,2},{4,5},{5,4},{6,7},{7,6},{8,9},{9,8},{10,11... | collective-permute-start | bytes 983048 | tf_op jit(solution)/shard_map/ppermute | solution.py:336
  98.0 21.7 %collective-permute-start.19 = (bf16[4,4,16,640]{3,2,1,0:T(8,128)(2,1)S(1)}, bf16[4,4,16,640]{3,2,1,0:T(8,128)(2,1)}, u32[]{:S(2)}, u32[]{:S(2)}) collective-permute-start(bf16[4,4,16,640]{3,2,1,0:T(8,128)(2,1)S(1)} %collective-permute-done.10.refs_7_), channel_id=1, source_target_pairs={{0,1},{1,0},{2,3},{3,2},{4,5},{5,4},{6,7},{7,6},{8,9},{9,8},{10,11... | collective-permute-start | bytes 983048 | tf_op jit(solution)/shard_map/ppermute | solution.py:336
  (8 other events, 31.0 us)
Sparse Core Ops, SparseCore 0:
  11.1 61.2 all-gather.3
  79.4 36.8 all-gather.5

commit v5 on v4

--- a/solution.py
+++ b/solution.py
@@ -255,7 +255,7 @@
             pltpu.VMEM((32 * MSG, 128), F32),
         ]
         + [pltpu.VMEM((8, D + 128), F32)] * 4,
-        compiler_params=pltpu.CompilerParams(vmem_limit_bytes=VMEM_LIMIT),
+        compiler_params=pltpu.CompilerParams(vmem_limit_bytes=12 << 20),
         cost_estimate=pl.CostEstimate(flops=10**6, bytes_accessed=2 * 10**6, transcendentals=0),
         name="unpack",
     )(idx, data)
@@ -375,8 +375,9 @@
     payload = pack_selected(fb, bb, nat, side, wg, wu, wd, res[0, 0])
     payload, nat, *mine = lax.optimization_barrier((payload, nat, *mine))
     received = lax.all_to_all(payload, T, 0, 0, tiled=True)
+    others = [swap_core(v) for v in mine]
+    nat, *others = lax.optimization_barrier((nat, *others))
     res_next = next_residual(fb, fc, nat, wd, res[0, 0])
-    others = [swap_core(v) for v in mine]
     idx = received[:, 160, : 2 * KMAX].astype(jnp.int32)
     layer_output, input_gradient = unpack(idx, received.reshape(32 * MSG, 128))
     gate_gradient, up_gradient, down_gradient = grads(which, everyone, mine, others)

time: 134 us -> 132 us (0.985)
    all_to_all x1, waiting for transfers between devices: 9.34 us -> 7.8 us  [shards(): received = lax.all_to_all(payload, T, 0, 0, tiled=True)]
    ppermute x8, waiting for transfers between devices: 1.48 us -> 2.99 us  [swap_core(): return lax.ppermute(v, 'core', [(0, 1), (1, 0)])]
    unnamed x34 -> x32, local copies, waits for them, and re-layouts: 3.55 us -> 2.36 us
  transfers between devices with their start and end apart: 24 -> 24, of which waited for: 13 -> 15; matrix products, arithmetic and copies ran while one was open for 5% -> 4% of each run, Pallas kernels for 15% -> 15%
where the time goes in v5:
time: 132 us; the launch traced here: 131 us
  waiting for transfers between devices  46.5 us (35%)
  Pallas kernels  31.8 us (24%)
  starting transfers between devices  30.2 us (23%)
  between operations  14.2 us (11%)
  other arithmetic  4.77 us (4%)
  local copies, waits for them, and re-layouts  3.08 us (2%)
    ppermute x12, waiting for transfers between devices, shift(): return lax.ppermute(v, axis, [(i, (i + by) % size) for i in range(size)])  22.7 us
    ppermute x12, starting transfers between devices, shift(): return lax.ppermute(v, axis, [(i, (i + by) % size) for i in range(size)])  12.3 us
    all_to_all x1, starting transfers between devices, shards(): lax.all_to_all(blocks, ('dp', 'core'), 0, 0, tiled=True).reshape(8, 16, 640)  10 us
    pallas_call x1, Pallas kernels, pack_selected(): pl.pallas_call(pack_kernel, in_specs=[smem] * 2 + [whole] * 2 + [anywhere...  8.81 us
    all_to_all x1, waiting for transfers between devices, shards(): received = lax.all_to_all(payload, T, 0, 0, tiled=True)  7.8 us
    pallas_call x1, Pallas kernels, next_residual(): pl.pallas_call(residual_kernel, grid_spec=pltpu.PrefetchScalarGridSpec(nu...  7.56 us
    all_to_all x1, waiting for transfers between devices, shards(): lax.all_to_all(blocks, ('dp', 'core'), 0, 0, tiled=True).reshape(8, 16, 640)  7.3 us
    pallas_call x1, Pallas kernels, acts(): pl.pallas_call(acts_kernel, grid=(steps,), in_specs=[pl.BlockSpec(memory_...  6.97 us
  transfers between devices with their start and end apart: 24, of which 15 were waited for; matrix products, arithmetic and copies ran while one was open for 4% of the time, Pallas kernels for 15%

profile of v5, /device:TPU:1, one launch (start us, length us, event | category | flops | bytes accessed | tf_op | source)
XLA Modules:
  0.0 130.6 jit_solution(2439466387836972809)
XLA Ops:
  7.2 1.6 %pad_maximum_fusion.2 = bf16[8,10240]{1,0:T(8,128)(2,1)} fusion(bf16[8,5120]{1,0:T(8,128)(2,1)} %param.17, bf16[8,5120]{1,0:T(8,128)(2,1)} %param.10), kind=kLoop, calls=%fused_computation.3 | loop fusion | flops 327680 | bytes 327680 | tf_op jit(solution)/shard_map/concatenate | solution.py:348
  8.8 0.9 pad_maximum_fusion.3
  10.5 10.0 %all-to-all-start = ((bf16[16,8,640]{2,1,0:T(8,128)(2,1)}), bf16[16,8,640]{2,1,0:T(8,128)(2,1)S(1)}, u32[]{:S(2)}, u32[]{:S(2)}) async-start(bf16[16,8,640]{2,1,0:T(8,128)(2,1)} %bitcast.10), calls=%async_computation | async-start | bytes 327680 | tf_op jit(solution)/shard_map/all_to_all | solution.py:352
  20.5 0.8 copy.21
  21.3 0.8 copy.22
  22.1 0.8 fusion
  22.8 7.3 %all-to-all-done = bf16[16,8,640]{2,1,0:T(8,128)(2,1)S(1)} async-done(((bf16[16,8,640]{2,1,0:T(8,128)(2,1)}), bf16[16,8,640]{2,1,0:T(8,128)(2,1)S(1)}, u32[]{:S(2)}, u32[]{:S(2)}) %all-to-all-start) | async-done | bytes 163872 | tf_op jit(solution)/shard_map/all_to_all | solution.py:352
  30.2 1.3 collective-permute-start
  31.4 1.3 collective-permute-start.2
  32.8 1.5 %collective-permute-start.4 = (bf16[4,16,640]{2,1,0:T(8,128)(2,1)S(1)}, bf16[4,16,640]{2,1,0:T(8,128)(2,1)S(1)}, u32[]{:S(2)}, u32[]{:S(2)}) collective-permute-start(bf16[4,16,640]{2,1,0:T(8,128)(2,1)S(1)} %bitcast.48), channel_id=1, source_target_pairs={{0,24},{8,0},{16,8},{24,16},{1,25},{9,1},{17,9},{25,17},{2,26},{10... | collective-permute-start | bytes 245768 | tf_op jit(solution)/shard_map/ppermute | solution.py:340
  34.3 1.4 %collective-permute-start.5 = (bf16[4,16,640]{2,1,0:T(8,128)(2,1)S(1)}, bf16[4,16,640]{2,1,0:T(8,128)(2,1)S(1)}, u32[]{:S(2)}, u32[]{:S(2)}) collective-permute-start(bf16[4,16,640]{2,1,0:T(8,128)(2,1)S(1)} %bitcast.45), channel_id=1, source_target_pairs={{0,6},{2,0},{4,2},{6,4},{1,7},{3,1},{5,3},{7,5},{8,14},{10,8},{12,... | collective-permute-start | bytes 245768 | tf_op jit(solution)/shard_map/ppermute | solution.py:340
  36.5 1.7 %collective-permute-done.2 = bf16[4,16,640]{2,1,0:T(8,128)(2,1)S(1)} collective-permute-done((bf16[4,16,640]{2,1,0:T(8,128)(2,1)S(1)}, bf16[4,16,640]{2,1,0:T(8,128)(2,1)S(1)}, u32[]{:S(2)}, u32[]{:S(2)}) %collective-permute-start.2) | collective-permute-done | bytes 81952 | tf_op jit(solution)/shard_map/ppermute | solution.py:340
  38.3 0.7 pad_convert_fusion.side
  39.0 2.0 %collective-permute-done.1 = bf16[4,16,640]{2,1,0:T(8,128)(2,1)S(1)} collective-permute-done((bf16[4,16,640]{2,1,0:T(8,128)(2,1)S(1)}, bf16[4,16,640]{2,1,0:T(8,128)(2,1)S(1)}, u32[]{:S(2)}, u32[]{:S(2)}) %collective-permute-start.1) | collective-permute-done | bytes 81952 | tf_op jit(solution)/shard_map/ppermute | solution.py:340
  41.0 1.8 %collective-permute-done.3 = bf16[4,16,640]{2,1,0:T(8,128)(2,1)S(1)} collective-permute-done((bf16[4,16,640]{2,1,0:T(8,128)(2,1)S(1)}, bf16[4,16,640]{2,1,0:T(8,128)(2,1)S(1)}, u32[]{:S(2)}, u32[]{:S(2)}) %collective-permute-start.3) | collective-permute-done | bytes 81952 | tf_op jit(solution)/shard_map/ppermute | solution.py:340
  42.9 1.0 collective-permute-start.7
  43.9 1.5 %collective-permute-start.10 = (bf16[4,4,16,640]{3,2,1,0:T(8,128)(2,1)S(1)}, bf16[4,4,16,640]{3,2,1,0:T(8,128)(2,1)S(1)}, u32[]{:S(2)}, u32[]{:S(2)}) collective-permute-start(bf16[4,4,16,640]{3,2,1,0:T(8,128)(2,1)S(1)} %get-tuple-element.76.refs_4_), channel_id=1, source_target_pairs={{0,24},{8,0},{16,8},{24,16},{1,25},{9,1},{17,9},{25,17},{2,26},{10... | collective-permute-start | bytes 983048 | tf_op jit(solution)/shard_map/ppermute | solution.py:340
  45.9 4.6 %collective-permute-done.7.refs_3_ = bf16[4,4,16,640]{3,2,1,0:T(8,128)(2,1)S(1)} collective-permute-done((bf16[4,4,16,640]{3,2,1,0:T(8,128)(2,1)S(1)}, bf16[4,4,16,640]{3,2,1,0:T(8,128)(2,1)S(1)}, u32[]{:S(2)}, u32[]{:S(2)}) %collective-permute-start.7) | collective-permute-done | bytes 327712 | tf_op jit(solution)/shard_map/ppermute | solution.py:340
  50.6 2.0 %collective-permute-start.8 = (bf16[4,4,16,640]{3,2,1,0:T(8,128)(2,1)S(1)}, bf16[4,4,16,640]{3,2,1,0:T(8,128)(2,1)S(1)}, u32[]{:S(2)}, u32[]{:S(2)}) collective-permute-start(bf16[4,4,16,640]{3,2,1,0:T(8,128)(2,1)S(1)} %collective-permute-done.7.refs_3_), channel_id=1, source_target_pairs={{0,6},{2,0},{4,2},{6,4},{1,7},{3,1},{5,3},{7,5},{8,14},{10,8},{12,... | collective-permute-start | bytes 983048 | tf_op jit(solution)/shard_map/ppermute | solution.py:340
  52.6 1.2 collective-permute-start.11
  54.4 11.8 %collective-permute-done.8.refs_2_ = bf16[4,4,16,640]{3,2,1,0:T(8,128)(2,1)S(1)} collective-permute-done((bf16[4,4,16,640]{3,2,1,0:T(8,128)(2,1)S(1)}, bf16[4,4,16,640]{3,2,1,0:T(8,128)(2,1)S(1)}, u32[]{:S(2)}, u32[]{:S(2)}) %collective-permute-start.8) | collective-permute-done | bytes 327712 | tf_op jit(solution)/shard_map/ppermute | solution.py:340
  66.7 5.7 %all-gather.4.cloned.1.call-done.tok.cot = bf16[256,10240]{1,0:T(8,128)(2,1)} async-done(((bf16[8,10240]{1,0:T(8,128)(2,1)}), bf16[256,10240]{1,0:T(8,128)(2,1)}) %all-gather.4.cloned.1.call-update) | async-done | bytes 5242896 | tf_op jit(solution)/shard_map/all_gather | solution.py:348
  72.4 7.0 %acts.1 = (bf16[3,256,216]{2,1,0:T(8,128)(2,1)}, bf16[3,216,256]{2,1,0:T(8,128)(2,1)}) custom-call(s32[2]{0:T(128)} %pad_add_fusion.1.where, bf16[256,10240]{1,0:T(8,128)(2,1)} %all-gather.4.cloned.1.call-done.tok.cot, bf16[256,10240]{1,0:T(8,128)(2,1)} %all-gather.4.cloned.1.call-done.tok.cot, bf16[216,5120]{1,0:T(8,128)(2,1)} %wg.3, bf16[216,5120]{1,0:T(8,128)(2,1)} %wu.3, ...), custom_call_target="tpu_custom_call" | custom-call | flops 1698693120 | bytes 11878400 | tf_op jit(solution)/shard_map/acts/pallas_call | solution.py:67
  79.4 8.8 %pack_selected.1 = bf16[32,176,128]{2,1,0:T(8,128)(2,1)} custom-call(s32[32,10]{1,0:T(8,128)} %bitcast.52, s32[32,10]{1,0:T(8,128)} %bitcast.54, bf16[3,256,216]{2,1,0:T(8,128)(2,1)} %get-tuple-element.80.act, f32[32,16,128]{2,1,0:T(8,128)} %pad_convert_fusion.side, bf16[216,5120]{1,0:T(8,128)(2,1)} %wg.3, bf16[216,5120]{1,0:T(8,128)(2,1)} %wu.3, ...), custom_call_target="tpu_custom_call" | custom-call | flops 1698693120 | bytes 9256960 | tf_op jit(solution)/shard_map/pack_selected/pallas_call | solution.py:160
  88.2 5.8 %all-to-all-start.1 = ((bf16[32,176,128]{2,1,0:T(8,128)(2,1)}), bf16[32,176,128]{2,1,0:T(8,128)(2,1)S(1)}, u32[]{:S(2)}, u32[]{:S(2)}) async-start(bf16[32,176,128]{2,1,0:T(8,128)(2,1)} %pack_selected.1), calls=%async_computation.1 | async-start | bytes 2883584 | tf_op jit(solution)/shard_map/all_to_all | solution.py:377
  96.5 0.9 collective-permute-done.14.refs_10_
  97.4 0.7 copy-done.10
  98.8 1.1 collective-permute-done.19.refs_15_
  99.9 7.6 %next_residual.1 = bf16[256,5120]{1,0:T(8,128)(2,1)} custom-call(s32[32,10]{1,0:T(8,128)} %bitcast.53, s32[32]{0:T(128)} %bitcast.62, bf16[3,256,216]{2,1,0:T(8,128)(2,1)} %get-tuple-element.80.act, bf16[216,5120]{1,0:T(8,128)(2,1)} %wd.5, bf16[256,5120]{1,0:T(8,128)(2,1)} %bitcast.41), custom_call_target="tpu_custom_call" | custom-call | flops 566231040 | bytes 7454720 | tf_op jit(solution)/shard_map/next_residual/pallas_call | solution.py:205
  107.5 7.8 %all-to-all-done.1 = bf16[32,176,128]{2,1,0:T(8,128)(2,1)S(1)} async-done(((bf16[32,176,128]{2,1,0:T(8,128)(2,1)}), bf16[32,176,128]{2,1,0:T(8,128)(2,1)S(1)}, u32[]{:S(2)}, u32[]{:S(2)}) %all-to-all-start.1) | async-done | bytes 1441824 | tf_op jit(solution)/shard_map/all_to_all | solution.py:377
  115.3 2.8 %unpack.1 = (bf16[8,5120]{1,0:T(8,128)(2,1)}, bf16[8,5120]{1,0:T(8,128)(2,1)}) custom-call(s32[32,20]{1,0:T(8,128)S(1)} %fusion.2.idx, bf16[5632,128]{1,0:T(8,128)(2,1)S(1)} %bitcast.39), custom_call_target="tpu_custom_call" | custom-call | flops 1000000 | bytes 2000000 | tf_op jit(solution)/shard_map/unpack/pallas_call | solution.py:249
  118.1 5.6 %grads.1 = (bf16[216,640]{1,0:T(8,128)(2,1)}, bf16[216,640]{1,0:T(8,128)(2,1)}, bf16[216,640]{1,0:T(8,128)(2,1)}) custom-call(s32[1]{0:T(128)} %bitcast.27.core, bf16[8,3,216,256]{3,2,1,0:T(8,128)(2,1)} %bitcast.42, bf16[4,4,16,640]{3,2,1,0:T(8,128)(2,1)} %copy-done, bf16[4,4,16,640]{3,2,1,0:T(8,128)(2,1)} %copy-done.4, bf16[4,4,16,640]{3,2,1,0:T(8,128)(2,1)} %copy-done.6, ...), custom_call_target="tpu_custom_call" | custom-call | flops 1698693120 | bytes 8000000 | tf_op jit(solution)/shard_map/grads/pallas_call | solution.py:316
  (67 shorter events, 6.6 us)
Async XLA Ops:
  7.2 65.2 %all-gather.4.cloned.1.call-start = ((), (), s32[]{:S(2)}) async-start(), calls=%async_computation.2 | async-start | bytes 5406720 | tf_op jit(solution)/shard_map/all_gather | solution.py:348
  10.5 19.7 %all-to-all-start = ((bf16[16,8,640]{2,1,0:T(8,128)(2,1)}), bf16[16,8,640]{2,1,0:T(8,128)(2,1)S(1)}, u32[]{:S(2)}, u32[]{:S(2)}) async-start(bf16[16,8,640]{2,1,0:T(8,128)(2,1)} %bitcast.10), calls=%async_computation | async-start | bytes 327680 | tf_op jit(solution)/shard_map/all_to_all | solution.py:352
  20.5 97.6 %all-gather.6.cloned.1.call-start = ((), (), s32[]{:S(2)}) async-start(), calls=%async_computation.3 | async-start | bytes 2985984 | tf_op jit(solution)/shard_map/all_gather | solution.py:374
  21.3 58.0 %copy-start.13 = (s32[1,1,32,10]{3,2,1,0:T(8,128)}, s32[1,1,32,10]{3,2,1,0:T(8,128)S(1)}, u32[]{:S(2)}) copy-start(s32[1,1,32,10]{3,2,1,0:T(8,128)S(1)} %copy.21) | copy-start | bytes 3844
  22.1 57.3 %copy-start.14 = (s32[1,1,32,10]{3,2,1,0:T(8,128)}, s32[1,1,32,10]{3,2,1,0:T(8,128)S(1)}, u32[]{:S(2)}) copy-start(s32[1,1,32,10]{3,2,1,0:T(8,128)S(1)} %copy.22) | copy-start | bytes 3844
  30.2 5.8 %collective-permute-start = (bf16[4,16,640]{2,1,0:T(8,128)(2,1)S(1)}, bf16[4,16,640]{2,1,0:T(8,128)(2,1)S(1)}, u32[]{:S(2)}, u32[]{:S(2)}) collective-permute-start(bf16[4,16,640]{2,1,0:T(8,128)(2,1)S(1)} %bitcast.47), channel_id=1, source_target_pairs={{0,8},{8,16},{16,24},{24,0},{1,9},{9,17},{17,25},{25,1},{2,10},{10... | collective-permute-start | bytes 245768 | tf_op jit(solution)/shard_map/ppermute | solution.py:340
  31.4 6.9 %collective-permute-start.2 = (bf16[4,16,640]{2,1,0:T(8,128)(2,1)S(1)}, bf16[4,16,640]{2,1,0:T(8,128)(2,1)S(1)}, u32[]{:S(2)}, u32[]{:S(2)}) collective-permute-start(bf16[4,16,640]{2,1,0:T(8,128)(2,1)S(1)} %bitcast.44), channel_id=1, source_target_pairs={{0,2},{2,4},{4,6},{6,0},{1,3},{3,5},{5,7},{7,1},{8,10},{10,12},{12... | collective-permute-start | bytes 245768 | tf_op jit(solution)/shard_map/ppermute | solution.py:340
  32.8 6.2 %collective-permute-start.4 = (bf16[4,16,640]{2,1,0:T(8,128)(2,1)S(1)}, bf16[4,16,640]{2,1,0:T(8,128)(2,1)S(1)}, u32[]{:S(2)}, u32[]{:S(2)}) collective-permute-start(bf16[4,16,640]{2,1,0:T(8,128)(2,1)S(1)} %bitcast.48), channel_id=1, source_target_pairs={{0,24},{8,0},{16,8},{24,16},{1,25},{9,1},{17,9},{25,17},{2,26},{10... | collective-permute-start | bytes 245768 | tf_op jit(solution)/shard_map/ppermute | solution.py:340
  34.3 4.8 %collective-permute-start.5 = (bf16[4,16,640]{2,1,0:T(8,128)(2,1)S(1)}, bf16[4,16,640]{2,1,0:T(8,128)(2,1)S(1)}, u32[]{:S(2)}, u32[]{:S(2)}) collective-permute-start(bf16[4,16,640]{2,1,0:T(8,128)(2,1)S(1)} %bitcast.45), channel_id=1, source_target_pairs={{0,6},{2,0},{4,2},{6,4},{1,7},{3,1},{5,3},{7,5},{8,14},{10,8},{12,... | collective-permute-start | bytes 245768 | tf_op jit(solution)/shard_map/ppermute | solution.py:340
  36.0 5.1 %collective-permute-start.1 = (bf16[4,16,640]{2,1,0:T(8,128)(2,1)S(1)}, bf16[4,16,640]{2,1,0:T(8,128)(2,1)S(1)}, u32[]{:S(2)}, u32[]{:S(2)}) collective-permute-start(bf16[4,16,640]{2,1,0:T(8,128)(2,1)S(1)} %collective-permute-done), channel_id=1, source_target_pairs={{0,8},{8,16},{16,24},{24,0},{1,9},{9,17},{17,25},{25,1},{2,10},{10... | collective-permute-start | bytes 245768 | tf_op jit(solution)/shard_map/ppermute | solution.py:340
  38.3 4.5 %collective-permute-start.3 = (bf16[4,16,640]{2,1,0:T(8,128)(2,1)S(1)}, bf16[4,16,640]{2,1,0:T(8,128)(2,1)S(1)}, u32[]{:S(2)}, u32[]{:S(2)}) collective-permute-start(bf16[4,16,640]{2,1,0:T(8,128)(2,1)S(1)} %collective-permute-done.2), channel_id=1, source_target_pairs={{0,2},{2,4},{4,6},{6,0},{1,3},{3,5},{5,7},{7,1},{8,10},{10,12},{12... | collective-permute-start | bytes 245768 | tf_op jit(solution)/shard_map/ppermute | solution.py:340
  42.9 51.2 %copy-start = (bf16[4,4,16,640]{3,2,1,0:T(8,128)(2,1)}, bf16[4,4,16,640]{3,2,1,0:T(8,128)(2,1)S(1)}, u32[]{:S(2)}) copy-start(bf16[4,4,16,640]{3,2,1,0:T(8,128)(2,1)S(1)} %get-tuple-element.72.refs_0_) | copy-start | bytes 983044
  42.9 52.3 %copy-start.1 = (bf16[4,4,16,640]{3,2,1,0:T(8,128)(2,1)}, bf16[4,4,16,640]{3,2,1,0:T(8,128)(2,1)S(1)}, u32[]{:S(2)}) copy-start(bf16[4,4,16,640]{3,2,1,0:T(8,128)(2,1)S(1)} %get-tuple-element.76.refs_4_) | copy-start | bytes 983044
  42.9 7.7 %collective-permute-start.7 = (bf16[4,4,16,640]{3,2,1,0:T(8,128)(2,1)S(1)}, bf16[4,4,16,640]{3,2,1,0:T(8,128)(2,1)S(1)}, u32[]{:S(2)}, u32[]{:S(2)}) collective-permute-start(bf16[4,4,16,640]{3,2,1,0:T(8,128)(2,1)S(1)} %get-tuple-element.72.refs_0_), channel_id=1, source_target_pairs={{0,6},{2,0},{4,2},{6,4},{1,7},{3,1},{5,3},{7,5},{8,14},{10,8},{12,... | collective-permute-start | bytes 983048 | tf_op jit(solution)/shard_map/ppermute | solution.py:340
  43.9 8.7 %collective-permute-start.10 = (bf16[4,4,16,640]{3,2,1,0:T(8,128)(2,1)S(1)}, bf16[4,4,16,640]{3,2,1,0:T(8,128)(2,1)S(1)}, u32[]{:S(2)}, u32[]{:S(2)}) collective-permute-start(bf16[4,4,16,640]{3,2,1,0:T(8,128)(2,1)S(1)} %get-tuple-element.76.refs_4_), channel_id=1, source_target_pairs={{0,24},{8,0},{16,8},{24,16},{1,25},{9,1},{17,9},{25,17},{2,26},{10... | collective-permute-start | bytes 983048 | tf_op jit(solution)/shard_map/ppermute | solution.py:340
  45.3 9.0 %collective-permute-start.6 = (bf16[4,4,16,640]{3,2,1,0:T(8,128)(2,1)S(1)}, bf16[4,4,16,640]{3,2,1,0:T(8,128)(2,1)S(1)}, u32[]{:S(2)}, u32[]{:S(2)}) collective-permute-start(bf16[4,4,16,640]{3,2,1,0:T(8,128)(2,1)S(1)} %get-tuple-element.72.refs_0_), channel_id=1, source_target_pairs={{0,2},{2,4},{4,6},{6,0},{1,3},{3,5},{5,7},{7,1},{8,10},{10,12},{12... | collective-permute-start | bytes 983048 | tf_op jit(solution)/shard_map/ppermute | solution.py:340
  45.3 9.0 %collective-permute-start.9 = (bf16[4,4,16,640]{3,2,1,0:T(8,128)(2,1)S(1)}, bf16[4,4,16,640]{3,2,1,0:T(8,128)(2,1)S(1)}, u32[]{:S(2)}, u32[]{:S(2)}) collective-permute-start(bf16[4,4,16,640]{3,2,1,0:T(8,128)(2,1)S(1)} %get-tuple-element.76.refs_4_), channel_id=1, source_target_pairs={{0,8},{8,16},{16,24},{24,0},{1,9},{9,17},{17,25},{25,1},{2,10},{10... | collective-permute-start | bytes 983048 | tf_op jit(solution)/shard_map/ppermute | solution.py:340
  50.6 44.3 %copy-start.2 = (bf16[4,4,16,640]{3,2,1,0:T(8,128)(2,1)}, bf16[4,4,16,640]{3,2,1,0:T(8,128)(2,1)S(1)}, u32[]{:S(2)}) copy-start(bf16[4,4,16,640]{3,2,1,0:T(8,128)(2,1)S(1)} %collective-permute-done.7.refs_3_) | copy-start | bytes 983044
  50.6 15.6 %collective-permute-start.8 = (bf16[4,4,16,640]{3,2,1,0:T(8,128)(2,1)S(1)}, bf16[4,4,16,640]{3,2,1,0:T(8,128)(2,1)S(1)}, u32[]{:S(2)}, u32[]{:S(2)}) collective-permute-start(bf16[4,4,16,640]{3,2,1,0:T(8,128)(2,1)S(1)} %collective-permute-done.7.refs_3_), channel_id=1, source_target_pairs={{0,6},{2,0},{4,2},{6,4},{1,7},{3,1},{5,3},{7,5},{8,14},{10,8},{12,... | collective-permute-start | bytes 983048 | tf_op jit(solution)/shard_map/ppermute | solution.py:340
  52.6 44.8 %copy-start.3 = (bf16[4,4,16,640]{3,2,1,0:T(8,128)(2,1)}, bf16[4,4,16,640]{3,2,1,0:T(8,128)(2,1)S(1)}, u32[]{:S(2)}) copy-start(bf16[4,4,16,640]{3,2,1,0:T(8,128)(2,1)S(1)} %collective-permute-done.10.refs_7_) | copy-start | bytes 983044
  52.6 14.1 %collective-permute-start.11 = (bf16[4,4,16,640]{3,2,1,0:T(8,128)(2,1)S(1)}, bf16[4,4,16,640]{3,2,1,0:T(8,128)(2,1)S(1)}, u32[]{:S(2)}, u32[]{:S(2)}) collective-permute-start(bf16[4,4,16,640]{3,2,1,0:T(8,128)(2,1)S(1)} %collective-permute-done.10.refs_7_), channel_id=1, source_target_pairs={{0,24},{8,0},{16,8},{24,16},{1,25},{9,1},{17,9},{25,17},{2,26},{10... | collective-permute-start | bytes 983048 | tf_op jit(solution)/shard_map/ppermute | solution.py:340
  54.4 40.0 %copy-start.4 = (bf16[4,4,16,640]{3,2,1,0:T(8,128)(2,1)}, bf16[4,4,16,640]{3,2,1,0:T(8,128)(2,1)S(1)}, u32[]{:S(2)}) copy-start(bf16[4,4,16,640]{3,2,1,0:T(8,128)(2,1)S(1)} %collective-permute-done.6.refs_1_) | copy-start | bytes 983044
  54.4 41.4 %copy-start.5 = (bf16[4,4,16,640]{3,2,1,0:T(8,128)(2,1)}, bf16[4,4,16,640]{3,2,1,0:T(8,128)(2,1)S(1)}, u32[]{:S(2)}) copy-start(bf16[4,4,16,640]{3,2,1,0:T(8,128)(2,1)S(1)} %collective-permute-done.9.refs_5_) | copy-start | bytes 983044
  88.2 27.0 %all-to-all-start.1 = ((bf16[32,176,128]{2,1,0:T(8,128)(2,1)}), bf16[32,176,128]{2,1,0:T(8,128)(2,1)S(1)}, u32[]{:S(2)}, u32[]{:S(2)}) async-start(bf16[32,176,128]{2,1,0:T(8,128)(2,1)} %pack_selected.1), calls=%async_computation.1 | async-start | bytes 2883584 | tf_op jit(solution)/shard_map/all_to_all | solution.py:377
  94.0 1.7 %collective-permute-start.12 = (bf16[4,4,16,640]{3,2,1,0:T(8,128)(2,1)S(1)}, bf16[4,4,16,640]{3,2,1,0:T(8,128)(2,1)S(1)}, u32[]{:S(2)}, u32[]{:S(2)}) collective-permute-start(bf16[4,4,16,640]{3,2,1,0:T(8,128)(2,1)S(1)} %get-tuple-element.72.refs_0_), channel_id=1, source_target_pairs={{0,1},{1,0},{2,3},{3,2},{4,5},{5,4},{6,7},{7,6},{8,9},{9,8},{10,11... | collective-permute-start | bytes 983048 | tf_op jit(solution)/shard_map/ppermute | solution.py:336
  94.4 1.9 %collective-permute-start.13 = (bf16[4,4,16,640]{3,2,1,0:T(8,128)(2,1)S(1)}, bf16[4,4,16,640]{3,2,1,0:T(8,128)(2,1)S(1)}, u32[]{:S(2)}, u32[]{:S(2)}) collective-permute-start(bf16[4,4,16,640]{3,2,1,0:T(8,128)(2,1)S(1)} %collective-permute-done.6.refs_1_), channel_id=1, source_target_pairs={{0,1},{1,0},{2,3},{3,2},{4,5},{5,4},{6,7},{7,6},{8,9},{9,8},{10,11... | collective-permute-start | bytes 983048 | tf_op jit(solution)/shard_map/ppermute | solution.py:336
  94.6 2.7 %collective-permute-start.14 = (bf16[4,4,16,640]{3,2,1,0:T(8,128)(2,1)}, bf16[4,4,16,640]{3,2,1,0:T(8,128)(2,1)S(1)}, u32[]{:S(2)}, u32[]{:S(2)}) collective-permute-start(bf16[4,4,16,640]{3,2,1,0:T(8,128)(2,1)} %copy-done.6), channel_id=1, source_target_pairs={{0,1},{1,0},{2,3},{3,2},{4,5},{5,4},{6,7},{7,6},{8,9},{9,8},{10,11... | collective-permute-start | bytes 983048 | tf_op jit(solution)/shard_map/ppermute | solution.py:336
  94.9 3.5 %collective-permute-start.15 = (bf16[4,4,16,640]{3,2,1,0:T(8,128)(2,1)S(1)}, bf16[4,4,16,640]{3,2,1,0:T(8,128)(2,1)}, u32[]{:S(2)}, u32[]{:S(2)}) collective-permute-start(bf16[4,4,16,640]{3,2,1,0:T(8,128)(2,1)S(1)} %collective-permute-done.7.refs_3_), channel_id=1, source_target_pairs={{0,1},{1,0},{2,3},{3,2},{4,5},{5,4},{6,7},{7,6},{8,9},{9,8},{10,11... | collective-permute-start | bytes 983048 | tf_op jit(solution)/shard_map/ppermute | solution.py:336
  95.2 3.2 %collective-permute-start.16 = (bf16[4,4,16,640]{3,2,1,0:T(8,128)(2,1)S(1)}, bf16[4,4,16,640]{3,2,1,0:T(8,128)(2,1)}, u32[]{:S(2)}, u32[]{:S(2)}) collective-permute-start(bf16[4,4,16,640]{3,2,1,0:T(8,128)(2,1)S(1)} %get-tuple-element.76.refs_4_), channel_id=1, source_target_pairs={{0,1},{1,0},{2,3},{3,2},{4,5},{5,4},{6,7},{7,6},{8,9},{9,8},{10,11... | collective-permute-start | bytes 983048 | tf_op jit(solution)/shard_map/ppermute | solution.py:336
  95.8 2.6 %collective-permute-start.17 = (bf16[4,4,16,640]{3,2,1,0:T(8,128)(2,1)S(1)}, bf16[4,4,16,640]{3,2,1,0:T(8,128)(2,1)S(1)}, u32[]{:S(2)}, u32[]{:S(2)}) collective-permute-start(bf16[4,4,16,640]{3,2,1,0:T(8,128)(2,1)S(1)} %collective-permute-done.9.refs_5_), channel_id=1, source_target_pairs={{0,1},{1,0},{2,3},{3,2},{4,5},{5,4},{6,7},{7,6},{8,9},{9,8},{10,11... | collective-permute-start | bytes 983048 | tf_op jit(solution)/shard_map/ppermute | solution.py:336
  96.2 2.6 %collective-permute-start.18 = (bf16[4,4,16,640]{3,2,1,0:T(8,128)(2,1)}, bf16[4,4,16,640]{3,2,1,0:T(8,128)(2,1)S(1)}, u32[]{:S(2)}, u32[]{:S(2)}) collective-permute-start(bf16[4,4,16,640]{3,2,1,0:T(8,128)(2,1)} %copy-done.7), channel_id=1, source_target_pairs={{0,1},{1,0},{2,3},{3,2},{4,5},{5,4},{6,7},{7,6},{8,9},{9,8},{10,11... | collective-permute-start | bytes 983048 | tf_op jit(solution)/shard_map/ppermute | solution.py:336
  98.1 1.8 %collective-permute-start.19 = (bf16[4,4,16,640]{3,2,1,0:T(8,128)(2,1)S(1)}, bf16[4,4,16,640]{3,2,1,0:T(8,128)(2,1)}, u32[]{:S(2)}, u32[]{:S(2)}) collective-permute-start(bf16[4,4,16,640]{3,2,1,0:T(8,128)(2,1)S(1)} %collective-permute-done.10.refs_7_), channel_id=1, source_target_pairs={{0,1},{1,0},{2,3},{3,2},{4,5},{5,4},{6,7},{7,6},{8,9},{9,8},{10,11... | collective-permute-start | bytes 983048 | tf_op jit(solution)/shard_map/ppermute | solution.py:336
  (7 other events, 46.3 us)
Sparse Core Ops, SparseCore 0:
  11.1 61.2 all-gather.3
  79.5 36.8 all-gather.5

commit v6 on v5

--- a/solution.py
+++ b/solution.py
@@ -84,12 +84,12 @@
             jax.ShapeDtypeStruct((3, F, G), BF),
         ],
         scratch_shapes=[pltpu.VMEM((G, F), F32)] * 3,
-        compiler_params=pltpu.CompilerParams(vmem_limit_bytes=VMEM_LIMIT),
+        compiler_params=pltpu.CompilerParams(vmem_limit_bytes=24 << 20),
         cost_estimate=pl.CostEstimate(
             flops=6 * G * F * D, bytes_accessed=2 * (2 * G * D + 3 * F * D), transcendentals=G * F
         ),
         name="acts",
-    )(where, rows, rows, wg, wu, wd)
+    )(where, hbm(rows), hbm(rows), hbm(wg), hbm(wu), hbm(wd))
 
 
 def hbm(v):
@@ -172,7 +172,7 @@
             pltpu.VMEM((32, MSG, 128), BF),
             pltpu.SemaphoreType.DMA((4 * CHUNKS + 2,)),
         ],
-        compiler_params=pltpu.CompilerParams(vmem_limit_bytes=VMEM_LIMIT),
+        compiler_params=pltpu.CompilerParams(vmem_limit_bytes=32 << 20),
         cost_estimate=pl.CostEstimate(
             flops=6 * G * F * D, bytes_accessed=2 * (G * D + 3 * F * D), transcendentals=0
         ),

time: 132 us -> 131 us (level)
  transfers between devices with their start and end apart: 24 -> 24, of which waited for: 15 -> 15; matrix products, arithmetic and copies ran while one was open for 4% -> 3% of each run, Pallas kernels for 15% -> 15%
where the time goes in v6:
time: 131 us; the launch traced here: 130 us
  waiting for transfers between devices  47.7 us (36%)
  Pallas kernels  31.4 us (24%)
  starting transfers between devices  30.2 us (23%)
  between operations  14.2 us (11%)
  other arithmetic  3.58 us (3%)
  local copies, waits for them, and re-layouts  3.07 us (2%)
    ppermute x12, waiting for transfers between devices, shift(): return lax.ppermute(v, axis, [(i, (i + by) % size) for i in range(size)])  23.8 us
    ppermute x12, starting transfers between devices, shift(): return lax.ppermute(v, axis, [(i, (i + by) % size) for i in range(size)])  12.3 us
    all_to_all x1, starting transfers between devices, shards(): lax.all_to_all(blocks, ('dp', 'core'), 0, 0, tiled=True).reshape(8, 16, 640)  10 us
    pallas_call x1, Pallas kernels, pack_selected(): pl.pallas_call(pack_kernel, in_specs=[smem] * 2 + [whole] * 2 + [anywhere...  8.69 us
    all_to_all x1, waiting for transfers between devices, shards(): received = lax.all_to_all(payload, T, 0, 0, tiled=True)  7.81 us
    pallas_call x1, Pallas kernels, next_residual(): pl.pallas_call(residual_kernel, grid_spec=pltpu.PrefetchScalarGridSpec(nu...  7.58 us
    all_to_all x1, waiting for transfers between devices, shards(): lax.all_to_all(blocks, ('dp', 'core'), 0, 0, tiled=True).reshape(8, 16, 640)  7.31 us
    pallas_call x1, Pallas kernels, acts(): pl.pallas_call(acts_kernel, grid=(steps,), in_specs=[pl.BlockSpec(memory_...  6.75 us
  transfers between devices with their start and end apart: 24, of which 15 were waited for; matrix products, arithmetic and copies ran while one was open for 3% of the time, Pallas kernels for 15%

profile of v6, /device:TPU:1, one launch (start us, length us, event | category | flops | bytes accessed | tf_op | source)
XLA Modules:
  0.0 130.2 jit_solution(13599898403050141267)
XLA Ops:
  7.2 1.6 %pad_maximum_fusion.2 = bf16[8,10240]{1,0:T(8,128)(2,1)} fusion(bf16[8,5120]{1,0:T(8,128)(2,1)} %param.17, bf16[8,5120]{1,0:T(8,128)(2,1)} %param.10), kind=kLoop, calls=%fused_computation.3 | loop fusion | flops 327680 | bytes 327680 | tf_op jit(solution)/shard_map/concatenate | solution.py:348
  8.8 0.9 pad_maximum_fusion.3
  9.8 0.7 copy.23
  10.5 10.0 %all-to-all-start = ((bf16[16,8,640]{2,1,0:T(8,128)(2,1)}), bf16[16,8,640]{2,1,0:T(8,128)(2,1)S(1)}, u32[]{:S(2)}, u32[]{:S(2)}) async-start(bf16[16,8,640]{2,1,0:T(8,128)(2,1)} %bitcast.10), calls=%async_computation | async-start | bytes 327680 | tf_op jit(solution)/shard_map/all_to_all | solution.py:352
  20.5 0.8 copy.21
  21.3 0.8 copy.22
  22.1 0.7 fusion
  22.8 7.3 %all-to-all-done = bf16[16,8,640]{2,1,0:T(8,128)(2,1)S(1)} async-done(((bf16[16,8,640]{2,1,0:T(8,128)(2,1)}), bf16[16,8,640]{2,1,0:T(8,128)(2,1)S(1)}, u32[]{:S(2)}, u32[]{:S(2)}) %all-to-all-start) | async-done | bytes 163872 | tf_op jit(solution)/shard_map/all_to_all | solution.py:352
  30.2 1.3 collective-permute-start
  31.4 1.3 collective-permute-start.2
  32.8 1.5 %collective-permute-start.4 = (bf16[4,16,640]{2,1,0:T(8,128)(2,1)S(1)}, bf16[4,16,640]{2,1,0:T(8,128)(2,1)S(1)}, u32[]{:S(2)}, u32[]{:S(2)}) collective-permute-start(bf16[4,16,640]{2,1,0:T(8,128)(2,1)S(1)} %bitcast.51), channel_id=1, source_target_pairs={{0,24},{8,0},{16,8},{24,16},{1,25},{9,1},{17,9},{25,17},{2,26},{10... | collective-permute-start | bytes 245768 | tf_op jit(solution)/shard_map/ppermute | solution.py:340
  34.3 1.4 %collective-permute-start.5 = (bf16[4,16,640]{2,1,0:T(8,128)(2,1)S(1)}, bf16[4,16,640]{2,1,0:T(8,128)(2,1)S(1)}, u32[]{:S(2)}, u32[]{:S(2)}) collective-permute-start(bf16[4,16,640]{2,1,0:T(8,128)(2,1)S(1)} %bitcast.48), channel_id=1, source_target_pairs={{0,6},{2,0},{4,2},{6,4},{1,7},{3,1},{5,3},{7,5},{8,14},{10,8},{12,... | collective-permute-start | bytes 245768 | tf_op jit(solution)/shard_map/ppermute | solution.py:340
  36.5 1.7 %collective-permute-done.2 = bf16[4,16,640]{2,1,0:T(8,128)(2,1)S(1)} collective-permute-done((bf16[4,16,640]{2,1,0:T(8,128)(2,1)S(1)}, bf16[4,16,640]{2,1,0:T(8,128)(2,1)S(1)}, u32[]{:S(2)}, u32[]{:S(2)}) %collective-permute-start.2) | collective-permute-done | bytes 81952 | tf_op jit(solution)/shard_map/ppermute | solution.py:340
  38.3 2.7 %collective-permute-done.1 = bf16[4,16,640]{2,1,0:T(8,128)(2,1)S(1)} collective-permute-done((bf16[4,16,640]{2,1,0:T(8,128)(2,1)S(1)}, bf16[4,16,640]{2,1,0:T(8,128)(2,1)S(1)}, u32[]{:S(2)}, u32[]{:S(2)}) %collective-permute-start.1) | collective-permute-done | bytes 81952 | tf_op jit(solution)/shard_map/ppermute | solution.py:340
  41.0 1.8 %collective-permute-done.3 = bf16[4,16,640]{2,1,0:T(8,128)(2,1)S(1)} collective-permute-done((bf16[4,16,640]{2,1,0:T(8,128)(2,1)S(1)}, bf16[4,16,640]{2,1,0:T(8,128)(2,1)S(1)}, u32[]{:S(2)}, u32[]{:S(2)}) %collective-permute-start.3) | collective-permute-done | bytes 81952 | tf_op jit(solution)/shard_map/ppermute | solution.py:340
  42.9 1.0 collective-permute-start.7
  43.9 1.5 %collective-permute-start.10 = (bf16[4,4,16,640]{3,2,1,0:T(8,128)(2,1)S(1)}, bf16[4,4,16,640]{3,2,1,0:T(8,128)(2,1)S(1)}, u32[]{:S(2)}, u32[]{:S(2)}) collective-permute-start(bf16[4,4,16,640]{3,2,1,0:T(8,128)(2,1)S(1)} %get-tuple-element.76.refs_4_), channel_id=1, source_target_pairs={{0,24},{8,0},{16,8},{24,16},{1,25},{9,1},{17,9},{25,17},{2,26},{10... | collective-permute-start | bytes 983048 | tf_op jit(solution)/shard_map/ppermute | solution.py:340
  45.9 4.6 %collective-permute-done.7.refs_3_ = bf16[4,4,16,640]{3,2,1,0:T(8,128)(2,1)S(1)} collective-permute-done((bf16[4,4,16,640]{3,2,1,0:T(8,128)(2,1)S(1)}, bf16[4,4,16,640]{3,2,1,0:T(8,128)(2,1)S(1)}, u32[]{:S(2)}, u32[]{:S(2)}) %collective-permute-start.7) | collective-permute-done | bytes 327712 | tf_op jit(solution)/shard_map/ppermute | solution.py:340
  50.6 2.0 %collective-permute-start.8 = (bf16[4,4,16,640]{3,2,1,0:T(8,128)(2,1)S(1)}, bf16[4,4,16,640]{3,2,1,0:T(8,128)(2,1)}, u32[]{:S(2)}, u32[]{:S(2)}) collective-permute-start(bf16[4,4,16,640]{3,2,1,0:T(8,128)(2,1)S(1)} %collective-permute-done.7.refs_3_), channel_id=1, source_target_pairs={{0,6},{2,0},{4,2},{6,4},{1,7},{3,1},{5,3},{7,5},{8,14},{10,8},{12,... | collective-permute-start | bytes 983048 | tf_op jit(solution)/shard_map/ppermute | solution.py:340
  52.6 1.2 collective-permute-start.11
  53.9 12.3 %collective-permute-done.8.refs_2_ = bf16[4,4,16,640]{3,2,1,0:T(8,128)(2,1)} collective-permute-done((bf16[4,4,16,640]{3,2,1,0:T(8,128)(2,1)S(1)}, bf16[4,4,16,640]{3,2,1,0:T(8,128)(2,1)}, u32[]{:S(2)}, u32[]{:S(2)}) %collective-permute-start.8) | collective-permute-done | bytes 327712 | tf_op jit(solution)/shard_map/ppermute | solution.py:340
  66.7 5.7 %all-gather.4.cloned.1.call-done.tok.cot = bf16[256,10240]{1,0:T(8,128)(2,1)} async-done(((bf16[8,10240]{1,0:T(8,128)(2,1)}), bf16[256,10240]{1,0:T(8,128)(2,1)}) %all-gather.4.cloned.1.call-update) | async-done | bytes 5242896 | tf_op jit(solution)/shard_map/all_gather | solution.py:348
  72.4 6.7 %acts.1 = (bf16[3,256,216]{2,1,0:T(8,128)(2,1)S(1)}, bf16[3,216,256]{2,1,0:T(8,128)(2,1)}) custom-call(s32[2]{0:T(128)S(1)} %pad_add_fusion.1.where, bf16[256,10240]{1,0:T(8,128)(2,1)} %all-gather.4.cloned.1.call-done.tok.cot, bf16[256,10240]{1,0:T(8,128)(2,1)} %all-gather.4.cloned.1.call-done.tok.cot, bf16[216,5120]{1,0:T(8,128)(2,1)} %wg.3, ...), custom_call_target="tpu_custom_call" | custom-call | flops 1698693120 | bytes 11878400 | tf_op jit(solution)/shard_map/acts/pallas_call | solution.py:67
  79.2 8.7 %pack_selected.1 = bf16[32,176,128]{2,1,0:T(8,128)(2,1)} custom-call(s32[32,10]{1,0:T(8,128)S(1)} %bitcast.40, s32[32,10]{1,0:T(8,128)S(1)} %bitcast.42, bf16[3,256,216]{2,1,0:T(8,128)(2,1)S(1)} %get-tuple-element.80.act, f32[32,16,128]{2,1,0:T(8,128)S(1)} %pad_convert_fusion.side, bf16[216,5120]{1,0:T(8,128)(2,1)} %wg.3, bf16[216,5120]{1,0:T(8,128)(2,1)} %wu.3, ...), custom_call_target="tpu_custom_call" | custom-call | flops 1698693120 | bytes 9256960 | tf_op jit(solution)/shard_map/pack_selected/pallas_call | solution.py:160
  87.9 5.8 %all-to-all-start.1 = ((bf16[32,176,128]{2,1,0:T(8,128)(2,1)}), bf16[32,176,128]{2,1,0:T(8,128)(2,1)S(1)}, u32[]{:S(2)}, u32[]{:S(2)}) async-start(bf16[32,176,128]{2,1,0:T(8,128)(2,1)} %pack_selected.1), calls=%async_computation.1 | async-start | bytes 2883584 | tf_op jit(solution)/shard_map/all_to_all | solution.py:377
  96.1 0.9 collective-permute-done.14.refs_10_
  97.0 0.7 copy-done.10
  98.4 1.1 collective-permute-done.19.refs_15_
  99.5 7.6 %next_residual.1 = bf16[256,5120]{1,0:T(8,128)(2,1)} custom-call(s32[32,10]{1,0:T(8,128)} %bitcast.41, s32[32]{0:T(128)} %bitcast.62, bf16[3,256,216]{2,1,0:T(8,128)(2,1)} %copy-done, bf16[216,5120]{1,0:T(8,128)(2,1)} %wd.5, bf16[256,5120]{1,0:T(8,128)(2,1)} %bitcast.44), custom_call_target="tpu_custom_call" | custom-call | flops 566231040 | bytes 7454720 | tf_op jit(solution)/shard_map/next_residual/pallas_call | solution.py:205
  107.1 7.8 %all-to-all-done.1 = bf16[32,176,128]{2,1,0:T(8,128)(2,1)S(1)} async-done(((bf16[32,176,128]{2,1,0:T(8,128)(2,1)}), bf16[32,176,128]{2,1,0:T(8,128)(2,1)S(1)}, u32[]{:S(2)}, u32[]{:S(2)}) %all-to-all-start.1) | async-done | bytes 1441824 | tf_op jit(solution)/shard_map/all_to_all | solution.py:377
  114.9 2.8 %unpack.1 = (bf16[8,5120]{1,0:T(8,128)(2,1)}, bf16[8,5120]{1,0:T(8,128)(2,1)}) custom-call(s32[32,20]{1,0:T(8,128)S(1)} %fusion.2.idx, bf16[5632,128]{1,0:T(8,128)(2,1)S(1)} %bitcast.39), custom_call_target="tpu_custom_call" | custom-call | flops 1000000 | bytes 2000000 | tf_op jit(solution)/shard_map/unpack/pallas_call | solution.py:249
  117.8 5.6 %grads.1 = (bf16[216,640]{1,0:T(8,128)(2,1)}, bf16[216,640]{1,0:T(8,128)(2,1)}, bf16[216,640]{1,0:T(8,128)(2,1)}) custom-call(s32[1]{0:T(128)} %bitcast.27.core, bf16[8,3,216,256]{3,2,1,0:T(8,128)(2,1)} %bitcast.45, bf16[4,4,16,640]{3,2,1,0:T(8,128)(2,1)} %copy-done.2, bf16[4,4,16,640]{3,2,1,0:T(8,128)(2,1)} %copy-done.6, ...), custom_call_target="tpu_custom_call" | custom-call | flops 1698693120 | bytes 8000000 | tf_op jit(solution)/shard_map/grads/pallas_call | solution.py:316
  (63 shorter events, 5.5 us)
Async XLA Ops:
  7.2 65.2 %all-gather.4.cloned.1.call-start = ((), (), s32[]{:S(2)}) async-start(), calls=%async_computation.2 | async-start | bytes 5406720 | tf_op jit(solution)/shard_map/all_gather | solution.py:348
  10.5 19.7 %all-to-all-start = ((bf16[16,8,640]{2,1,0:T(8,128)(2,1)}), bf16[16,8,640]{2,1,0:T(8,128)(2,1)S(1)}, u32[]{:S(2)}, u32[]{:S(2)}) async-start(bf16[16,8,640]{2,1,0:T(8,128)(2,1)} %bitcast.10), calls=%async_computation | async-start | bytes 327680 | tf_op jit(solution)/shard_map/all_to_all | solution.py:352
  20.5 97.3 %all-gather.6.cloned.1.call-start = ((), (), s32[]{:S(2)}) async-start(), calls=%async_computation.3 | async-start | bytes 2985984 | tf_op jit(solution)/shard_map/all_gather | solution.py:374
  21.3 57.8 %copy-start.1 = (s32[1,1,32,10]{3,2,1,0:T(8,128)}, s32[1,1,32,10]{3,2,1,0:T(8,128)S(1)}, u32[]{:S(2)}) copy-start(s32[1,1,32,10]{3,2,1,0:T(8,128)S(1)} %copy.21) | copy-start | bytes 3844
  30.2 5.8 %collective-permute-start = (bf16[4,16,640]{2,1,0:T(8,128)(2,1)S(1)}, bf16[4,16,640]{2,1,0:T(8,128)(2,1)S(1)}, u32[]{:S(2)}, u32[]{:S(2)}) collective-permute-start(bf16[4,16,640]{2,1,0:T(8,128)(2,1)S(1)} %bitcast.50), channel_id=1, source_target_pairs={{0,8},{8,16},{16,24},{24,0},{1,9},{9,17},{17,25},{25,1},{2,10},{10... | collective-permute-start | bytes 245768 | tf_op jit(solution)/shard_map/ppermute | solution.py:340
  31.4 6.9 %collective-permute-start.2 = (bf16[4,16,640]{2,1,0:T(8,128)(2,1)S(1)}, bf16[4,16,640]{2,1,0:T(8,128)(2,1)S(1)}, u32[]{:S(2)}, u32[]{:S(2)}) collective-permute-start(bf16[4,16,640]{2,1,0:T(8,128)(2,1)S(1)} %bitcast.47), channel_id=1, source_target_pairs={{0,2},{2,4},{4,6},{6,0},{1,3},{3,5},{5,7},{7,1},{8,10},{10,12},{12... | collective-permute-start | bytes 245768 | tf_op jit(solution)/shard_map/ppermute | solution.py:340
  32.8 5.5 %collective-permute-start.4 = (bf16[4,16,640]{2,1,0:T(8,128)(2,1)S(1)}, bf16[4,16,640]{2,1,0:T(8,128)(2,1)S(1)}, u32[]{:S(2)}, u32[]{:S(2)}) collective-permute-start(bf16[4,16,640]{2,1,0:T(8,128)(2,1)S(1)} %bitcast.51), channel_id=1, source_target_pairs={{0,24},{8,0},{16,8},{24,16},{1,25},{9,1},{17,9},{25,17},{2,26},{10... | collective-permute-start | bytes 245768 | tf_op jit(solution)/shard_map/ppermute | solution.py:340
  34.3 4.1 %collective-permute-start.5 = (bf16[4,16,640]{2,1,0:T(8,128)(2,1)S(1)}, bf16[4,16,640]{2,1,0:T(8,128)(2,1)S(1)}, u32[]{:S(2)}, u32[]{:S(2)}) collective-permute-start(bf16[4,16,640]{2,1,0:T(8,128)(2,1)S(1)} %bitcast.48), channel_id=1, source_target_pairs={{0,6},{2,0},{4,2},{6,4},{1,7},{3,1},{5,3},{7,5},{8,14},{10,8},{12,... | collective-permute-start | bytes 245768 | tf_op jit(solution)/shard_map/ppermute | solution.py:340
  36.0 5.1 %collective-permute-start.1 = (bf16[4,16,640]{2,1,0:T(8,128)(2,1)S(1)}, bf16[4,16,640]{2,1,0:T(8,128)(2,1)S(1)}, u32[]{:S(2)}, u32[]{:S(2)}) collective-permute-start(bf16[4,16,640]{2,1,0:T(8,128)(2,1)S(1)} %collective-permute-done), channel_id=1, source_target_pairs={{0,8},{8,16},{16,24},{24,0},{1,9},{9,17},{17,25},{25,1},{2,10},{10... | collective-permute-start | bytes 245768 | tf_op jit(solution)/shard_map/ppermute | solution.py:340
  38.3 4.5 %collective-permute-start.3 = (bf16[4,16,640]{2,1,0:T(8,128)(2,1)S(1)}, bf16[4,16,640]{2,1,0:T(8,128)(2,1)S(1)}, u32[]{:S(2)}, u32[]{:S(2)}) collective-permute-start(bf16[4,16,640]{2,1,0:T(8,128)(2,1)S(1)} %collective-permute-done.2), channel_id=1, source_target_pairs={{0,2},{2,4},{4,6},{6,0},{1,3},{3,5},{5,7},{7,1},{8,10},{10,12},{12... | collective-permute-start | bytes 245768 | tf_op jit(solution)/shard_map/ppermute | solution.py:340
  42.9 50.8 %copy-start.2 = (bf16[4,4,16,640]{3,2,1,0:T(8,128)(2,1)}, bf16[4,4,16,640]{3,2,1,0:T(8,128)(2,1)S(1)}, u32[]{:S(2)}) copy-start(bf16[4,4,16,640]{3,2,1,0:T(8,128)(2,1)S(1)} %get-tuple-element.72.refs_0_) | copy-start | bytes 983044
  42.9 51.9 %copy-start.3 = (bf16[4,4,16,640]{3,2,1,0:T(8,128)(2,1)}, bf16[4,4,16,640]{3,2,1,0:T(8,128)(2,1)S(1)}, u32[]{:S(2)}) copy-start(bf16[4,4,16,640]{3,2,1,0:T(8,128)(2,1)S(1)} %get-tuple-element.76.refs_4_) | copy-start | bytes 983044
  42.9 7.7 %collective-permute-start.7 = (bf16[4,4,16,640]{3,2,1,0:T(8,128)(2,1)S(1)}, bf16[4,4,16,640]{3,2,1,0:T(8,128)(2,1)S(1)}, u32[]{:S(2)}, u32[]{:S(2)}) collective-permute-start(bf16[4,4,16,640]{3,2,1,0:T(8,128)(2,1)S(1)} %get-tuple-element.72.refs_0_), channel_id=1, source_target_pairs={{0,6},{2,0},{4,2},{6,4},{1,7},{3,1},{5,3},{7,5},{8,14},{10,8},{12,... | collective-permute-start | bytes 983048 | tf_op jit(solution)/shard_map/ppermute | solution.py:340
  43.9 8.7 %collective-permute-start.10 = (bf16[4,4,16,640]{3,2,1,0:T(8,128)(2,1)S(1)}, bf16[4,4,16,640]{3,2,1,0:T(8,128)(2,1)S(1)}, u32[]{:S(2)}, u32[]{:S(2)}) collective-permute-start(bf16[4,4,16,640]{3,2,1,0:T(8,128)(2,1)S(1)} %get-tuple-element.76.refs_4_), channel_id=1, source_target_pairs={{0,24},{8,0},{16,8},{24,16},{1,25},{9,1},{17,9},{25,17},{2,26},{10... | collective-permute-start | bytes 983048 | tf_op jit(solution)/shard_map/ppermute | solution.py:340
  45.3 8.5 %collective-permute-start.6 = (bf16[4,4,16,640]{3,2,1,0:T(8,128)(2,1)S(1)}, bf16[4,4,16,640]{3,2,1,0:T(8,128)(2,1)S(1)}, u32[]{:S(2)}, u32[]{:S(2)}) collective-permute-start(bf16[4,4,16,640]{3,2,1,0:T(8,128)(2,1)S(1)} %get-tuple-element.72.refs_0_), channel_id=1, source_target_pairs={{0,2},{2,4},{4,6},{6,0},{1,3},{3,5},{5,7},{7,1},{8,10},{10,12},{12... | collective-permute-start | bytes 983048 | tf_op jit(solution)/shard_map/ppermute | solution.py:340
  45.3 8.5 %collective-permute-start.9 = (bf16[4,4,16,640]{3,2,1,0:T(8,128)(2,1)S(1)}, bf16[4,4,16,640]{3,2,1,0:T(8,128)(2,1)S(1)}, u32[]{:S(2)}, u32[]{:S(2)}) collective-permute-start(bf16[4,4,16,640]{3,2,1,0:T(8,128)(2,1)S(1)} %get-tuple-element.76.refs_4_), channel_id=1, source_target_pairs={{0,8},{8,16},{16,24},{24,0},{1,9},{9,17},{17,25},{25,1},{2,10},{10... | collective-permute-start | bytes 983048 | tf_op jit(solution)/shard_map/ppermute | solution.py:340
  50.6 44.0 %copy-start.4 = (bf16[4,4,16,640]{3,2,1,0:T(8,128)(2,1)}, bf16[4,4,16,640]{3,2,1,0:T(8,128)(2,1)S(1)}, u32[]{:S(2)}) copy-start(bf16[4,4,16,640]{3,2,1,0:T(8,128)(2,1)S(1)} %collective-permute-done.7.refs_3_) | copy-start | bytes 983044
  50.6 15.6 %collective-permute-start.8 = (bf16[4,4,16,640]{3,2,1,0:T(8,128)(2,1)S(1)}, bf16[4,4,16,640]{3,2,1,0:T(8,128)(2,1)}, u32[]{:S(2)}, u32[]{:S(2)}) collective-permute-start(bf16[4,4,16,640]{3,2,1,0:T(8,128)(2,1)S(1)} %collective-permute-done.7.refs_3_), channel_id=1, source_target_pairs={{0,6},{2,0},{4,2},{6,4},{1,7},{3,1},{5,3},{7,5},{8,14},{10,8},{12,... | collective-permute-start | bytes 983048 | tf_op jit(solution)/shard_map/ppermute | solution.py:340
  52.6 44.4 %copy-start.5 = (bf16[4,4,16,640]{3,2,1,0:T(8,128)(2,1)}, bf16[4,4,16,640]{3,2,1,0:T(8,128)(2,1)S(1)}, u32[]{:S(2)}) copy-start(bf16[4,4,16,640]{3,2,1,0:T(8,128)(2,1)S(1)} %collective-permute-done.10.refs_7_) | copy-start | bytes 983044
  52.6 14.1 %collective-permute-start.11 = (bf16[4,4,16,640]{3,2,1,0:T(8,128)(2,1)S(1)}, bf16[4,4,16,640]{3,2,1,0:T(8,128)(2,1)}, u32[]{:S(2)}, u32[]{:S(2)}) collective-permute-start(bf16[4,4,16,640]{3,2,1,0:T(8,128)(2,1)S(1)} %collective-permute-done.10.refs_7_), channel_id=1, source_target_pairs={{0,24},{8,0},{16,8},{24,16},{1,25},{9,1},{17,9},{25,17},{2,26},{10... | collective-permute-start | bytes 983048 | tf_op jit(solution)/shard_map/ppermute | solution.py:340
  53.9 40.1 %copy-start.6 = (bf16[4,4,16,640]{3,2,1,0:T(8,128)(2,1)}, bf16[4,4,16,640]{3,2,1,0:T(8,128)(2,1)S(1)}, u32[]{:S(2)}) copy-start(bf16[4,4,16,640]{3,2,1,0:T(8,128)(2,1)S(1)} %collective-permute-done.6.refs_1_) | copy-start | bytes 983044
  53.9 41.5 %copy-start.7 = (bf16[4,4,16,640]{3,2,1,0:T(8,128)(2,1)}, bf16[4,4,16,640]{3,2,1,0:T(8,128)(2,1)S(1)}, u32[]{:S(2)}) copy-start(bf16[4,4,16,640]{3,2,1,0:T(8,128)(2,1)S(1)} %collective-permute-done.9.refs_5_) | copy-start | bytes 983044
  87.9 27.0 %all-to-all-start.1 = ((bf16[32,176,128]{2,1,0:T(8,128)(2,1)}), bf16[32,176,128]{2,1,0:T(8,128)(2,1)S(1)}, u32[]{:S(2)}, u32[]{:S(2)}) async-start(bf16[32,176,128]{2,1,0:T(8,128)(2,1)} %pack_selected.1), calls=%async_computation.1 | async-start | bytes 2883584 | tf_op jit(solution)/shard_map/all_to_all | solution.py:377
  93.7 1.7 %collective-permute-start.12 = (bf16[4,4,16,640]{3,2,1,0:T(8,128)(2,1)S(1)}, bf16[4,4,16,640]{3,2,1,0:T(8,128)(2,1)S(1)}, u32[]{:S(2)}, u32[]{:S(2)}) collective-permute-start(bf16[4,4,16,640]{3,2,1,0:T(8,128)(2,1)S(1)} %get-tuple-element.72.refs_0_), channel_id=1, source_target_pairs={{0,1},{1,0},{2,3},{3,2},{4,5},{5,4},{6,7},{7,6},{8,9},{9,8},{10,11... | collective-permute-start | bytes 983048 | tf_op jit(solution)/shard_map/ppermute | solution.py:336
  94.0 1.9 %collective-permute-start.13 = (bf16[4,4,16,640]{3,2,1,0:T(8,128)(2,1)S(1)}, bf16[4,4,16,640]{3,2,1,0:T(8,128)(2,1)S(1)}, u32[]{:S(2)}, u32[]{:S(2)}) collective-permute-start(bf16[4,4,16,640]{3,2,1,0:T(8,128)(2,1)S(1)} %collective-permute-done.6.refs_1_), channel_id=1, source_target_pairs={{0,1},{1,0},{2,3},{3,2},{4,5},{5,4},{6,7},{7,6},{8,9},{9,8},{10,11... | collective-permute-start | bytes 983048 | tf_op jit(solution)/shard_map/ppermute | solution.py:336
  94.3 2.7 %collective-permute-start.14 = (bf16[4,4,16,640]{3,2,1,0:T(8,128)(2,1)}, bf16[4,4,16,640]{3,2,1,0:T(8,128)(2,1)S(1)}, u32[]{:S(2)}, u32[]{:S(2)}) collective-permute-start(bf16[4,4,16,640]{3,2,1,0:T(8,128)(2,1)} %collective-permute-done.8.refs_2_), channel_id=1, source_target_pairs={{0,1},{1,0},{2,3},{3,2},{4,5},{5,4},{6,7},{7,6},{8,9},{9,8},{10,11... | collective-permute-start | bytes 983048 | tf_op jit(solution)/shard_map/ppermute | solution.py:336
  94.5 3.5 %collective-permute-start.15 = (bf16[4,4,16,640]{3,2,1,0:T(8,128)(2,1)S(1)}, bf16[4,4,16,640]{3,2,1,0:T(8,128)(2,1)}, u32[]{:S(2)}, u32[]{:S(2)}) collective-permute-start(bf16[4,4,16,640]{3,2,1,0:T(8,128)(2,1)S(1)} %collective-permute-done.7.refs_3_), channel_id=1, source_target_pairs={{0,1},{1,0},{2,3},{3,2},{4,5},{5,4},{6,7},{7,6},{8,9},{9,8},{10,11... | collective-permute-start | bytes 983048 | tf_op jit(solution)/shard_map/ppermute | solution.py:336
  94.8 3.2 %collective-permute-start.16 = (bf16[4,4,16,640]{3,2,1,0:T(8,128)(2,1)S(1)}, bf16[4,4,16,640]{3,2,1,0:T(8,128)(2,1)}, u32[]{:S(2)}, u32[]{:S(2)}) collective-permute-start(bf16[4,4,16,640]{3,2,1,0:T(8,128)(2,1)S(1)} %get-tuple-element.76.refs_4_), channel_id=1, source_target_pairs={{0,1},{1,0},{2,3},{3,2},{4,5},{5,4},{6,7},{7,6},{8,9},{9,8},{10,11... | collective-permute-start | bytes 983048 | tf_op jit(solution)/shard_map/ppermute | solution.py:336
  95.4 2.6 %collective-permute-start.17 = (bf16[4,4,16,640]{3,2,1,0:T(8,128)(2,1)S(1)}, bf16[4,4,16,640]{3,2,1,0:T(8,128)(2,1)S(1)}, u32[]{:S(2)}, u32[]{:S(2)}) collective-permute-start(bf16[4,4,16,640]{3,2,1,0:T(8,128)(2,1)S(1)} %collective-permute-done.9.refs_5_), channel_id=1, source_target_pairs={{0,1},{1,0},{2,3},{3,2},{4,5},{5,4},{6,7},{7,6},{8,9},{9,8},{10,11... | collective-permute-start | bytes 983048 | tf_op jit(solution)/shard_map/ppermute | solution.py:336
  95.9 2.6 %collective-permute-start.18 = (bf16[4,4,16,640]{3,2,1,0:T(8,128)(2,1)}, bf16[4,4,16,640]{3,2,1,0:T(8,128)(2,1)S(1)}, u32[]{:S(2)}, u32[]{:S(2)}) collective-permute-start(bf16[4,4,16,640]{3,2,1,0:T(8,128)(2,1)} %collective-permute-done.11.refs_6_), channel_id=1, source_target_pairs={{0,1},{1,0},{2,3},{3,2},{4,5},{5,4},{6,7},{7,6},{8,9},{9,8},{10,11... | collective-permute-start | bytes 983048 | tf_op jit(solution)/shard_map/ppermute | solution.py:336
  97.8 1.8 %collective-permute-start.19 = (bf16[4,4,16,640]{3,2,1,0:T(8,128)(2,1)S(1)}, bf16[4,4,16,640]{3,2,1,0:T(8,128)(2,1)}, u32[]{:S(2)}, u32[]{:S(2)}) collective-permute-start(bf16[4,4,16,640]{3,2,1,0:T(8,128)(2,1)S(1)} %collective-permute-done.10.refs_7_), channel_id=1, source_target_pairs={{0,1},{1,0},{2,3},{3,2},{4,5},{5,4},{6,7},{7,6},{8,9},{9,8},{10,11... | collective-permute-start | bytes 983048 | tf_op jit(solution)/shard_map/ppermute | solution.py:336
  98.0 9.1 %copy-start.11 = (bf16[4,4,16,640]{3,2,1,0:T(8,128)(2,1)}, bf16[4,4,16,640]{3,2,1,0:T(8,128)(2,1)S(1)}, u32[]{:S(2)}) copy-start(bf16[4,4,16,640]{3,2,1,0:T(8,128)(2,1)S(1)} %collective-permute-done.17.refs_13_) | copy-start | bytes 983044
  (5 other events, 20.0 us)
Sparse Core Ops, SparseCore 0:
  11.1 61.2 all-gather.3
  79.3 36.9 all-gather.5
